TPU v7x, 128 devices: a whole 4x4x4 slice. The times are simulated.
128 devices in a mesh: rows: 4 (over x_hi, core), cols: 8 (over y, x_lo), depth: 4 (over z).
Axes of the slice: x: 4 (x_hi: 2, x_lo: 2; x = x_hi * 2 + x_lo), y: 4, z: 4, core: 2. Of those that a mesh axis runs over, the one named last changes fastest.
Arguments:
- left_factor: bfloat16 [5000, 4096], P('rows', ('cols', 'depth')), may hold values from -0.71875 to 0.71875
- right_factor: bfloat16 [5000, 4, 4096], P('rows', 'depth', 'cols'), may hold values from -0.71875 to 0.71875
- amplitudes: bfloat16 [4096, 4, 2048], P('rows', 'depth'), may hold values from -0.119628906 to 0.119628906
- pair_list: int32 [4096, 2], P(('rows', 'depth')), may hold values from 0 to 119, as said below
- offsets: int32 [2], replicated, may hold values from 0 to 1272
- occ_energy: float32 [120], replicated, may hold values from -1.5 to -0.5
- virt_energy: float32 [1400], replicated, may hold values from 0.2 to 1.5
Outputs:
- update: float32 [4096, 8192], P(('rows', 'depth'), 'cols')
Inputs may be any that keep to these rules, and one draw needn't show every extreme that they name: `pair_list`: each row is a pair i <= j of occupied orbitals, no pair occurs twice, and the pair (0, 119) is always present.
All inputs are finite; a program needn't handle non-finite values.
Results may differ from a plain program's by a relative error of at most 0.0029.
Values may be sent and summed in bfloat16 or wider, within the bound.
No kernel may reach another device: no remote copies, remote signals or barrier semaphores. Data moves between devices by JAX's collectives and lax.ppermute only.
A program may use at most 64 MiB of HBM per device.

v0:
```python
import jax
import jax.numpy as jnp
from jax import lax
from jax.sharding import PartitionSpec as P

A = 64
B = 128
C = 64
D = 128


def per_device(left_factor, right_factor, amplitudes, pair_list, offsets, occ_energy, virt_energy):
    aux_rows = right_factor.shape[0]
    local_cols = right_factor.shape[2]
    right_rows = right_factor.reshape(aux_rows, local_cols)
    b_local = B // lax.axis_size("cols")
    d_local = D // lax.axis_size("depth")
    v_partial = lax.dot_general(
        lax.all_gather(left_factor, ("cols", "depth"), axis=1, tiled=True),
        right_rows,
        (((0,), (0,)), ((), ())),
        preferred_element_type=jnp.float32,
    )
    v_tile = lax.psum(v_partial, "rows").astype(jnp.bfloat16)
    width_a = A
    width_c = C
    v_tile = (
        v_tile.reshape(width_a, width_c, b_local, d_local)
        .transpose(1, 3, 2, 0)
        .reshape(width_c * d_local, b_local * width_a)
    )
    pair_rows = amplitudes.shape[0]
    amp_rows = amplitudes.reshape(pair_rows, width_c * d_local)
    ladder = lax.psum_scatter(
        jnp.dot(amp_rows, v_tile, preferred_element_type=jnp.float32),
        "depth",
        scatter_dimension=0,
        tiled=True,
    )
    mine = ladder.shape[0]
    ladder = ladder.reshape(mine, b_local, width_a)
    energy_a = lax.dynamic_slice(virt_energy, (offsets[0],), (width_a,))
    b_start = offsets[1] + lax.axis_index("cols") * b_local
    energy_b = lax.dynamic_slice(virt_energy, (b_start,), (b_local,))
    first = pair_list[:, 0:1]
    second = pair_list[:, 1:2]
    levels = jnp.arange(occ_energy.shape[0], dtype=jnp.int32)[None, :]
    occupied = jnp.sum(jnp.where(first == levels, occ_energy[None, :], 0.0), axis=1) + jnp.sum(
        jnp.where(second == levels, occ_energy[None, :], 0.0), axis=1
    )
    weight = jnp.where(pair_list[:, 0] == pair_list[:, 1], 0.5, 1.0).astype(jnp.float32)
    denominator = energy_b[None, :, None] + energy_a[None, None, :] - occupied[:, None, None]
    return (ladder * weight[:, None, None] / denominator).reshape(mine, b_local * width_a)


def solution(mesh):
    placed = (
        P("rows", ("cols", "depth")),
        P("rows", "depth", "cols"),
        P("rows", "depth", None),
        P(("rows", "depth"), None),
        P(),
        P(),
        P(),
    )
    return jax.shard_map(
        per_device,
        mesh=mesh,
        in_specs=placed,
        out_specs=P(("rows", "depth"), "cols"),
        check_vma=False,
    )
```

profile of v0, /device:TPU:1, one launch (start us, length us, event | category | flops | bytes accessed | tf_op | source)
XLA Modules:
  0.0 470.4 jit_solution(1277238772526354914)
XLA Ops:
  6.5 0.0 copy-start
  6.5 0.0 all-gather.2.cloned.1.call-start
  6.5 0.7 all-gather.2.cloned.1.call-update
  7.3 0.0 reduce-scatter.2.cloned.1.call-start
  7.3 173.3 %all-gather.2.cloned.1.call-done = bf16[1250,4096]{1,0:T(8,128)(2,1)} async-done(((bf16[1250,128]{1,0:T(8,128)(2,1)}), bf16[1250,4096]{1,0:T(8,128)(2,1)}) %all-gather.2.cloned.1.call-update) | async-done | bytes 10240016 | tf_op jit(solution)/shard_map/all_gather | solution.py:19
  180.6 0.0 copy-done
  180.6 10.6 %fusion.5 = f32[4096,512]{1,0:T(8,128)} fusion(bf16[1250,4096]{1,0:T(8,128)(2,1)} %all-gather.2.cloned.1.call-done, bf16[1250,1,512]{2,0,1:T(8,128)(2,1)S(1)} %copy-done), kind=kOutput, calls=%fused_computation.3 | convolution fusion | flops 5242880000 | bytes 19908608 | tf_op jit(solution)/shard_map/dot_general | solution.py:18
  191.2 167.6 %all-reduce.1 = bf16[4096,512]{1,0:T(8,128)(2,1)} all-reduce(f32[4096,512]{1,0:T(8,128)} %fusion.5), channel_id=1, replica_groups=mesh['rows'=4,'cols'=8,'depth'=4] {'rows'}, use_global_device_ids=true, to_apply=%region_0.0 | all-reduce | flops 2097152 | bytes 12582912 | tf_op jit(solution)/shard_map/psum | solution.py:24
  358.8 6.4 %copy.12 = bf16[4096,512]{0,1:T(8,128)(2,1)} copy(bf16[4096,512]{1,0:T(8,128)(2,1)} %all-reduce.1) | data formatting | bytes 8388608 | tf_op jit(solution)/shard_map/convert_element_type | solution.py:24
  365.2 12.6 %reshape.61 = bf16[64,64,16,32]{1,0,3,2:T(8,128)(2,1)} reshape(bf16[4096,512]{0,1:T(8,128)(2,1)} %copy.12) | data formatting | bytes 8388608 | tf_op jit(solution)/shard_map/reshape | solution.py:28
  377.7 12.6 %copy.13 = bf16[64,32,16,64]{3,2,1,0:T(8,128)(2,1)} copy(bf16[64,32,16,64]{0,3,1,2:T(8,128)(2,1)} %bitcast.21) | data formatting | bytes 8388608 | tf_op jit(solution)/shard_map/transpose | solution.py:29
  390.3 11.9 %reshape.62 = bf16[2048,1024]{1,0:T(8,128)(2,1)} reshape(bf16[64,32,16,64]{3,2,1,0:T(8,128)(2,1)} %copy.13) | data formatting | bytes 8388608 | tf_op jit(solution)/shard_map/reshape | solution.py:30
  402.2 9.9 %fusion.2 = f32[1024,1024]{0,1:T(8,128)} fusion(bf16[2048,1024]{1,0:T(8,128)(2,1)} %reshape.62, bf16[1024,1,2048]{2,0,1:T(8,128)(2,1)} %param.9), kind=kOutput, calls=%fused_computation.2 | convolution fusion | flops 4294967296 | bytes 12582912 | tf_op jit(solution)/shard_map/dot_general | solution.py:35
  412.1 0.0 copy-start.2
  412.1 0.0 copy-start.1
  412.2 0.0 copy-start.3
  412.2 0.0 reduce-scatter.2.cloned.1.call-update
  412.2 0.6 copy-done.2
  412.8 0.6 fusion.8
  415.3 0.8 dynamic_slice.6
  416.1 0.1 broadcast_reduce_fusion
  416.2 0.1 add.45
  417.0 0.8 dynamic_slice.7
  417.7 0.1 add.48
  417.8 0.0 copy-done.1
  417.8 0.0 copy-done.3
  417.8 0.1 select_reduce_fusion
  418.0 42.8 %reduce-scatter.2.cloned.1.call-done = f32[256,1024]{0,1:T(8,128)} async-done(((f32[1024,1024]{0,1:T(8,128)}), f32[256,1024]{0,1:T(8,128)}) %reduce-scatter.2.cloned.1.call-update) | async-done | bytes 1048592 | tf_op jit(solution)/shard_map/reduce_scatter | solution.py:34
  460.8 1.4 subtract_divide_fusion
  462.2 1.3 copy.14
  (5 shorter events, 0.0 us)
Async XLA Ops:
  6.5 174.1 %copy-start = (bf16[1250,1,512]{2,0,1:T(8,128)(2,1)S(1)}, bf16[1250,1,512]{2,0,1:T(8,128)(2,1)}, u32[]{:S(2)}) copy-start(bf16[1250,1,512]{2,0,1:T(8,128)(2,1)} %param.8) | copy-start | bytes 3840004
  6.5 174.1 %all-gather.2.cloned.1.call-start = ((), (), s32[]{:S(2)}) async-start(), calls=%async_computation.1 | async-start | bytes 10610688 | tf_op jit(solution)/shard_map/all_gather | solution.py:19
  7.3 453.5 %reduce-scatter.2.cloned.1.call-start = ((), (), s32[]{:S(2)}) async-start(), calls=%async_computation.2 | async-start | bytes 5242880 | tf_op jit(solution)/shard_map/reduce_scatter | solution.py:34
  412.1 0.7 copy-start.2
  412.1 5.6 %copy-start.1 = (s32[256,2]{0,1:T(2,128)S(1)}, s32[256,2]{0,1:T(2,128)}, u32[]{:S(2)}) copy-start(s32[256,2]{0,1:T(2,128)} %param.10) | copy-start | bytes 6148
  412.2 5.7 %copy-start.3 = (f32[120]{0:T(128)S(1)}, f32[120]{0:T(128)}, u32[]{:S(2)}) copy-start(f32[120]{0:T(128)} %param.12) | copy-start | bytes 1444
Sparse Core Ops, SparseCore 0:
  8.9 171.6 all-gather.1
  412.3 48.4 reduce-scatter.1
where the time goes:
time: 472 us; the launch traced here: 470 us
  waiting for transfers between devices  217 us (46%)
  blocking collectives  168 us (36%)
  local copies, waits for them, and re-layouts  47.8 us (10%)
  matrix products  20.6 us (4%)
  between operations  16 us (3%)
    all_gather x1, waiting for transfers between devices, per_device(): lax.all_gather(left_factor, ('cols', 'depth'), axis=1, tiled=True)  173 us
    psum x1, blocking collectives, per_device(): v_tile = lax.psum(v_partial, 'rows').astype(jnp.bfloat16)  168 us
    reduce_scatter x1, waiting for transfers between devices, per_device(): lax.psum_scatter(jnp.dot(amp_rows, v_tile, preferred_element_type=jnp.flo...  42.8 us
    transpose x1, local copies, waits for them, and re-layouts, per_device(): v_tile = v_tile.reshape(width_a, width_c, b_local, d_local).transpose(1,...  12.6 us
    reshape x1, local copies, waits for them, and re-layouts, per_device(): v_tile.reshape(width_a, width_c, b_local, d_local).transpose(1, 3, 2, 0)  12.6 us
    reshape x1, local copies, waits for them, and re-layouts, per_device(): v_tile = v_tile.reshape(width_a, width_c, b_local, d_local).transpose(1,...  11.9 us
    dot_general x1, matrix products, per_device(): lax.dot_general(lax.all_gather(left_factor, ('cols', 'depth'), axis=1, ti...  10.6 us
    dot_general x1, matrix products, per_device(): jnp.dot(amp_rows, v_tile, preferred_element_type=jnp.float32)  9.93 us
  transfers between devices with their start and end apart: 2, of which 2 were waited for; matrix products, arithmetic and copies ran while one was open for 1% of the time, Pallas kernels for 0%

commit v1 on v0

v1 whole, which is shorter than its diff:
```python
import functools

import jax
import jax.numpy as jnp
import numpy as np
from jax import lax
from jax.experimental import pallas as pl
from jax.experimental.pallas import tpu as pltpu
from jax.sharding import PartitionSpec as P

A = 64
B = 128
C = 64
DL = 32
CHUNKS = 2
AXES = ("rows", "cols", "depth")
VMEM = pl.BlockSpec(memory_space=pltpu.VMEM)
SMEM = pl.BlockSpec(memory_space=pltpu.SMEM)
MIB = 1 << 20


def swap_table(xh=0, core=0, y=0, xl=0, z=0):
    table = []
    for i in range(128):
        rows, cols, depth = i // 32, (i // 4) % 8, i % 4
        rows ^= xh * 2 + core
        cols ^= y * 2 + xl
        table.append((i, rows * 32 + cols * 4 + (depth ^ z)))
    return table


def swap(x, **by):
    return lax.ppermute(x, AXES, swap_table(**by))


def dot_nt(u, v):
    return lax.dot_general(u, v, (((1,), (1,)), ((), ())), preferred_element_type=jnp.float32)


def tile_kernel(*refs):
    z, la, lb, r = refs[0], refs[1:5], refs[5:9], refs[9:17]
    keep, send = refs[17:19]
    acc = refs[19]
    r_own = jnp.concatenate([r[0][...], r[1][...], r[4][...], r[5][...]], axis=1)
    r_far = jnp.concatenate([r[2][...], r[3][...], r[6][...], r[7][...]], axis=1)
    for zr in range(4):
        out = jnp.dot(la[zr][...], r_own, preferred_element_type=jnp.float32)
        for yr in range(4):
            acc[yr, z[0] ^ zr] = out[yr * 64:(yr + 1) * 64]
    for yr in range(4):
        out = jnp.dot(lb[yr][...], r_far, preferred_element_type=jnp.float32)
        for zr in range(4):
            at = z[0] ^ zr
            total = acc[yr, at] + out[zr * 64:(zr + 1) * 64]
            rows = pl.ds(pl.multiple_of(yr * 256 + at * 64, 64), 64)
            for part in range(2):
                keep[part, rows, :] = total[:, part * 128:part * 128 + 128]
                send[part, rows, :] = total[:, part * 128 + 256:part * 128 + 384]


def tile(z, la, lb, r):
    return pl.pallas_call(
        tile_kernel,
        out_shape=[jax.ShapeDtypeStruct((2, 1024, 128), jnp.float32)] * 2,
        in_specs=[SMEM] + [VMEM] * 16,
        out_specs=[VMEM] * 2,
        scratch_shapes=[pltpu.VMEM((4, 4, 64, 512), jnp.float32)],
        compiler_params=pltpu.CompilerParams(vmem_limit_bytes=40 * MIB),
        cost_estimate=pl.CostEstimate(flops=2 * 1024 * 2500 * 512, bytes_accessed=10 * MIB, transcendentals=0),
        name="tile",
    )(z, *la, *lb, *r)


def turn_kernel(keep, got, own, other):
    lane = lax.broadcasted_iota(jnp.int32, (16, 128), 1)
    odd = (lane // 32) % 2 == 1
    high = lane // 64 == 1
    for part, out in ((0, own), (1, other)):
        for group in range(16):
            v = []
            for c in range(4):
                rows = pl.ds(group * 4 + c, 16, stride=64)
                v.append(keep[part, rows, :] + got[part, rows, :])
            w = [
                jnp.where(odd, pltpu.roll(v[1], 32, 1), v[0]),
                jnp.where(odd, v[1], pltpu.roll(v[0], 96, 1)),
                jnp.where(odd, pltpu.roll(v[3], 32, 1), v[2]),
                jnp.where(odd, v[3], pltpu.roll(v[2], 96, 1)),
            ]
            t = [
                jnp.where(high, pltpu.roll(w[2], 64, 1), w[0]),
                jnp.where(high, pltpu.roll(w[3], 64, 1), w[1]),
                jnp.where(high, w[2], pltpu.roll(w[0], 64, 1)),
                jnp.where(high, w[3], pltpu.roll(w[1], 64, 1)),
            ]
            for b in range(4):
                out[b * 16:(b + 1) * 16, group * 128:(group + 1) * 128] = t[b].astype(jnp.bfloat16)


def turn(keep, got):
    return pl.pallas_call(
        turn_kernel,
        out_shape=[jax.ShapeDtypeStruct((64, 2048), jnp.bfloat16)] * 2,
        in_specs=[VMEM] * 2,
        out_specs=[VMEM] * 2,
        compiler_params=pltpu.CompilerParams(vmem_limit_bytes=16 * MIB),
        cost_estimate=pl.CostEstimate(flops=2 * MIB, bytes_accessed=3 * MIB, transcendentals=0),
        name="turn",
    )(keep, got)


def ladder_kernel(z, amp, *refs):
    parts, own, out, held = refs[:8], refs[8], refs[9:12], refs[12]
    for i in range(8):
        held[i * 64:(i + 1) * 64, :] = parts[i][...]
    for s in range(4):
        rows = pl.ds(pl.multiple_of((z[0] ^ s) * 256, 256), 256)
        part = dot_nt(amp[rows, :], held[...])
        if s == 0:
            own[...] = part
        else:
            out[s - 1][...] = part.astype(jnp.bfloat16)


def ladder(z, amp, parts):
    return pl.pallas_call(
        ladder_kernel,
        out_shape=[jax.ShapeDtypeStruct((256, 512), jnp.float32)] + [jax.ShapeDtypeStruct((256, 512), jnp.bfloat16)] * 3,
        in_specs=[SMEM] + [VMEM] * 9,
        out_specs=[VMEM] * 4,
        scratch_shapes=[pltpu.VMEM((512, 2048), jnp.bfloat16)],
        compiler_params=pltpu.CompilerParams(vmem_limit_bytes=32 * MIB),
        cost_estimate=pl.CostEstimate(flops=2 * 1024 * 2048 * 512, bytes_accessed=8 * MIB, transcendentals=0),
        name="ladder",
    )(z, amp, *parts)


def finish_kernel(own, r1, r2, r3, order, scale, out):
    total = own[...] + r1[...].astype(jnp.float32) + r2[...].astype(jnp.float32) + r3[...].astype(jnp.float32)
    turned = None
    for _ in range(3):
        term = total.astype(jnp.bfloat16)
        total = total - term.astype(jnp.float32)
        placed = jnp.dot(term, order[...], preferred_element_type=jnp.float32)
        turned = placed if turned is None else turned + placed
    out[...] = turned * scale[...]


def finish(own, got, order, scale):
    return pl.pallas_call(
        finish_kernel,
        out_shape=jax.ShapeDtypeStruct((256, 512), jnp.float32),
        in_specs=[VMEM] * 6,
        out_specs=VMEM,
        compiler_params=pltpu.CompilerParams(vmem_limit_bytes=16 * MIB),
        cost_estimate=pl.CostEstimate(flops=6 * 256 * 512 * 512, bytes_accessed=4 * MIB, transcendentals=0),
        name="finish",
    )(own, *got, order, scale)


def gather(x, axis):
    return [x] + [swap(x, **{axis: s}) for s in (1, 2, 3)]


def column_order(xh, core, y, xl):
    s = jnp.arange(512, dtype=jnp.int32)
    pc, px, b, yr, zr = s // 256, (s // 64) % 4, (s // 16) % 4, (s // 4) % 4, s % 4
    xl_of, xh_of = xl ^ (px % 2), xh ^ (px // 2)
    a = 16 * (y ^ yr) + 8 * xl_of + 2 * zr + xh_of
    target = (4 * (core ^ pc) + b) * 64 + a
    return (target[:, None] == jnp.arange(512, dtype=jnp.int32)[None, :]).astype(jnp.bfloat16)


def per_device(left, right, amplitudes, pair_list, offsets, occ_energy, virt_energy):
    rows, cols, z = (lax.axis_index(n) for n in AXES)
    xh, core, y, xl = rows // 2, rows % 2, cols // 2, cols % 2
    right = right.reshape(right.shape[0], 512)
    amp = amplitudes.reshape(1024, 2048)

    def group(j, mine):
        at = 2 * j + (core if mine else 1 - core)
        return lax.dynamic_slice(right, (0, at * 128), (right.shape[0], 128))

    r = []
    for j in range(CHUNKS):
        kept, sent = group(j, True), group(j, False)
        k1, s1 = swap(kept, xl=1), swap(sent, xl=1)
        k3, s3 = swap(kept, xl=1, xh=1), swap(sent, xl=1, xh=1)
        k2, s2 = swap(k1, xl=1, xh=1), swap(s3, xl=1)
        r.append((kept, k1, k2, k3, sent, s1, s2, s3))

    lt = left.T
    mine = lax.dynamic_slice(lt, (xh * 64, 0), (64, lt.shape[1]))
    theirs = lax.dynamic_slice(lt, ((1 - xh) * 64, 0), (64, lt.shape[1]))
    far = swap(theirs, xh=1)
    la = gather(jnp.concatenate(gather(mine, "y"), axis=0), "z")
    lb = gather(jnp.concatenate(gather(far, "z"), axis=0), "y")

    order = column_order(xh, core, y, xl)
    energy_a = lax.dynamic_slice(virt_energy, (offsets[0],), (A,))
    b_start = offsets[1] + cols * 16
    energy_b = lax.dynamic_slice(virt_energy, (b_start,), (16,))
    first = pair_list[:, 0:1]
    second = pair_list[:, 1:2]
    levels = jnp.arange(occ_energy.shape[0], dtype=jnp.int32)[None, :]
    occupied = jnp.sum(jnp.where(first == levels, occ_energy[None, :], 0.0), axis=1) + jnp.sum(
        jnp.where(second == levels, occ_energy[None, :], 0.0), axis=1
    )
    weight = jnp.where(pair_list[:, 0] == pair_list[:, 1], 0.5, 1.0).astype(jnp.float32)
    ab = (energy_b[:, None] + energy_a[None, :]).reshape(1, 1024)
    scale = weight[:, None] / (ab - occupied[:, None])

    zs = z.reshape(1).astype(jnp.int32)
    outs = []
    for j in range(CHUNKS):
        keep, send = tile(zs, la, lb, r[j])
        own, other = turn(keep, swap(send, core=1))
        mine4 = [own, swap(other, xl=1), swap(own, xh=1), swap(other, xl=1, xh=1)]
        parts = mine4 + [swap(v, core=1) for v in mine4]
        l0, l1, l2, l3 = ladder(zs, amp, parts)
        got = [swap(l1, z=1), swap(l2, z=2), swap(l3, z=3)]
        outs.append(finish(l0, got, order, scale[:, j * 512:(j + 1) * 512]))
    return jnp.concatenate(outs, axis=1)


def solution(mesh):
    placed = (
        P("rows", ("cols", "depth")),
        P("rows", "depth", "cols"),
        P("rows", "depth", None),
        P(("rows", "depth"), None),
        P(),
        P(),
        P(),
    )
    return jax.shard_map(
        per_device,
        mesh=mesh,
        in_specs=placed,
        out_specs=P(("rows", "depth"), "cols"),
        check_vma=False,
    )
```

time: 472 us -> 191 us (0.40)
  blocking collectives: 168 us -> 0 us
  waiting for transfers between devices: 217 us -> 61.4 us
  starting transfers between devices: 0.04 us -> 59.4 us
  Pallas kernels: 0 us -> 23 us
  matrix products: 20.6 us -> 0 us
  between operations: 16 us -> 2.8 us
  local copies, waits for them, and re-layouts: 47.8 us -> 41.4 us
    all_gather x1 -> x0, waiting for transfers between devices: 173 us -> none  [per_device(): lax.all_gather(left_factor, ('cols', 'depth'), axis=1, tiled=True)]
    psum x1 -> x0, blocking collectives: 168 us -> none  [per_device(): v_tile = lax.psum(v_partial, 'rows').astype(jnp.bfloat16)]
    ppermute x0 -> x47, waiting for transfers between devices: none -> 61.4 us  [swap(): return lax.ppermute(x, AXES, swap_table(**by))]
    ppermute x0 -> x47, starting transfers between devices: none -> 59.4 us  [swap(): return lax.ppermute(x, AXES, swap_table(**by))]
    reduce_scatter x1 -> x0, waiting for transfers between devices: 42.8 us -> none  [per_device(): lax.psum_scatter(jnp.dot(amp_rows, v_tile, preferred_element_type=jnp.flo...]
    reshape x2 -> x0, local copies, waits for them, and re-layouts: 24.4 us -> none  [the longest x1 12.6 us: per_device(): v_tile.reshape(width_a, width_c, b_local, d_local).transpose(1, 3, 2, 0)]
    pallas_call x0 -> x8, Pallas kernels: none -> 23 us  [the longest x2 10.5 us: tile(): pl.pallas_call(tile_kernel, out_shape=[jax.ShapeDtypeStruct((2, 1024, 128...]
    dot_general x2 -> x0, matrix products: 20.6 us -> none  [the longest x1 10.6 us: per_device(): lax.dot_general(lax.all_gather(left_factor, ('cols', 'depth'), axis=1, ti...]
  transfers between devices with their start and end apart: 2 -> 47, of which waited for: 2 -> 16; matrix products, arithmetic and copies ran while one was open for 1% -> 12% of each run, Pallas kernels for 0% -> 12%
where the time goes in v1:
time: 191 us; the launch traced here: 190 us
  waiting for transfers between devices  61.4 us (32%)
  starting transfers between devices  59.4 us (31%)
  local copies, waits for them, and re-layouts  41.4 us (22%)
  Pallas kernels  23 us (12%)
  between operations  2.8 us (1%)
    ppermute x47, waiting for transfers between devices, swap(): return lax.ppermute(x, AXES, swap_table(**by))  61.4 us
    ppermute x47, starting transfers between devices, swap(): return lax.ppermute(x, AXES, swap_table(**by))  59.4 us
    unnamed x67, local copies, waits for them, and re-layouts  20.1 us
    ppermute x6, local copies, waits for them, and re-layouts, swap(): return lax.ppermute(x, AXES, swap_table(**by))  12.6 us
    pallas_call x2, Pallas kernels, tile(): pl.pallas_call(tile_kernel, out_shape=[jax.ShapeDtypeStruct((2, 1024, 128...  10.5 us
    pallas_call x2, Pallas kernels, turn(): pl.pallas_call(turn_kernel, out_shape=[jax.ShapeDtypeStruct((64, 2048), j...  6.51 us
    pallas_call x2, Pallas kernels, ladder(): pl.pallas_call(ladder_kernel, out_shape=[jax.ShapeDtypeStruct((256, 512),...  4.79 us
  transfers between devices with their start and end apart: 47, of which 16 were waited for; matrix products, arithmetic and copies ran while one was open for 12% of the time, Pallas kernels for 12%

profile of v1, /device:TPU:1, one launch (start us, length us, event | category | flops | bytes accessed | tf_op | source)
XLA Modules:
  0.0 189.7 jit_solution(6961691635262818842)
XLA Ops:
  1.5 2.2 %collective-permute-start = (bf16[64,1250]{1,0:T(8,128)(2,1)S(1)}, bf16[64,1250]{1,0:T(8,128)(2,1)S(1)}, u32[]{:S(2)}, u32[]{:S(2)}) collective-permute-start(bf16[64,1250]{1,0:T(8,128)(2,1)S(1)} %bitcast.19), channel_id=1, source_target_pairs={{0,8},{1,9},{2,10},{3,11},{4,12},{5,13},{6,14},{7,15},{8,0},{9,1},... | collective-permute-start | bytes 480008 | tf_op jit(solution)/shard_map/ppermute | solution.py:33
  3.7 2.6 %collective-permute-start.1 = (bf16[64,1250]{1,0:T(8,128)(2,1)S(1)}, bf16[64,1250]{1,0:T(8,128)(2,1)S(1)}, u32[]{:S(2)}, u32[]{:S(2)}) collective-permute-start(bf16[64,1250]{1,0:T(8,128)(2,1)S(1)} %bitcast.20), channel_id=1, source_target_pairs={{0,16},{1,17},{2,18},{3,19},{4,20},{5,21},{6,22},{7,23},{8,24},{9,... | collective-permute-start | bytes 480008 | tf_op jit(solution)/shard_map/ppermute | solution.py:33
  6.5 2.8 %collective-permute-start.6 = (bf16[64,1250]{1,0:T(8,128)(2,1)S(1)}, bf16[64,1250]{1,0:T(8,128)(2,1)}, u32[]{:S(2)}, u32[]{:S(2)}) collective-permute-start(bf16[64,1250]{1,0:T(8,128)(2,1)S(1)} %bitcast.23), channel_id=1, source_target_pairs={{0,64},{1,65},{2,66},{3,67},{4,68},{5,69},{6,70},{7,71},{8,72},{9,... | collective-permute-start | bytes 480008 | tf_op jit(solution)/shard_map/ppermute | solution.py:33
  9.3 2.1 %dynamic-slice_bitcast_fusion.2 = (bf16[1250,128]{1,0:T(8,128)(2,1)S(1)}, bf16[1250,128]{1,0:T(8,128)(2,1)S(1)}, bf16[1250,128]{1,0:T(8,128)(2,1)S(1)}, bf16[1250,128]{1,0:T(8,128)(2,1)}) fusion(bf16[1250,1,512]{2,0,1:T(8,128)(2,1)} %param.8, s32[]{:T(128)S(6)} %select_n.142, s32[]{:T(128)S(6)} %select_n.141, s32[]{:T(128)S(6)} %select_n.161, s32[]{:T(128)S(6)} %select_n.160), kind=kLoop, calls=%fused_computation.7 | loop fusion | bytes 2560016 | tf_op jit(solution)/shard_map/dynamic_slice | solution.py:182
  12.5 2.5 %collective-permute-start.15 = (bf16[1250,128]{1,0:T(8,128)(2,1)S(1)}, bf16[1250,128]{1,0:T(8,128)(2,1)S(1)}, u32[]{:S(2)}, u32[]{:S(2)}) collective-permute-start(bf16[1250,128]{1,0:T(8,128)(2,1)S(1)} %get-tuple-element.40.refs_9_), channel_id=1, source_target_pairs={{0,68},{1,69},{2,70},{3,71},{4,64},{5,65},{6,66},{7,67},{8,76},{9,... | collective-permute-start | bytes 960008 | tf_op jit(solution)/shard_map/ppermute | solution.py:33
  15.2 1.6 collective-permute-start.7
  16.8 3.3 %collective-permute-start.8 = (bf16[64,1250]{1,0:T(8,128)(2,1)}, bf16[64,1250]{1,0:T(8,128)(2,1)S(1)}, u32[]{:S(2)}, u32[]{:S(2)}) collective-permute-start(bf16[64,1250]{1,0:T(8,128)(2,1)} %collective-permute-done.6), channel_id=1, source_target_pairs={{0,2},{1,3},{2,0},{3,1},{4,6},{5,7},{6,4},{7,5},{8,10},{9,11},{10,... | collective-permute-start | bytes 480008 | tf_op jit(solution)/shard_map/ppermute | solution.py:33
  21.1 3.7 %collective-permute-done.8 = bf16[64,1250]{1,0:T(8,128)(2,1)S(1)} collective-permute-done((bf16[64,1250]{1,0:T(8,128)(2,1)}, bf16[64,1250]{1,0:T(8,128)(2,1)S(1)}, u32[]{:S(2)}, u32[]{:S(2)}) %collective-permute-start.8) | collective-permute-done | bytes 160032 | tf_op jit(solution)/shard_map/ppermute | solution.py:33
  25.5 3.0 %collective-permute-start.9 = (bf16[64,1250]{1,0:T(8,128)(2,1)}, bf16[64,1250]{1,0:T(8,128)(2,1)}, u32[]{:S(2)}, u32[]{:S(2)}) collective-permute-start(bf16[64,1250]{1,0:T(8,128)(2,1)} %collective-permute-done.6), channel_id=1, source_target_pairs={{0,3},{1,2},{2,1},{3,0},{4,7},{5,6},{6,5},{7,4},{8,11},{9,10},{10,... | collective-permute-start | bytes 480008 | tf_op jit(solution)/shard_map/ppermute | solution.py:33
  32.4 1.4 collective-permute-start.30
  33.8 1.6 collective-permute-start.34
  35.4 3.9 %collective-permute-start.4 = (bf16[256,1250]{0,1:T(8,128)(2,1)}, bf16[256,1250]{0,1:T(8,128)(2,1)}, u32[]{:S(2)}, u32[]{:S(2)}) collective-permute-start(bf16[256,1250]{0,1:T(8,128)(2,1)} %copy.31), channel_id=1, source_target_pairs={{0,2},{1,3},{2,0},{3,1},{4,6},{5,7},{6,4},{7,5},{8,10},{9,11},{10,... | collective-permute-start | bytes 1920008 | tf_op jit(solution)/shard_map/ppermute | solution.py:33
  43.4 6.4 %collective-permute-done.14.refs_11_ = bf16[1250,128]{1,0:T(8,128)(2,1)S(1)} collective-permute-done((bf16[1250,128]{1,0:T(8,128)(2,1)S(1)}, bf16[1250,128]{1,0:T(8,128)(2,1)S(1)}, u32[]{:S(2)}, u32[]{:S(2)}) %collective-permute-start.14) | collective-permute-done | bytes 320032 | tf_op jit(solution)/shard_map/ppermute | solution.py:33
  49.9 10.9 %collective-permute-done.4 = bf16[256,1250]{0,1:T(8,128)(2,1)} collective-permute-done((bf16[256,1250]{0,1:T(8,128)(2,1)}, bf16[256,1250]{0,1:T(8,128)(2,1)}, u32[]{:S(2)}, u32[]{:S(2)}) %collective-permute-start.4) | collective-permute-done | bytes 640032 | tf_op jit(solution)/shard_map/ppermute | solution.py:33
  62.1 10.2 %collective-permute-done.5 = bf16[256,1250]{0,1:T(8,128)(2,1)} collective-permute-done((bf16[256,1250]{0,1:T(8,128)(2,1)}, bf16[256,1250]{0,1:T(8,128)(2,1)}, u32[]{:S(2)}, u32[]{:S(2)}) %collective-permute-start.5) | collective-permute-done | bytes 640032 | tf_op jit(solution)/shard_map/ppermute | solution.py:33
  72.3 1.7 collective-permute-start.32
  75.0 4.5 %collective-permute-done.12 = bf16[256,1250]{0,1:T(8,128)(2,1)} collective-permute-done((bf16[256,1250]{0,1:T(8,128)(2,1)}, bf16[256,1250]{0,1:T(8,128)(2,1)}, u32[]{:S(2)}, u32[]{:S(2)}) %collective-permute-start.12) | collective-permute-done | bytes 640032 | tf_op jit(solution)/shard_map/ppermute | solution.py:33
  80.9 2.4 %copy.39.refs_3_ = bf16[256,1250]{1,0:T(8,128)(2,1)} copy(bf16[256,1250]{0,1:T(8,128)(2,1)} %collective-permute-done.4) | data formatting | bytes 1280000 | tf_op jit(solution)/shard_map/ppermute | solution.py:33
  83.4 2.2 %copy.40.refs_4_ = bf16[256,1250]{1,0:T(8,128)(2,1)} copy(bf16[256,1250]{0,1:T(8,128)(2,1)} %collective-permute-done.5) | data formatting | bytes 1280000 | tf_op jit(solution)/shard_map/ppermute | solution.py:33
  85.5 2.2 %copy.41.refs_6_ = bf16[256,1250]{1,0:T(8,128)(2,1)} copy(bf16[256,1250]{0,1:T(8,128)(2,1)} %collective-permute-done.10) | data formatting | bytes 1280000 | tf_op jit(solution)/shard_map/ppermute | solution.py:33
  87.7 2.2 %copy.42.refs_7_ = bf16[256,1250]{1,0:T(8,128)(2,1)} copy(bf16[256,1250]{0,1:T(8,128)(2,1)} %collective-permute-done.11) | data formatting | bytes 1280000 | tf_op jit(solution)/shard_map/ppermute | solution.py:33
  89.9 2.2 %copy.43.refs_8_ = bf16[256,1250]{1,0:T(8,128)(2,1)} copy(bf16[256,1250]{0,1:T(8,128)(2,1)} %collective-permute-done.12) | data formatting | bytes 1280000 | tf_op jit(solution)/shard_map/ppermute | solution.py:33
  105.1 5.0 %tile.2 = (f32[2,1024,128]{2,1,0:T(8,128)S(1)}, f32[2,1024,128]{2,1,0:T(8,128)}) custom-call(s32[1]{0:T(128)} %bitcast.refs_0_.z, bf16[256,1250]{1,0:T(8,128)(2,1)S(1)} %pad_maximum_fusion.1.refs_1_, bf16[256,1250]{1,0:T(8,128)(2,1)S(1)} %copy.38.refs_2_, bf16[256,1250]{1,0:T(8,128)(2,1)S(1)} %copy-done.2, bf16[256,1250]{1,0:T(8,128)(2,1)S(1)} %copy-done.4, ...), custom_call_target="tpu_custom_call" | custom-call | flops 2621440000 | bytes 10485760 | tf_op jit(solution)/shard_map/tile/pallas_call | solution.py:62
  110.2 2.5 %collective-permute-start.19 = (f32[2,1024,128]{2,1,0:T(8,128)}, f32[2,1024,128]{2,1,0:T(8,128)}, u32[]{:S(2)}, u32[]{:S(2)}) collective-permute-start(f32[2,1024,128]{2,1,0:T(8,128)} %get-tuple-element.22), channel_id=1, source_target_pairs={{0,32},{1,33},{2,34},{3,35},{4,36},{5,37},{6,38},{7,39},{8,40},{9,... | collective-permute-start | bytes 3145736 | tf_op jit(solution)/shard_map/ppermute | solution.py:33
  113.8 5.5 %tile.3 = (f32[2,1024,128]{2,1,0:T(8,128)S(1)}, f32[2,1024,128]{2,1,0:T(8,128)}) custom-call(s32[1]{0:T(128)} %bitcast.refs_0_.z, bf16[256,1250]{1,0:T(8,128)(2,1)S(1)} %pad_maximum_fusion.1.refs_1_, bf16[256,1250]{1,0:T(8,128)(2,1)S(1)} %copy-done.1, bf16[256,1250]{1,0:T(8,128)(2,1)S(1)} %copy-done.3, bf16[256,1250]{1,0:T(8,128)(2,1)S(1)} %copy-done.4, ...), custom_call_target="tpu_custom_call" | custom-call | flops 2621440000 | bytes 10485760 | tf_op jit(solution)/shard_map/tile/pallas_call | solution.py:62
  124.0 3.3 %turn.2 = (bf16[64,2048]{1,0:T(8,128)(2,1)S(1)}, bf16[64,2048]{1,0:T(8,128)(2,1)S(1)}) custom-call(f32[2,1024,128]{2,1,0:T(8,128)S(1)} %get-tuple-element.21.keep, f32[2,1024,128]{2,1,0:T(8,128)} %collective-permute-done.19.got), custom_call_target="tpu_custom_call" | custom-call | flops 2097152 | bytes 3145728 | tf_op jit(solution)/shard_map/turn/pallas_call | solution.py:101
  127.2 1.8 collective-permute-start.20
  129.6 1.3 collective-permute-start.21
  132.0 3.3 %turn.3 = (bf16[64,2048]{1,0:T(8,128)(2,1)S(1)}, bf16[64,2048]{1,0:T(8,128)(2,1)S(1)}) custom-call(f32[2,1024,128]{2,1,0:T(8,128)S(1)} %get-tuple-element.29.keep, f32[2,1024,128]{2,1,0:T(8,128)} %collective-permute-done.36.got), custom_call_target="tpu_custom_call" | custom-call | flops 2097152 | bytes 3145728 | tf_op jit(solution)/shard_map/turn/pallas_call | solution.py:101
  135.3 1.7 collective-permute-start.37
  138.0 3.2 %collective-permute-done.21.refs_2_ = bf16[64,2048]{1,0:T(8,128)(2,1)S(1)} collective-permute-done((bf16[64,2048]{1,0:T(8,128)(2,1)S(1)}, bf16[64,2048]{1,0:T(8,128)(2,1)S(1)}, u32[]{:S(2)}, u32[]{:S(2)}) %collective-permute-start.21) | collective-permute-done | bytes 262176 | tf_op jit(solution)/shard_map/ppermute | solution.py:33
  141.2 2.4 %collective-permute-start.38 = (bf16[64,2048]{1,0:T(8,128)(2,1)S(1)}, bf16[64,2048]{1,0:T(8,128)(2,1)S(1)}, u32[]{:S(2)}, u32[]{:S(2)}) collective-permute-start(bf16[64,2048]{1,0:T(8,128)(2,1)S(1)} %get-tuple-element.31.refs_0_), channel_id=1, source_target_pairs={{0,64},{1,65},{2,66},{3,67},{4,68},{5,69},{6,70},{7,71},{8,72},{9,... | collective-permute-start | bytes 786440 | tf_op jit(solution)/shard_map/ppermute | solution.py:33
  143.6 2.6 %collective-permute-start.24 = (bf16[64,2048]{1,0:T(8,128)(2,1)S(1)}, bf16[64,2048]{1,0:T(8,128)(2,1)S(1)}, u32[]{:S(2)}, u32[]{:S(2)}) collective-permute-start(bf16[64,2048]{1,0:T(8,128)(2,1)S(1)} %collective-permute-done.20.refs_1_), channel_id=1, source_target_pairs={{0,32},{1,33},{2,34},{3,35},{4,36},{5,37},{6,38},{7,39},{8,40},{9,... | collective-permute-start | bytes 786440 | tf_op jit(solution)/shard_map/ppermute | solution.py:33
  146.6 1.6 collective-permute-start.26
  148.3 4.2 %collective-permute-done.38.refs_2_ = bf16[64,2048]{1,0:T(8,128)(2,1)S(1)} collective-permute-done((bf16[64,2048]{1,0:T(8,128)(2,1)S(1)}, bf16[64,2048]{1,0:T(8,128)(2,1)S(1)}, u32[]{:S(2)}, u32[]{:S(2)}) %collective-permute-start.38) | collective-permute-done | bytes 262176 | tf_op jit(solution)/shard_map/ppermute | solution.py:33
  154.2 1.7 collective-permute-start.41
  156.4 2.2 %copy-done.14 = bf16[1024,1,2048]{2,0,1:T(8,128)(2,1)S(1)} copy-done((bf16[1024,1,2048]{2,0,1:T(8,128)(2,1)S(1)}, bf16[1024,1,2048]{2,0,1:T(8,128)(2,1)}, u32[]{:S(2)}) %copy-start.14) | copy-done | bytes 4194328
  158.6 2.4 %ladder.2 = (f32[256,512]{1,0:T(8,128)S(1)}, bf16[256,512]{1,0:T(8,128)(2,1)S(1)}, bf16[256,512]{1,0:T(8,128)(2,1)S(1)}, bf16[256,512]{1,0:T(8,128)(2,1)S(1)}) custom-call(s32[1]{0:T(128)} %bitcast.refs_0_.z, bf16[1024,2048]{1,0:T(8,128)(2,1)S(1)} %bitcast.17, bf16[64,2048]{1,0:T(8,128)(2,1)S(1)} %get-tuple-element.23.refs_0_, ...), custom_call_target="tpu_custom_call" | custom-call | flops 2147483648 | bytes 8388608 | tf_op jit(solution)/shard_map/ladder/pallas_call | solution.py:126
  161.1 1.6 collective-permute-start.28
  162.7 2.3 %collective-permute-start.29 = (bf16[256,512]{1,0:T(8,128)(2,1)S(1)}, bf16[256,512]{1,0:T(8,128)(2,1)S(1)}, u32[]{:S(2)}, u32[]{:S(2)}) collective-permute-start(bf16[256,512]{1,0:T(8,128)(2,1)S(1)} %get-tuple-element.28), channel_id=1, source_target_pairs={{0,3},{1,2},{2,1},{3,0},{4,7},{5,6},{6,5},{7,4},{8,11},{9,10},{10,... | collective-permute-start | bytes 786440 | tf_op jit(solution)/shard_map/ppermute | solution.py:33
  165.0 2.4 %ladder.3 = (f32[256,512]{1,0:T(8,128)S(1)}, bf16[256,512]{1,0:T(8,128)(2,1)S(1)}, bf16[256,512]{1,0:T(8,128)(2,1)S(1)}, bf16[256,512]{1,0:T(8,128)(2,1)S(1)}) custom-call(s32[1]{0:T(128)} %bitcast.refs_0_.z, bf16[1024,2048]{1,0:T(8,128)(2,1)S(1)} %bitcast.18, bf16[64,2048]{1,0:T(8,128)(2,1)S(1)} %get-tuple-element.31.refs_0_, ...), custom_call_target="tpu_custom_call" | custom-call | flops 2147483648 | bytes 8388608 | tf_op jit(solution)/shard_map/ladder/pallas_call | solution.py:126
  167.5 1.5 collective-permute-start.45
  169.0 2.3 %collective-permute-start.46 = (bf16[256,512]{1,0:T(8,128)(2,1)S(1)}, bf16[256,512]{1,0:T(8,128)(2,1)S(1)}, u32[]{:S(2)}, u32[]{:S(2)}) collective-permute-start(bf16[256,512]{1,0:T(8,128)(2,1)S(1)} %get-tuple-element.36), channel_id=1, source_target_pairs={{0,3},{1,2},{2,1},{3,0},{4,7},{5,6},{6,5},{7,4},{8,11},{9,10},{10,... | collective-permute-start | bytes 786440 | tf_op jit(solution)/shard_map/ppermute | solution.py:33
  171.5 3.1 %collective-permute-done.28.r2 = bf16[256,512]{1,0:T(8,128)(2,1)S(1)} collective-permute-done((bf16[256,512]{1,0:T(8,128)(2,1)S(1)}, bf16[256,512]{1,0:T(8,128)(2,1)S(1)}, u32[]{:S(2)}, u32[]{:S(2)}) %collective-permute-start.28) | collective-permute-done | bytes 262176 | tf_op jit(solution)/shard_map/ppermute | solution.py:33
  174.6 2.1 %collective-permute-done.29.r3 = bf16[256,512]{1,0:T(8,128)(2,1)S(1)} collective-permute-done((bf16[256,512]{1,0:T(8,128)(2,1)S(1)}, bf16[256,512]{1,0:T(8,128)(2,1)S(1)}, u32[]{:S(2)}, u32[]{:S(2)}) %collective-permute-start.29) | collective-permute-done | bytes 262176 | tf_op jit(solution)/shard_map/ppermute | solution.py:33
  177.3 2.8 %collective-permute-done.44.r1 = bf16[256,512]{1,0:T(8,128)(2,1)S(1)} collective-permute-done((bf16[256,512]{1,0:T(8,128)(2,1)S(1)}, bf16[256,512]{1,0:T(8,128)(2,1)S(1)}, u32[]{:S(2)}, u32[]{:S(2)}) %collective-permute-start.44) | collective-permute-done | bytes 262176 | tf_op jit(solution)/shard_map/ppermute | solution.py:33
  180.2 5.7 %collective-permute-done.45.r2 = bf16[256,512]{1,0:T(8,128)(2,1)S(1)} collective-permute-done((bf16[256,512]{1,0:T(8,128)(2,1)S(1)}, bf16[256,512]{1,0:T(8,128)(2,1)S(1)}, u32[]{:S(2)}, u32[]{:S(2)}) %collective-permute-start.45) | collective-permute-done | bytes 262176 | tf_op jit(solution)/shard_map/ppermute | solution.py:33
  185.9 2.1 %collective-permute-done.46.r3 = bf16[256,512]{1,0:T(8,128)(2,1)S(1)} collective-permute-done((bf16[256,512]{1,0:T(8,128)(2,1)S(1)}, bf16[256,512]{1,0:T(8,128)(2,1)S(1)}, u32[]{:S(2)}, u32[]{:S(2)}) %collective-permute-start.46) | collective-permute-done | bytes 262176 | tf_op jit(solution)/shard_map/ppermute | solution.py:33
  (147 shorter events, 40.7 us)
Async XLA Ops:
  1.5 13.5 %collective-permute-start = (bf16[64,1250]{1,0:T(8,128)(2,1)S(1)}, bf16[64,1250]{1,0:T(8,128)(2,1)S(1)}, u32[]{:S(2)}, u32[]{:S(2)}) collective-permute-start(bf16[64,1250]{1,0:T(8,128)(2,1)S(1)} %bitcast.19), channel_id=1, source_target_pairs={{0,8},{1,9},{2,10},{3,11},{4,12},{5,13},{6,14},{7,15},{8,0},{9,1},... | collective-permute-start | bytes 480008 | tf_op jit(solution)/shard_map/ppermute | solution.py:33
  3.7 11.5 %collective-permute-start.1 = (bf16[64,1250]{1,0:T(8,128)(2,1)S(1)}, bf16[64,1250]{1,0:T(8,128)(2,1)S(1)}, u32[]{:S(2)}, u32[]{:S(2)}) collective-permute-start(bf16[64,1250]{1,0:T(8,128)(2,1)S(1)} %bitcast.20), channel_id=1, source_target_pairs={{0,16},{1,17},{2,18},{3,19},{4,20},{5,21},{6,22},{7,23},{8,24},{9,... | collective-permute-start | bytes 480008 | tf_op jit(solution)/shard_map/ppermute | solution.py:33
  6.3 10.5 %collective-permute-start.2 = (bf16[64,1250]{1,0:T(8,128)(2,1)S(1)}, bf16[64,1250]{1,0:T(8,128)(2,1)S(1)}, u32[]{:S(2)}, u32[]{:S(2)}) collective-permute-start(bf16[64,1250]{1,0:T(8,128)(2,1)S(1)} %bitcast.21), channel_id=1, source_target_pairs={{0,24},{1,25},{2,26},{3,27},{4,28},{5,29},{6,30},{7,31},{8,16},{9,... | collective-permute-start | bytes 480008 | tf_op jit(solution)/shard_map/ppermute | solution.py:33
  6.5 6.0 %collective-permute-start.6 = (bf16[64,1250]{1,0:T(8,128)(2,1)S(1)}, bf16[64,1250]{1,0:T(8,128)(2,1)}, u32[]{:S(2)}, u32[]{:S(2)}) collective-permute-start(bf16[64,1250]{1,0:T(8,128)(2,1)S(1)} %bitcast.23), channel_id=1, source_target_pairs={{0,64},{1,65},{2,66},{3,67},{4,68},{5,69},{6,70},{7,71},{8,72},{9,... | collective-permute-start | bytes 480008 | tf_op jit(solution)/shard_map/ppermute | solution.py:33
  11.4 62.5 %copy-start.8 = (bf16[1250,128]{1,0:T(8,128)(2,1)}, bf16[1250,128]{1,0:T(8,128)(2,1)S(1)}, u32[]{:S(2)}) copy-start(bf16[1250,128]{1,0:T(8,128)(2,1)S(1)} %get-tuple-element.41.refs_13_) | copy-start | bytes 960004
  11.4 21.0 %collective-permute-start.13 = (bf16[1250,128]{1,0:T(8,128)(2,1)S(1)}, bf16[1250,128]{1,0:T(8,128)(2,1)S(1)}, u32[]{:S(2)}, u32[]{:S(2)}) collective-permute-start(bf16[1250,128]{1,0:T(8,128)(2,1)S(1)} %get-tuple-element.40.refs_9_), channel_id=1, source_target_pairs={{0,4},{1,5},{2,6},{3,7},{4,0},{5,1},{6,2},{7,3},{8,12},{9,13},{10,... | collective-permute-start | bytes 960008 | tf_op jit(solution)/shard_map/ppermute | solution.py:33
  12.5 22.9 %collective-permute-start.15 = (bf16[1250,128]{1,0:T(8,128)(2,1)S(1)}, bf16[1250,128]{1,0:T(8,128)(2,1)S(1)}, u32[]{:S(2)}, u32[]{:S(2)}) collective-permute-start(bf16[1250,128]{1,0:T(8,128)(2,1)S(1)} %get-tuple-element.40.refs_9_), channel_id=1, source_target_pairs={{0,68},{1,69},{2,70},{3,71},{4,64},{5,65},{6,66},{7,67},{8,76},{9,... | collective-permute-start | bytes 960008 | tf_op jit(solution)/shard_map/ppermute | solution.py:33
  15.0 18.8 %collective-permute-start.17 = (bf16[1250,128]{1,0:T(8,128)(2,1)S(1)}, bf16[1250,128]{1,0:T(8,128)(2,1)}, u32[]{:S(2)}, u32[]{:S(2)}) collective-permute-start(bf16[1250,128]{1,0:T(8,128)(2,1)S(1)} %get-tuple-element.39.refs_13_), channel_id=1, source_target_pairs={{0,68},{1,69},{2,70},{3,71},{4,64},{5,65},{6,66},{7,67},{8,76},{9,... | collective-permute-start | bytes 960008 | tf_op jit(solution)/shard_map/ppermute | solution.py:33
  15.2 5.0 %collective-permute-start.7 = (bf16[64,1250]{1,0:T(8,128)(2,1)}, bf16[64,1250]{1,0:T(8,128)(2,1)S(1)}, u32[]{:S(2)}, u32[]{:S(2)}) collective-permute-start(bf16[64,1250]{1,0:T(8,128)(2,1)} %collective-permute-done.6), channel_id=1, source_target_pairs={{0,1},{1,0},{2,3},{3,2},{4,5},{5,4},{6,7},{7,6},{8,9},{9,8},{10,11... | collective-permute-start | bytes 480008 | tf_op jit(solution)/shard_map/ppermute | solution.py:33
  16.8 8.0 %collective-permute-start.8 = (bf16[64,1250]{1,0:T(8,128)(2,1)}, bf16[64,1250]{1,0:T(8,128)(2,1)S(1)}, u32[]{:S(2)}, u32[]{:S(2)}) collective-permute-start(bf16[64,1250]{1,0:T(8,128)(2,1)} %collective-permute-done.6), channel_id=1, source_target_pairs={{0,2},{1,3},{2,0},{3,1},{4,6},{5,7},{6,4},{7,5},{8,10},{9,11},{10,... | collective-permute-start | bytes 480008 | tf_op jit(solution)/shard_map/ppermute | solution.py:33
  20.2 19.0 %collective-permute-start.16 = (bf16[1250,128]{1,0:T(8,128)(2,1)S(1)}, bf16[1250,128]{1,0:T(8,128)(2,1)S(1)}, u32[]{:S(2)}, u32[]{:S(2)}) collective-permute-start(bf16[1250,128]{1,0:T(8,128)(2,1)S(1)} %get-tuple-element.39.refs_13_), channel_id=1, source_target_pairs={{0,4},{1,5},{2,6},{3,7},{4,0},{5,1},{6,2},{7,3},{8,12},{9,13},{10,... | collective-permute-start | bytes 960008 | tf_op jit(solution)/shard_map/ppermute | solution.py:33
  25.5 6.0 %collective-permute-start.9 = (bf16[64,1250]{1,0:T(8,128)(2,1)}, bf16[64,1250]{1,0:T(8,128)(2,1)}, u32[]{:S(2)}, u32[]{:S(2)}) collective-permute-start(bf16[64,1250]{1,0:T(8,128)(2,1)} %collective-permute-done.6), channel_id=1, source_target_pairs={{0,3},{1,2},{2,1},{3,0},{4,7},{5,6},{6,5},{7,4},{8,11},{9,10},{10,... | collective-permute-start | bytes 480008 | tf_op jit(solution)/shard_map/ppermute | solution.py:33
  31.5 18.3 %collective-permute-start.3 = (bf16[256,1250]{0,1:T(8,128)(2,1)}, bf16[256,1250]{0,1:T(8,128)(2,1)}, u32[]{:S(2)}, u32[]{:S(2)}) collective-permute-start(bf16[256,1250]{0,1:T(8,128)(2,1)} %copy.31), channel_id=1, source_target_pairs={{0,1},{1,0},{2,3},{3,2},{4,5},{5,4},{6,7},{7,6},{8,9},{9,8},{10,11... | collective-permute-start | bytes 1920008 | tf_op jit(solution)/shard_map/ppermute | solution.py:33
  32.4 10.9 %collective-permute-start.30 = (bf16[1250,128]{1,0:T(8,128)(2,1)}, bf16[1250,128]{1,0:T(8,128)(2,1)}, u32[]{:S(2)}, u32[]{:S(2)}) collective-permute-start(bf16[1250,128]{1,0:T(8,128)(2,1)} %get-tuple-element.42.refs_9_), channel_id=1, source_target_pairs={{0,4},{1,5},{2,6},{3,7},{4,0},{5,1},{6,2},{7,3},{8,12},{9,13},{10,... | collective-permute-start | bytes 960008 | tf_op jit(solution)/shard_map/ppermute | solution.py:33
  33.8 9.5 %collective-permute-start.34 = (bf16[1250,128]{1,0:T(8,128)(2,1)S(1)}, bf16[1250,128]{1,0:T(8,128)(2,1)}, u32[]{:S(2)}, u32[]{:S(2)}) collective-permute-start(bf16[1250,128]{1,0:T(8,128)(2,1)S(1)} %get-tuple-element.41.refs_13_), channel_id=1, source_target_pairs={{0,68},{1,69},{2,70},{3,71},{4,64},{5,65},{6,66},{7,67},{8,76},{9,... | collective-permute-start | bytes 960008 | tf_op jit(solution)/shard_map/ppermute | solution.py:33
  35.4 25.4 %collective-permute-start.4 = (bf16[256,1250]{0,1:T(8,128)(2,1)}, bf16[256,1250]{0,1:T(8,128)(2,1)}, u32[]{:S(2)}, u32[]{:S(2)}) collective-permute-start(bf16[256,1250]{0,1:T(8,128)(2,1)} %copy.31), channel_id=1, source_target_pairs={{0,2},{1,3},{2,0},{3,1},{4,6},{5,7},{6,4},{7,5},{8,10},{9,11},{10,... | collective-permute-start | bytes 1920008 | tf_op jit(solution)/shard_map/ppermute | solution.py:33
  39.3 10.6 %collective-permute-start.14 = (bf16[1250,128]{1,0:T(8,128)(2,1)S(1)}, bf16[1250,128]{1,0:T(8,128)(2,1)S(1)}, u32[]{:S(2)}, u32[]{:S(2)}) collective-permute-start(bf16[1250,128]{1,0:T(8,128)(2,1)S(1)} %collective-permute-done.13.refs_10_), channel_id=1, source_target_pairs={{0,68},{1,69},{2,70},{3,71},{4,64},{5,65},{6,66},{7,67},{8,76},{9,... | collective-permute-start | bytes 960008 | tf_op jit(solution)/shard_map/ppermute | solution.py:33
  43.3 28.9 %collective-permute-start.5 = (bf16[256,1250]{0,1:T(8,128)(2,1)}, bf16[256,1250]{0,1:T(8,128)(2,1)}, u32[]{:S(2)}, u32[]{:S(2)}) collective-permute-start(bf16[256,1250]{0,1:T(8,128)(2,1)} %copy.31), channel_id=1, source_target_pairs={{0,3},{1,2},{2,1},{3,0},{4,7},{5,6},{6,5},{7,4},{8,11},{9,10},{10,... | collective-permute-start | bytes 1920008 | tf_op jit(solution)/shard_map/ppermute | solution.py:33
  43.3 30.6 %collective-permute-start.10 = (bf16[256,1250]{0,1:T(8,128)(2,1)}, bf16[256,1250]{0,1:T(8,128)(2,1)}, u32[]{:S(2)}, u32[]{:S(2)}) collective-permute-start(bf16[256,1250]{0,1:T(8,128)(2,1)} %copy.35), channel_id=1, source_target_pairs={{0,8},{1,9},{2,10},{3,11},{4,12},{5,13},{6,14},{7,15},{8,0},{9,1},... | collective-permute-start | bytes 1920008 | tf_op jit(solution)/shard_map/ppermute | solution.py:33
  49.8 24.1 %collective-permute-start.11 = (bf16[256,1250]{0,1:T(8,128)(2,1)}, bf16[256,1250]{0,1:T(8,128)(2,1)}, u32[]{:S(2)}, u32[]{:S(2)}) collective-permute-start(bf16[256,1250]{0,1:T(8,128)(2,1)} %copy.35), channel_id=1, source_target_pairs={{0,16},{1,17},{2,18},{3,19},{4,20},{5,21},{6,22},{7,23},{8,24},{9,... | collective-permute-start | bytes 1920008 | tf_op jit(solution)/shard_map/ppermute | solution.py:33
  49.8 29.8 %collective-permute-start.12 = (bf16[256,1250]{0,1:T(8,128)(2,1)}, bf16[256,1250]{0,1:T(8,128)(2,1)}, u32[]{:S(2)}, u32[]{:S(2)}) collective-permute-start(bf16[256,1250]{0,1:T(8,128)(2,1)} %copy.35), channel_id=1, source_target_pairs={{0,24},{1,25},{2,26},{3,27},{4,28},{5,29},{6,30},{7,31},{8,16},{9,... | collective-permute-start | bytes 1920008 | tf_op jit(solution)/shard_map/ppermute | solution.py:33
  60.8 31.3 %collective-permute-start.18 = (bf16[1250,128]{1,0:T(8,128)(2,1)}, bf16[1250,128]{1,0:T(8,128)(2,1)S(1)}, u32[]{:S(2)}, u32[]{:S(2)}) collective-permute-start(bf16[1250,128]{1,0:T(8,128)(2,1)} %collective-permute-done.17.refs_16_), channel_id=1, source_target_pairs={{0,4},{1,5},{2,6},{3,7},{4,0},{5,1},{6,2},{7,3},{8,12},{9,13},{10,... | collective-permute-start | bytes 960008 | tf_op jit(solution)/shard_map/ppermute | solution.py:33
  72.3 40.5 %collective-permute-start.32 = (bf16[1250,128]{1,0:T(8,128)(2,1)}, bf16[1250,128]{1,0:T(8,128)(2,1)}, u32[]{:S(2)}, u32[]{:S(2)}) collective-permute-start(bf16[1250,128]{1,0:T(8,128)(2,1)} %get-tuple-element.42.refs_9_), channel_id=1, source_target_pairs={{0,68},{1,69},{2,70},{3,71},{4,64},{5,65},{6,66},{7,67},{8,76},{9,... | collective-permute-start | bytes 960008 | tf_op jit(solution)/shard_map/ppermute | solution.py:33
  73.9 38.8 %collective-permute-start.33 = (bf16[1250,128]{1,0:T(8,128)(2,1)S(1)}, bf16[1250,128]{1,0:T(8,128)(2,1)}, u32[]{:S(2)}, u32[]{:S(2)}) collective-permute-start(bf16[1250,128]{1,0:T(8,128)(2,1)S(1)} %get-tuple-element.41.refs_13_), channel_id=1, source_target_pairs={{0,4},{1,5},{2,6},{3,7},{4,0},{5,1},{6,2},{7,3},{8,12},{9,13},{10,... | collective-permute-start | bytes 960008 | tf_op jit(solution)/shard_map/ppermute | solution.py:33
  73.9 38.8 %collective-permute-start.31 = (bf16[1250,128]{1,0:T(8,128)(2,1)}, bf16[1250,128]{1,0:T(8,128)(2,1)}, u32[]{:S(2)}, u32[]{:S(2)}) collective-permute-start(bf16[1250,128]{1,0:T(8,128)(2,1)} %collective-permute-done.30.refs_10_), channel_id=1, source_target_pairs={{0,68},{1,69},{2,70},{3,71},{4,64},{5,65},{6,66},{7,67},{8,76},{9,... | collective-permute-start | bytes 960008 | tf_op jit(solution)/shard_map/ppermute | solution.py:33
  79.6 33.2 %collective-permute-start.35 = (bf16[1250,128]{1,0:T(8,128)(2,1)}, bf16[1250,128]{1,0:T(8,128)(2,1)}, u32[]{:S(2)}, u32[]{:S(2)}) collective-permute-start(bf16[1250,128]{1,0:T(8,128)(2,1)} %collective-permute-done.34.refs_16_), channel_id=1, source_target_pairs={{0,4},{1,5},{2,6},{3,7},{4,0},{5,1},{6,2},{7,3},{8,12},{9,13},{10,... | collective-permute-start | bytes 960008 | tf_op jit(solution)/shard_map/ppermute | solution.py:33
  110.2 13.8 %collective-permute-start.19 = (f32[2,1024,128]{2,1,0:T(8,128)}, f32[2,1024,128]{2,1,0:T(8,128)}, u32[]{:S(2)}, u32[]{:S(2)}) collective-permute-start(f32[2,1024,128]{2,1,0:T(8,128)} %get-tuple-element.22), channel_id=1, source_target_pairs={{0,32},{1,33},{2,34},{3,35},{4,36},{5,37},{6,38},{7,39},{8,40},{9,... | collective-permute-start | bytes 3145736 | tf_op jit(solution)/shard_map/ppermute | solution.py:33
  119.3 12.7 %collective-permute-start.36 = (f32[2,1024,128]{2,1,0:T(8,128)}, f32[2,1024,128]{2,1,0:T(8,128)}, u32[]{:S(2)}, u32[]{:S(2)}) collective-permute-start(f32[2,1024,128]{2,1,0:T(8,128)} %get-tuple-element.30), channel_id=1, source_target_pairs={{0,32},{1,33},{2,34},{3,35},{4,36},{5,37},{6,38},{7,39},{8,40},{9,... | collective-permute-start | bytes 3145736 | tf_op jit(solution)/shard_map/ppermute | solution.py:33
  127.2 10.2 %collective-permute-start.20 = (bf16[64,2048]{1,0:T(8,128)(2,1)S(1)}, bf16[64,2048]{1,0:T(8,128)(2,1)S(1)}, u32[]{:S(2)}, u32[]{:S(2)}) collective-permute-start(bf16[64,2048]{1,0:T(8,128)(2,1)S(1)} %get-tuple-element.24), channel_id=1, source_target_pairs={{0,4},{1,5},{2,6},{3,7},{4,0},{5,1},{6,2},{7,3},{8,12},{9,13},{10,... | collective-permute-start | bytes 786440 | tf_op jit(solution)/shard_map/ppermute | solution.py:33
  129.1 14.6 %collective-permute-start.22 = (bf16[64,2048]{1,0:T(8,128)(2,1)S(1)}, bf16[64,2048]{1,0:T(8,128)(2,1)S(1)}, u32[]{:S(2)}, u32[]{:S(2)}) collective-permute-start(bf16[64,2048]{1,0:T(8,128)(2,1)S(1)} %get-tuple-element.24), channel_id=1, source_target_pairs={{0,68},{1,69},{2,70},{3,71},{4,64},{5,65},{6,66},{7,67},{8,76},{9,... | collective-permute-start | bytes 786440 | tf_op jit(solution)/shard_map/ppermute | solution.py:33
  129.6 11.6 %collective-permute-start.21 = (bf16[64,2048]{1,0:T(8,128)(2,1)S(1)}, bf16[64,2048]{1,0:T(8,128)(2,1)S(1)}, u32[]{:S(2)}, u32[]{:S(2)}) collective-permute-start(bf16[64,2048]{1,0:T(8,128)(2,1)S(1)} %get-tuple-element.23.refs_0_), channel_id=1, source_target_pairs={{0,64},{1,65},{2,66},{3,67},{4,68},{5,69},{6,70},{7,71},{8,72},{9,... | collective-permute-start | bytes 786440 | tf_op jit(solution)/shard_map/ppermute | solution.py:33
  130.9 15.2 %collective-permute-start.23 = (bf16[64,2048]{1,0:T(8,128)(2,1)S(1)}, bf16[64,2048]{1,0:T(8,128)(2,1)S(1)}, u32[]{:S(2)}, u32[]{:S(2)}) collective-permute-start(bf16[64,2048]{1,0:T(8,128)(2,1)S(1)} %get-tuple-element.23.refs_0_), channel_id=1, source_target_pairs={{0,32},{1,33},{2,34},{3,35},{4,36},{5,37},{6,38},{7,39},{8,40},{9,... | collective-permute-start | bytes 786440 | tf_op jit(solution)/shard_map/ppermute | solution.py:33
  135.3 11.3 %collective-permute-start.37 = (bf16[64,2048]{1,0:T(8,128)(2,1)S(1)}, bf16[64,2048]{1,0:T(8,128)(2,1)S(1)}, u32[]{:S(2)}, u32[]{:S(2)}) collective-permute-start(bf16[64,2048]{1,0:T(8,128)(2,1)S(1)} %get-tuple-element.32), channel_id=1, source_target_pairs={{0,4},{1,5},{2,6},{3,7},{4,0},{5,1},{6,2},{7,3},{8,12},{9,13},{10,... | collective-permute-start | bytes 786440 | tf_op jit(solution)/shard_map/ppermute | solution.py:33
  137.4 16.8 %collective-permute-start.39 = (bf16[64,2048]{1,0:T(8,128)(2,1)S(1)}, bf16[64,2048]{1,0:T(8,128)(2,1)S(1)}, u32[]{:S(2)}, u32[]{:S(2)}) collective-permute-start(bf16[64,2048]{1,0:T(8,128)(2,1)S(1)} %get-tuple-element.32), channel_id=1, source_target_pairs={{0,68},{1,69},{2,70},{3,71},{4,64},{5,65},{6,66},{7,67},{8,76},{9,... | collective-permute-start | bytes 786440 | tf_op jit(solution)/shard_map/ppermute | solution.py:33
  141.2 11.3 %collective-permute-start.38 = (bf16[64,2048]{1,0:T(8,128)(2,1)S(1)}, bf16[64,2048]{1,0:T(8,128)(2,1)S(1)}, u32[]{:S(2)}, u32[]{:S(2)}) collective-permute-start(bf16[64,2048]{1,0:T(8,128)(2,1)S(1)} %get-tuple-element.31.refs_0_), channel_id=1, source_target_pairs={{0,64},{1,65},{2,66},{3,67},{4,68},{5,69},{6,70},{7,71},{8,72},{9,... | collective-permute-start | bytes 786440 | tf_op jit(solution)/shard_map/ppermute | solution.py:33
  143.6 12.2 %collective-permute-start.24 = (bf16[64,2048]{1,0:T(8,128)(2,1)S(1)}, bf16[64,2048]{1,0:T(8,128)(2,1)S(1)}, u32[]{:S(2)}, u32[]{:S(2)}) collective-permute-start(bf16[64,2048]{1,0:T(8,128)(2,1)S(1)} %collective-permute-done.20.refs_1_), channel_id=1, source_target_pairs={{0,32},{1,33},{2,34},{3,35},{4,36},{5,37},{6,38},{7,39},{8,40},{9,... | collective-permute-start | bytes 786440 | tf_op jit(solution)/shard_map/ppermute | solution.py:33
  146.2 9.7 %collective-permute-start.25 = (bf16[64,2048]{1,0:T(8,128)(2,1)S(1)}, bf16[64,2048]{1,0:T(8,128)(2,1)S(1)}, u32[]{:S(2)}, u32[]{:S(2)}) collective-permute-start(bf16[64,2048]{1,0:T(8,128)(2,1)S(1)} %collective-permute-done.21.refs_2_), channel_id=1, source_target_pairs={{0,32},{1,33},{2,34},{3,35},{4,36},{5,37},{6,38},{7,39},{8,40},{9,... | collective-permute-start | bytes 786440 | tf_op jit(solution)/shard_map/ppermute | solution.py:33
  146.6 9.8 %collective-permute-start.26 = (bf16[64,2048]{1,0:T(8,128)(2,1)S(1)}, bf16[64,2048]{1,0:T(8,128)(2,1)S(1)}, u32[]{:S(2)}, u32[]{:S(2)}) collective-permute-start(bf16[64,2048]{1,0:T(8,128)(2,1)S(1)} %collective-permute-done.22.refs_3_), channel_id=1, source_target_pairs={{0,32},{1,33},{2,34},{3,35},{4,36},{5,37},{6,38},{7,39},{8,40},{9,... | collective-permute-start | bytes 786440 | tf_op jit(solution)/shard_map/ppermute | solution.py:33
  152.5 8.6 %collective-permute-start.40 = (bf16[64,2048]{1,0:T(8,128)(2,1)S(1)}, bf16[64,2048]{1,0:T(8,128)(2,1)S(1)}, u32[]{:S(2)}, u32[]{:S(2)}) collective-permute-start(bf16[64,2048]{1,0:T(8,128)(2,1)S(1)} %get-tuple-element.31.refs_0_), channel_id=1, source_target_pairs={{0,32},{1,33},{2,34},{3,35},{4,36},{5,37},{6,38},{7,39},{8,40},{9,... | collective-permute-start | bytes 786440 | tf_op jit(solution)/shard_map/ppermute | solution.py:33
  154.2 8.5 %collective-permute-start.41 = (bf16[64,2048]{1,0:T(8,128)(2,1)S(1)}, bf16[64,2048]{1,0:T(8,128)(2,1)S(1)}, u32[]{:S(2)}, u32[]{:S(2)}) collective-permute-start(bf16[64,2048]{1,0:T(8,128)(2,1)S(1)} %collective-permute-done.37.refs_1_), channel_id=1, source_target_pairs={{0,32},{1,33},{2,34},{3,35},{4,36},{5,37},{6,38},{7,39},{8,40},{9,... | collective-permute-start | bytes 786440 | tf_op jit(solution)/shard_map/ppermute | solution.py:33
  155.8 9.2 %collective-permute-start.42 = (bf16[64,2048]{1,0:T(8,128)(2,1)S(1)}, bf16[64,2048]{1,0:T(8,128)(2,1)S(1)}, u32[]{:S(2)}, u32[]{:S(2)}) collective-permute-start(bf16[64,2048]{1,0:T(8,128)(2,1)S(1)} %collective-permute-done.38.refs_2_), channel_id=1, source_target_pairs={{0,32},{1,33},{2,34},{3,35},{4,36},{5,37},{6,38},{7,39},{8,40},{9,... | collective-permute-start | bytes 786440 | tf_op jit(solution)/shard_map/ppermute | solution.py:33
  155.9 9.2 %collective-permute-start.43 = (bf16[64,2048]{1,0:T(8,128)(2,1)S(1)}, bf16[64,2048]{1,0:T(8,128)(2,1)S(1)}, u32[]{:S(2)}, u32[]{:S(2)}) collective-permute-start(bf16[64,2048]{1,0:T(8,128)(2,1)S(1)} %collective-permute-done.39.refs_3_), channel_id=1, source_target_pairs={{0,32},{1,33},{2,34},{3,35},{4,36},{5,37},{6,38},{7,39},{8,40},{9,... | collective-permute-start | bytes 786440 | tf_op jit(solution)/shard_map/ppermute | solution.py:33
  161.0 8.1 %collective-permute-start.27 = (bf16[256,512]{1,0:T(8,128)(2,1)S(1)}, bf16[256,512]{1,0:T(8,128)(2,1)S(1)}, u32[]{:S(2)}, u32[]{:S(2)}) collective-permute-start(bf16[256,512]{1,0:T(8,128)(2,1)S(1)} %get-tuple-element.26), channel_id=1, source_target_pairs={{0,1},{1,0},{2,3},{3,2},{4,5},{5,4},{6,7},{7,6},{8,9},{9,8},{10,11... | collective-permute-start | bytes 786440 | tf_op jit(solution)/shard_map/ppermute | solution.py:33
  161.1 13.5 %collective-permute-start.28 = (bf16[256,512]{1,0:T(8,128)(2,1)S(1)}, bf16[256,512]{1,0:T(8,128)(2,1)S(1)}, u32[]{:S(2)}, u32[]{:S(2)}) collective-permute-start(bf16[256,512]{1,0:T(8,128)(2,1)S(1)} %get-tuple-element.27), channel_id=1, source_target_pairs={{0,2},{1,3},{2,0},{3,1},{4,6},{5,7},{6,4},{7,5},{8,10},{9,11},{10,... | collective-permute-start | bytes 786440 | tf_op jit(solution)/shard_map/ppermute | solution.py:33
  162.7 14.1 %collective-permute-start.29 = (bf16[256,512]{1,0:T(8,128)(2,1)S(1)}, bf16[256,512]{1,0:T(8,128)(2,1)S(1)}, u32[]{:S(2)}, u32[]{:S(2)}) collective-permute-start(bf16[256,512]{1,0:T(8,128)(2,1)S(1)} %get-tuple-element.28), channel_id=1, source_target_pairs={{0,3},{1,2},{2,1},{3,0},{4,7},{5,6},{6,5},{7,4},{8,11},{9,10},{10,... | collective-permute-start | bytes 786440 | tf_op jit(solution)/shard_map/ppermute | solution.py:33
  167.4 12.8 %collective-permute-start.44 = (bf16[256,512]{1,0:T(8,128)(2,1)S(1)}, bf16[256,512]{1,0:T(8,128)(2,1)S(1)}, u32[]{:S(2)}, u32[]{:S(2)}) collective-permute-start(bf16[256,512]{1,0:T(8,128)(2,1)S(1)} %get-tuple-element.34), channel_id=1, source_target_pairs={{0,1},{1,0},{2,3},{3,2},{4,5},{5,4},{6,7},{7,6},{8,9},{9,8},{10,11... | collective-permute-start | bytes 786440 | tf_op jit(solution)/shard_map/ppermute | solution.py:33
  167.5 18.4 %collective-permute-start.45 = (bf16[256,512]{1,0:T(8,128)(2,1)S(1)}, bf16[256,512]{1,0:T(8,128)(2,1)S(1)}, u32[]{:S(2)}, u32[]{:S(2)}) collective-permute-start(bf16[256,512]{1,0:T(8,128)(2,1)S(1)} %get-tuple-element.35), channel_id=1, source_target_pairs={{0,2},{1,3},{2,0},{3,1},{4,6},{5,7},{6,4},{7,5},{8,10},{9,11},{10,... | collective-permute-start | bytes 786440 | tf_op jit(solution)/shard_map/ppermute | solution.py:33
  169.0 18.9 %collective-permute-start.46 = (bf16[256,512]{1,0:T(8,128)(2,1)S(1)}, bf16[256,512]{1,0:T(8,128)(2,1)S(1)}, u32[]{:S(2)}, u32[]{:S(2)}) collective-permute-start(bf16[256,512]{1,0:T(8,128)(2,1)S(1)} %get-tuple-element.36), channel_id=1, source_target_pairs={{0,3},{1,2},{2,1},{3,0},{4,7},{5,6},{6,5},{7,4},{8,11},{9,10},{10,... | collective-permute-start | bytes 786440 | tf_op jit(solution)/shard_map/ppermute | solution.py:33
  (30 other events, 303.3 us)

commit v2 on v0

v2 whole, which is shorter than its diff:
```python
import functools

import jax
import jax.numpy as jnp
import numpy as np
from jax import lax
from jax.experimental import pallas as pl
from jax.experimental.pallas import tpu as pltpu
from jax.sharding import PartitionSpec as P

CHUNKS = 2
AXES = ("xh", "core", "y", "xl", "z")
SHAPE = (2, 2, 4, 2, 4)
VMEM = pl.BlockSpec(memory_space=pltpu.VMEM)
SMEM = pl.BlockSpec(memory_space=pltpu.SMEM)
HBM = pl.BlockSpec(memory_space=pltpu.HBM)
MIB = 1 << 20
BF16 = jnp.bfloat16
F32 = jnp.float32
XH, CORE, Y, XL, Z = range(5)


def swap_table(xh=0, core=0, y=0, xl=0, z=0):
    by = (xh, core, y, xl, z)
    table = []
    for i in range(128):
        to = tuple(int(v) ^ w for v, w in zip(np.unravel_index(i, SHAPE), by))
        table.append((i, int(np.ravel_multi_index(to, SHAPE))))
    return table


def swap(x, **by):
    return lax.ppermute(x, AXES, swap_table(**by))


def dot_nt(u, v):
    return lax.dot_general(u, v, (((1,), (1,)), ((), ())), preferred_element_type=jnp.float32)


def call(body, shapes, inputs, places, name, out_place=None, scratch=(), limit=4, flops=0, size=MIB, **more):
    many = isinstance(shapes, list)
    shapes = shapes if many else [shapes]
    got = pl.pallas_call(
        body,
        out_shape=[jax.ShapeDtypeStruct(*v) for v in shapes],
        in_specs=places,
        out_specs=[out_place or VMEM] * len(shapes),
        scratch_shapes=list(scratch),
        compiler_params=pltpu.CompilerParams(vmem_limit_bytes=limit * MIB),
        cost_estimate=pl.CostEstimate(flops=flops, bytes_accessed=size, transcendentals=0),
        name=name,
        **more,
    )(*inputs)
    return got if many else got[0]


def split_kernel(at, left, mine, theirs):
    t = left[...].T
    upper, lower = t[:64], t[64:]
    mine[...] = jnp.where(at[XH] == 0, upper, lower)
    theirs[...] = jnp.where(at[XH] == 0, lower, upper)


def split(at, left):
    return call(split_kernel, [((64, 1280), BF16)] * 2, (at, left), [SMEM, VMEM], "split")


def cut_kernel(cuts, source, *refs):
    for cut, out in zip(cuts, refs[len(refs) - len(cuts):]):
        out[...] = source[cut]


def cut(source, cuts, after=()):
    shapes = [(tuple(len(range(n)[c]) for c, n in zip(cut, source.shape)), BF16) for cut in cuts]
    return call(functools.partial(cut_kernel, cuts), shapes, (source, *after), [VMEM] + [HBM] * len(after), "cut")


def stack_kernel(n, *refs):
    for i in range(n):
        refs[-1][i * 64:(i + 1) * 64, :] = refs[i][...]


def stack(pieces, after=()):
    n = len(pieces)
    shape = ((64 * n, pieces[0].shape[1]), BF16)
    return call(functools.partial(stack_kernel, n), shape, (*pieces, *after), [VMEM] * n + [HBM] * len(after), "stack")


def tile_kernel(at, *refs):
    la, lb, r = refs[0:5], refs[5:10], refs[10:15]
    keep, send, acc = refs[-3:]
    first = at[CORE] == 0
    place = ((0, 0, 4), (1, 0, 4), (3, 0, 4), (2, 0, 2), (2, 2, 2))
    for part in range(2):
        right = r[part][...]
        for k, (zr, start, count) in enumerate(place):
            out = jnp.dot(la[k][:, :1250], right, preferred_element_type=jnp.float32)
            for i in range(count):
                acc[part, start + i, at[Z] ^ zr] = out[i * 64:(i + 1) * 64]
    for part in range(2):
        right = jnp.concatenate([r[3][...], r[4][...]], axis=1) if part == 0 else r[2][...]
        for k, (yr, start, count) in enumerate(place):
            out = jnp.dot(lb[k][:, :1250], right, preferred_element_type=jnp.float32)
            for i in range(count):
                zs = at[Z] ^ (start + i)
                total = acc[part, yr, zs] + out[i * 64:(i + 1) * 64]
                rows = pl.ds(pl.multiple_of(yr * 256 + zs * 64, 64), 64)
                keep[part, rows, :] = jnp.where(first, total[:, :128], total[:, 128:])
                send[part, rows, :] = jnp.where(first, total[:, 128:], total[:, :128])


def tile(at, la, lb, r, after=()):
    return call(
        tile_kernel,
        [((2, 1024, 128), F32)] * 2,
        (at, *la, *lb, *r, *after),
        [SMEM] + [VMEM] * 15 + [HBM] * len(after),
        "tile",
        scratch=[pltpu.VMEM((2, 4, 4, 64, 256), F32)],
        limit=6,
        flops=2 * 1024 * 2500 * 512,
        size=10 * MIB,
    )


def turn_kernel(keep, got, own, other):
    lane = lax.broadcasted_iota(jnp.int32, (16, 128), 1)
    odd = (lane // 32) % 2 == 1
    high = lane // 64 == 1
    for part, out in ((0, own), (1, other)):
        for group in range(16):
            v = []
            for c in range(4):
                rows = pl.ds(group * 4 + c, 16, stride=64)
                v.append(keep[part, rows, :] + got[part, rows, :])
            w = [
                jnp.where(odd, pltpu.roll(v[1], 32, 1), v[0]),
                jnp.where(odd, v[1], pltpu.roll(v[0], 96, 1)),
                jnp.where(odd, pltpu.roll(v[3], 32, 1), v[2]),
                jnp.where(odd, v[3], pltpu.roll(v[2], 96, 1)),
            ]
            t = [
                jnp.where(high, pltpu.roll(w[2], 64, 1), w[0]),
                jnp.where(high, pltpu.roll(w[3], 64, 1), w[1]),
                jnp.where(high, w[2], pltpu.roll(w[0], 64, 1)),
                jnp.where(high, w[3], pltpu.roll(w[1], 64, 1)),
            ]
            for b in range(4):
                out[b * 16:(b + 1) * 16, group * 128:(group + 1) * 128] = t[b].astype(jnp.bfloat16)


def turn(keep, got):
    return call(turn_kernel, [((64, 2048), BF16)] * 2, (keep, got), [VMEM] * 2, "turn", size=3 * MIB)


def ladder_kernel(at, amp, mine, peer, own, *out):
    for s in range(4):
        rows = pl.ds(pl.multiple_of((at[Z] ^ s) * 256, 256), 256)
        for k, part in enumerate((mine, peer)):
            lanes = slice(k * 256, (k + 1) * 256)
            total = dot_nt(amp[rows, :], part[...])
            if s == 0:
                own[:, lanes] = total
            else:
                out[s - 1][:, lanes] = total.astype(BF16)


def ladder(at, amp, mine, peer):
    shapes = [((256, 512), F32)] + [((256, 512), BF16)] * 3
    inputs = (at, amp, mine, peer)
    return call(ladder_kernel, shapes, inputs, [SMEM] + [VMEM] * 3, "ladder", flops=2 * 1024 * 2048 * 512, size=8 * MIB)


def finish_kernel(j, own, r1, r2, r3, order, scale, *refs):
    out, held, sem = refs[-3:]
    total = own[...] + r1[...].astype(F32) + r2[...].astype(F32) + r3[...].astype(F32)
    turned = None
    for _ in range(3):
        term = total.astype(BF16)
        total = total - term.astype(F32)
        placed = jnp.dot(term, order[...], preferred_element_type=F32)
        turned = placed if turned is None else turned + placed
    lanes = pl.ds(j * 512, 512)
    held[...] = turned * scale[:, lanes]
    copy = pltpu.make_async_copy(held, out.at[:, lanes], sem)
    copy.start()
    copy.wait()


def finish(j, own, got, order, scale, out):
    before = [] if out is None else [out]
    return call(
        functools.partial(finish_kernel, j),
        ((256, 1024), F32),
        (own, *got, order, scale, *before),
        [VMEM] * 6 + [HBM] * len(before),
        "finish",
        out_place=HBM,
        scratch=[pltpu.VMEM((256, 512), F32), pltpu.SemaphoreType.DMA],
        flops=6 * 256 * 512 * 512,
        size=4 * MIB,
        input_output_aliases={6: 0} if before else {},
    )


def prepare_kernel(at, offsets, virt, pairs, occ, order, scale):
    s = lax.broadcasted_iota(jnp.int32, (512, 1), 0)
    pc, px, b, yr, zr = s // 256, (s // 64) % 4, (s // 16) % 4, (s // 4) % 4, s % 4
    xl, xh = at[XL] ^ (px % 2), at[XH] ^ (px // 2)
    target = (4 * (at[CORE] ^ pc) + b) * 64 + 16 * (at[Y] ^ yr) + 8 * xl + 2 * zr + xh
    columns = lax.broadcasted_iota(jnp.int32, (512, 512), 1)
    order[...] = jnp.where(columns == target, 1.0, 0.0).astype(BF16)

    lane = lax.broadcasted_iota(jnp.int32, (8, 128), 1)
    ea = jnp.zeros((8, 128), F32)
    for a in range(64):
        ea = jnp.where(lane % 64 == a, virt[offsets[0] + a], ea)
    b_start = offsets[1] + (at[Y] * 2 + at[XL]) * 16
    first, second = pairs[:, 0:1], pairs[:, 1:2]
    levels = lax.broadcasted_iota(jnp.int32, (256, 120), 1)
    occupied = jnp.sum(jnp.where(levels == first, occ[...], 0.0), axis=1, keepdims=True)
    occupied += jnp.sum(jnp.where(levels == second, occ[...], 0.0), axis=1, keepdims=True)
    weight = jnp.where(first == second, 0.5, 1.0)
    for b in range(0, 16, 2):
        eb = jnp.where(lane < 64, virt[b_start + b], virt[b_start + b + 1])
        scale[:, b * 64:(b + 2) * 64] = weight / ((eb + ea)[:1] - occupied)


def prepare(at, offsets, virt, pairs, occ):
    return call(
        prepare_kernel,
        [((512, 512), BF16), ((256, 1024), F32)],
        (at, offsets, virt, pairs, occ.reshape(1, -1)),
        [SMEM] * 3 + [VMEM] * 2,
        "prepare",
    )


def spread(x, axis):
    one, three = swap(x, **{axis: 1}), swap(x, **{axis: 3})
    (upper,), (lower,) = cut(one, [np.s_[:128, :]]), cut(three, [np.s_[128:, :]])
    return [x, one, three, swap(upper, **{axis: 3}), swap(lower, **{axis: 1})]


def around(x):
    one, three = swap(x, xl=1), swap(x, xl=1, xh=1)
    (near,), (far,) = cut(one, [np.s_[:, :128]]), cut(three, [np.s_[:, 128:]])
    return [x, one, three, swap(near, xl=1, xh=1), swap(far, xl=1)]


def per_device(left, right, amplitudes, pair_list, offsets, occ_energy, virt_energy):
    at = jnp.stack([lax.axis_index(n) for n in AXES]).astype(jnp.int32)
    right = right.reshape(right.shape[0], 512)
    amp = amplitudes.reshape(1024, 2048)

    mine, theirs = split(at, jnp.pad(left, ((0, 30), (0, 0))))
    far = swap(theirs, xh=1)
    mine = stack([mine], (far,))
    far4 = [far] + [swap(far, z=s) for s in (1, 2, 3)]
    mine4 = [mine] + [swap(mine, y=s) for s in (1, 2, 3)]
    la = spread(stack(mine4, tuple(far4[1:])), "z")
    lb = spread(stack(far4, tuple(mine4[1:])), "y")

    r = [around(v) for v in cut(right, [np.s_[:, :256], np.s_[:, 256:]], (far,))]
    order, scale = prepare(at, offsets, virt_energy, pair_list, occ_energy)

    turned, after = [], ()
    for j in range(CHUNKS):
        keep, send = tile(at, la, lb, r[j], after)
        turned.append(turn(keep, swap(send, core=1)))
    out, after = None, (turned[1][0],)
    for j in range(CHUNKS):
        own, other = turned[j]
        held = stack([own, swap(other, xl=1), swap(own, xh=1), swap(other, xl=1, xh=1)], after)
        l0, l1, l2, l3 = ladder(at, amp, held, swap(held, core=1))
        got = [swap(l1, z=1), swap(l2, z=2), swap(l3, z=3)]
        after = (got[0], got[2])
        out = finish(j, l0, got, order, scale, out)
    return out


def solution(mesh):
    mesh = jax.sharding.Mesh(mesh.devices.reshape(SHAPE), AXES)
    rows, cols = ("xh", "core"), ("y", "xl")
    placed = (
        P(rows, (*cols, "z")),
        P(rows, "z", cols),
        P(rows, "z", None),
        P((*rows, "z"), None),
        P(),
        P(),
        P(),
    )
    return jax.shard_map(
        per_device,
        mesh=mesh,
        in_specs=placed,
        out_specs=P((*rows, "z"), cols),
        check_vma=False,
    )
```

time: 472 us -> 145 us (0.31)
  blocking collectives: 168 us -> 0 us
  waiting for transfers between devices: 217 us -> 54.2 us
  starting transfers between devices: 0.04 us -> 63.2 us
  local copies, waits for them, and re-layouts: 47.8 us -> 2.55 us
  Pallas kernels: 0 us -> 23.4 us
  matrix products: 20.6 us -> 0 us
  between operations: 16 us -> 0.46 us
    all_gather x1 -> x0, waiting for transfers between devices: 173 us -> none  [per_device(): lax.all_gather(left_factor, ('cols', 'depth'), axis=1, tiled=True)]
    psum x1 -> x0, blocking collectives: 168 us -> none  [per_device(): v_tile = lax.psum(v_partial, 'rows').astype(jnp.bfloat16)]
    ppermute x0 -> x39, starting transfers between devices: none -> 63.2 us  [swap(): return lax.ppermute(x, AXES, swap_table(**by))]
    ppermute x0 -> x39, waiting for transfers between devices: none -> 54.2 us  [swap(): return lax.ppermute(x, AXES, swap_table(**by))]
    reduce_scatter x1 -> x0, waiting for transfers between devices: 42.8 us -> none  [per_device(): lax.psum_scatter(jnp.dot(amp_rows, v_tile, preferred_element_type=jnp.flo...]
    reshape x2 -> x0, local copies, waits for them, and re-layouts: 24.4 us -> none  [the longest x1 12.6 us: per_device(): v_tile.reshape(width_a, width_c, b_local, d_local).transpose(1, 3, 2, 0)]
    pallas_call x0 -> x24, Pallas kernels: none -> 23.4 us  [call(): pl.pallas_call(body, out_shape=[jax.ShapeDtypeStruct(*v) for v in shapes]...]
    dot_general x2 -> x0, matrix products: 20.6 us -> none  [the longest x1 10.6 us: per_device(): lax.dot_general(lax.all_gather(left_factor, ('cols', 'depth'), axis=1, ti...]
  transfers between devices with their start and end apart: 2 -> 39, of which waited for: 2 -> 19; matrix products, arithmetic and copies ran while one was open for 1% -> 0% of each run, Pallas kernels for 0% -> 15%
where the time goes in v2:
time: 145 us; the launch traced here: 144 us
  starting transfers between devices  63.2 us (44%)
  waiting for transfers between devices  54.2 us (37%)
  Pallas kernels  23.4 us (16%)
  local copies, waits for them, and re-layouts  2.55 us (2%)
    ppermute x39, starting transfers between devices, swap(): return lax.ppermute(x, AXES, swap_table(**by))  63.2 us
    ppermute x39, waiting for transfers between devices, swap(): return lax.ppermute(x, AXES, swap_table(**by))  54.2 us
    pallas_call x24, Pallas kernels, call(): pl.pallas_call(body, out_shape=[jax.ShapeDtypeStruct(*v) for v in shapes]...  23.4 us
  transfers between devices with their start and end apart: 39, of which 19 were waited for; matrix products, arithmetic and copies ran while one was open for 0% of the time, Pallas kernels for 15%

profile of v2, /device:TPU:1, one launch (start us, length us, event | category | flops | bytes accessed | tf_op | source)
XLA Modules:
  0.0 143.8 jit_solution(13780307037966335964)
XLA Ops:
  1.8 3.7 %collective-permute-start = (bf16[64,1280]{1,0:T(8,128)(2,1)S(1)}, bf16[64,1280]{1,0:T(8,128)(2,1)S(1)}, u32[]{:S(2)}, u32[]{:S(2)}) collective-permute-start(bf16[64,1280]{1,0:T(8,128)(2,1)S(1)} %get-tuple-element.28), channel_id=1, source_target_pairs={{0,64},{1,65},{2,66},{3,67},{4,68},{5,69},{6,70},{7,71},{8,72},{9,... | collective-permute-start | bytes 491528 | tf_op jit(solution)/shard_map/ppermute | solution.py:33
  5.4 3.4 %collective-permute-done.refs_1_.refs_0_ = bf16[64,1280]{1,0:T(8,128)(2,1)S(1)} collective-permute-done((bf16[64,1280]{1,0:T(8,128)(2,1)S(1)}, bf16[64,1280]{1,0:T(8,128)(2,1)S(1)}, u32[]{:S(2)}, u32[]{:S(2)}) %collective-permute-start) | collective-permute-done | bytes 163872 | tf_op jit(solution)/shard_map/ppermute | solution.py:33
  8.9 1.8 %collective-permute-start.1 = (bf16[64,1280]{1,0:T(8,128)(2,1)S(1)}, bf16[64,1280]{1,0:T(8,128)(2,1)S(1)}, u32[]{:S(2)}, u32[]{:S(2)}) collective-permute-start(bf16[64,1280]{1,0:T(8,128)(2,1)S(1)} %stack.29.refs_0_), channel_id=1, source_target_pairs={{0,8},{1,9},{2,10},{3,11},{4,12},{5,13},{6,14},{7,15},{8,0},{9,1},... | collective-permute-start | bytes 491528 | tf_op jit(solution)/shard_map/ppermute | solution.py:33
  10.6 2.6 %collective-permute-start.2 = (bf16[64,1280]{1,0:T(8,128)(2,1)S(1)}, bf16[64,1280]{1,0:T(8,128)(2,1)S(1)}, u32[]{:S(2)}, u32[]{:S(2)}) collective-permute-start(bf16[64,1280]{1,0:T(8,128)(2,1)S(1)} %stack.29.refs_0_), channel_id=1, source_target_pairs={{0,16},{1,17},{2,18},{3,19},{4,20},{5,21},{6,22},{7,23},{8,24},{9,... | collective-permute-start | bytes 491528 | tf_op jit(solution)/shard_map/ppermute | solution.py:33
  13.3 1.6 %collective-permute-start.4 = (bf16[64,1280]{1,0:T(8,128)(2,1)S(1)}, bf16[64,1280]{1,0:T(8,128)(2,1)S(1)}, u32[]{:S(2)}, u32[]{:S(2)}) collective-permute-start(bf16[64,1280]{1,0:T(8,128)(2,1)S(1)} %collective-permute-done.refs_1_.refs_0_), channel_id=1, source_target_pairs={{0,1},{1,0},{2,3},{3,2},{4,5},{5,4},{6,7},{7,6},{8,9},{9,8},{10,11... | collective-permute-start | bytes 491528 | tf_op jit(solution)/shard_map/ppermute | solution.py:33
  14.9 3.3 %collective-permute-start.5 = (bf16[64,1280]{1,0:T(8,128)(2,1)S(1)}, bf16[64,1280]{1,0:T(8,128)(2,1)S(1)}, u32[]{:S(2)}, u32[]{:S(2)}) collective-permute-start(bf16[64,1280]{1,0:T(8,128)(2,1)S(1)} %collective-permute-done.refs_1_.refs_0_), channel_id=1, source_target_pairs={{0,2},{1,3},{2,0},{3,1},{4,6},{5,7},{6,4},{7,5},{8,10},{9,11},{10,... | collective-permute-start | bytes 491528 | tf_op jit(solution)/shard_map/ppermute | solution.py:33
  18.2 1.3 copy-done
  19.6 1.3 collective-permute-start.23
  22.1 1.2 collective-permute-done.5.refs_5_.refs_2_
  24.6 2.5 %collective-permute-start.24 = (bf16[1250,256]{1,0:T(8,128)(2,1)S(1)}, bf16[1250,256]{1,0:T(8,128)(2,1)S(1)}, u32[]{:S(2)}, u32[]{:S(2)}) collective-permute-start(bf16[1250,256]{1,0:T(8,128)(2,1)S(1)} %get-tuple-element.34.refs_10_), channel_id=1, source_target_pairs={{0,68},{1,69},{2,70},{3,71},{4,64},{5,65},{6,66},{7,67},{8,76},{9,... | collective-permute-start | bytes 1920008 | tf_op jit(solution)/shard_map/ppermute | solution.py:33
  27.1 2.7 %collective-permute-start.12 = (bf16[256,1280]{1,0:T(8,128)(2,1)S(1)}, bf16[256,1280]{1,0:T(8,128)(2,1)S(1)}, u32[]{:S(2)}, u32[]{:S(2)}) collective-permute-start(bf16[256,1280]{1,0:T(8,128)(2,1)S(1)} %stack.31.refs_5_), channel_id=1, source_target_pairs={{0,24},{1,25},{2,26},{3,27},{4,28},{5,29},{6,30},{7,31},{8,16},{9,... | collective-permute-start | bytes 1966088 | tf_op jit(solution)/shard_map/ppermute | solution.py:33
  29.8 3.0 %collective-permute-start.8 = (bf16[256,1280]{1,0:T(8,128)(2,1)S(1)}, bf16[256,1280]{1,0:T(8,128)(2,1)S(1)}, u32[]{:S(2)}, u32[]{:S(2)}) collective-permute-start(bf16[256,1280]{1,0:T(8,128)(2,1)S(1)} %stack.30.refs_0_), channel_id=1, source_target_pairs={{0,3},{1,2},{2,1},{3,0},{4,7},{5,6},{6,5},{7,4},{8,11},{9,10},{10,... | collective-permute-start | bytes 1966088 | tf_op jit(solution)/shard_map/ppermute | solution.py:33
  33.9 3.5 %collective-permute-done.24.source.refs_12_ = bf16[1250,256]{1,0:T(8,128)(2,1)S(1)} collective-permute-done((bf16[1250,256]{1,0:T(8,128)(2,1)S(1)}, bf16[1250,256]{1,0:T(8,128)(2,1)S(1)}, u32[]{:S(2)}, u32[]{:S(2)}) %collective-permute-start.24) | collective-permute-done | bytes 640032 | tf_op jit(solution)/shard_map/ppermute | solution.py:33
  37.4 2.5 %collective-permute-start.16 = (bf16[1250,256]{1,0:T(8,128)(2,1)S(1)}, bf16[1250,256]{1,0:T(8,128)(2,1)S(1)}, u32[]{:S(2)}, u32[]{:S(2)}) collective-permute-start(bf16[1250,256]{1,0:T(8,128)(2,1)S(1)} %get-tuple-element.29.refs_10_), channel_id=1, source_target_pairs={{0,68},{1,69},{2,70},{3,71},{4,64},{5,65},{6,66},{7,67},{8,76},{9,... | collective-permute-start | bytes 1920008 | tf_op jit(solution)/shard_map/ppermute | solution.py:33
  40.3 4.3 %collective-permute-done.8.source.refs_2_ = bf16[256,1280]{1,0:T(8,128)(2,1)S(1)} collective-permute-done((bf16[256,1280]{1,0:T(8,128)(2,1)S(1)}, bf16[256,1280]{1,0:T(8,128)(2,1)S(1)}, u32[]{:S(2)}, u32[]{:S(2)}) %collective-permute-start.8) | collective-permute-done | bytes 655392 | tf_op jit(solution)/shard_map/ppermute | solution.py:33
  45.8 1.3 collective-permute-done.15.source.refs_11_
  47.1 1.2 collective-permute-start.14
  48.3 2.0 %collective-permute-done.16.source.refs_12_ = bf16[1250,256]{1,0:T(8,128)(2,1)S(1)} collective-permute-done((bf16[1250,256]{1,0:T(8,128)(2,1)S(1)}, bf16[1250,256]{1,0:T(8,128)(2,1)S(1)}, u32[]{:S(2)}, u32[]{:S(2)}) %collective-permute-start.16) | collective-permute-done | bytes 640032 | tf_op jit(solution)/shard_map/ppermute | solution.py:33
  50.3 6.9 %collective-permute-done.25.refs_13_ = bf16[1250,128]{1,0:T(8,128)(2,1)S(1)} collective-permute-done((bf16[1250,128]{1,0:T(8,128)(2,1)S(1)}, bf16[1250,128]{1,0:T(8,128)(2,1)S(1)}, u32[]{:S(2)}, u32[]{:S(2)}) %collective-permute-start.25) | collective-permute-done | bytes 320032 | tf_op jit(solution)/shard_map/ppermute | solution.py:33
  57.2 6.7 %collective-permute-start.9 = (bf16[128,1280]{1,0:T(8,128)(2,1)S(1)}, bf16[128,1280]{1,0:T(8,128)(2,1)S(1)}, u32[]{:S(2)}, u32[]{:S(2)}) collective-permute-start(bf16[128,1280]{1,0:T(8,128)(2,1)S(1)} %cut.9), channel_id=1, source_target_pairs={{0,3},{1,2},{2,1},{3,0},{4,7},{5,6},{6,5},{7,4},{8,11},{9,10},{10,... | collective-permute-start | bytes 983048 | tf_op jit(solution)/shard_map/ppermute | solution.py:33
  64.1 2.4 %collective-permute-start.17 = (bf16[1250,128]{1,0:T(8,128)(2,1)S(1)}, bf16[1250,128]{1,0:T(8,128)(2,1)S(1)}, u32[]{:S(2)}, u32[]{:S(2)}) collective-permute-start(bf16[1250,128]{1,0:T(8,128)(2,1)S(1)} %cut.14), channel_id=1, source_target_pairs={{0,68},{1,69},{2,70},{3,71},{4,64},{5,65},{6,66},{7,67},{8,76},{9,... | collective-permute-start | bytes 960008 | tf_op jit(solution)/shard_map/ppermute | solution.py:33
  66.5 1.9 %collective-permute-done.9.refs_3_ = bf16[128,1280]{1,0:T(8,128)(2,1)S(1)} collective-permute-done((bf16[128,1280]{1,0:T(8,128)(2,1)S(1)}, bf16[128,1280]{1,0:T(8,128)(2,1)S(1)}, u32[]{:S(2)}, u32[]{:S(2)}) %collective-permute-start.9) | collective-permute-done | bytes 327712 | tf_op jit(solution)/shard_map/ppermute | solution.py:33
  68.4 3.6 %tile.3 = (f32[2,1024,128]{2,1,0:T(8,128)S(1)}, f32[2,1024,128]{2,1,0:T(8,128)S(1)}) custom-call(s32[5]{0:T(128)S(1)} %stack.28.at, bf16[256,1280]{1,0:T(8,128)(2,1)S(1)} %stack.30.refs_0_, bf16[256,1280]{1,0:T(8,128)(2,1)S(1)} %collective-permute-done.7.source.refs_1_, bf16[256,1280]{1,0:T(8,128)(2,1)S(1)} %collective-permute-done.8.source.refs_2_, ...), custom_call_target="tpu_custom_call" | custom-call | flops 2621440000 | bytes 10485760 | tf_op jit(solution)/shard_map/tile/pallas_call | solution.py:43
  72.0 5.1 %collective-permute-start.27 = (f32[2,1024,128]{2,1,0:T(8,128)S(1)}, f32[2,1024,128]{2,1,0:T(8,128)S(1)}, u32[]{:S(2)}, u32[]{:S(2)}) collective-permute-start(f32[2,1024,128]{2,1,0:T(8,128)S(1)} %get-tuple-element.36), channel_id=1, source_target_pairs={{0,32},{1,33},{2,34},{3,35},{4,36},{5,37},{6,38},{7,39},{8,40},{9,... | collective-permute-start | bytes 3145736 | tf_op jit(solution)/shard_map/ppermute | solution.py:33
  77.2 3.6 %tile.2 = (f32[2,1024,128]{2,1,0:T(8,128)S(1)}, f32[2,1024,128]{2,1,0:T(8,128)S(1)}) custom-call(s32[5]{0:T(128)S(1)} %stack.28.at, bf16[256,1280]{1,0:T(8,128)(2,1)S(1)} %stack.30.refs_0_, bf16[256,1280]{1,0:T(8,128)(2,1)S(1)} %collective-permute-done.7.source.refs_1_, bf16[256,1280]{1,0:T(8,128)(2,1)S(1)} %collective-permute-done.8.source.refs_2_, ...), custom_call_target="tpu_custom_call" | custom-call | flops 2621440000 | bytes 10485760 | tf_op jit(solution)/shard_map/tile/pallas_call | solution.py:43
  81.7 2.1 %turn.3 = (bf16[64,2048]{1,0:T(8,128)(2,1)S(1)}, bf16[64,2048]{1,0:T(8,128)(2,1)S(1)}) custom-call(f32[2,1024,128]{2,1,0:T(8,128)S(1)} %get-tuple-element.35.keep, f32[2,1024,128]{2,1,0:T(8,128)S(1)} %collective-permute-done.27.got), custom_call_target="tpu_custom_call" | custom-call | bytes 3145728 | tf_op jit(solution)/shard_map/turn/pallas_call | solution.py:43
  84.3 2.2 %collective-permute-start.29 = (bf16[64,2048]{1,0:T(8,128)(2,1)S(1)}, bf16[64,2048]{1,0:T(8,128)(2,1)S(1)}, u32[]{:S(2)}, u32[]{:S(2)}) collective-permute-start(bf16[64,2048]{1,0:T(8,128)(2,1)S(1)} %get-tuple-element.37.refs_0_), channel_id=1, source_target_pairs={{0,64},{1,65},{2,66},{3,67},{4,68},{5,69},{6,70},{7,71},{8,72},{9,... | collective-permute-start | bytes 786440 | tf_op jit(solution)/shard_map/ppermute | solution.py:33
  87.7 2.1 %turn.2 = (bf16[64,2048]{1,0:T(8,128)(2,1)S(1)}, bf16[64,2048]{1,0:T(8,128)(2,1)S(1)}) custom-call(f32[2,1024,128]{2,1,0:T(8,128)S(1)} %get-tuple-element.30.keep, f32[2,1024,128]{2,1,0:T(8,128)S(1)} %collective-permute-done.19.got), custom_call_target="tpu_custom_call" | custom-call | bytes 3145728 | tf_op jit(solution)/shard_map/turn/pallas_call | solution.py:43
  89.8 2.0 %collective-permute-done.28.refs_1_ = bf16[64,2048]{1,0:T(8,128)(2,1)S(1)} collective-permute-done((bf16[64,2048]{1,0:T(8,128)(2,1)S(1)}, bf16[64,2048]{1,0:T(8,128)(2,1)S(1)}, u32[]{:S(2)}, u32[]{:S(2)}) %collective-permute-start.28) | collective-permute-done | bytes 262176 | tf_op jit(solution)/shard_map/ppermute | solution.py:33
  91.8 6.3 %collective-permute-done.29.refs_2_ = bf16[64,2048]{1,0:T(8,128)(2,1)S(1)} collective-permute-done((bf16[64,2048]{1,0:T(8,128)(2,1)S(1)}, bf16[64,2048]{1,0:T(8,128)(2,1)S(1)}, u32[]{:S(2)}, u32[]{:S(2)}) %collective-permute-start.29) | collective-permute-done | bytes 262176 | tf_op jit(solution)/shard_map/ppermute | solution.py:33
  98.1 2.0 %collective-permute-done.30.refs_3_ = bf16[64,2048]{1,0:T(8,128)(2,1)S(1)} collective-permute-done((bf16[64,2048]{1,0:T(8,128)(2,1)S(1)}, bf16[64,2048]{1,0:T(8,128)(2,1)S(1)}, u32[]{:S(2)}, u32[]{:S(2)}) %collective-permute-start.30) | collective-permute-done | bytes 262176 | tf_op jit(solution)/shard_map/ppermute | solution.py:33
  100.2 2.0 %collective-permute-start.31 = (bf16[256,2048]{1,0:T(8,128)(2,1)S(1)}, bf16[256,2048]{1,0:T(8,128)(2,1)S(1)}, u32[]{:S(2)}, u32[]{:S(2)}) collective-permute-start(bf16[256,2048]{1,0:T(8,128)(2,1)S(1)} %stack.32.mine), channel_id=1, source_target_pairs={{0,32},{1,33},{2,34},{3,35},{4,36},{5,37},{6,38},{7,39},{8,40},{9,... | collective-permute-start | bytes 3145736 | tf_op jit(solution)/shard_map/ppermute | solution.py:33
  102.2 1.8 %collective-permute-start.20 = (bf16[64,2048]{1,0:T(8,128)(2,1)S(1)}, bf16[64,2048]{1,0:T(8,128)(2,1)S(1)}, u32[]{:S(2)}, u32[]{:S(2)}) collective-permute-start(bf16[64,2048]{1,0:T(8,128)(2,1)S(1)} %get-tuple-element.33), channel_id=1, source_target_pairs={{0,4},{1,5},{2,6},{3,7},{4,0},{5,1},{6,2},{7,3},{8,12},{9,13},{10,... | collective-permute-start | bytes 786440 | tf_op jit(solution)/shard_map/ppermute | solution.py:33
  104.0 1.5 %collective-permute-start.22 = (bf16[64,2048]{1,0:T(8,128)(2,1)S(1)}, bf16[64,2048]{1,0:T(8,128)(2,1)S(1)}, u32[]{:S(2)}, u32[]{:S(2)}) collective-permute-start(bf16[64,2048]{1,0:T(8,128)(2,1)S(1)} %get-tuple-element.33), channel_id=1, source_target_pairs={{0,68},{1,69},{2,70},{3,71},{4,64},{5,65},{6,66},{7,67},{8,76},{9,... | collective-permute-start | bytes 786440 | tf_op jit(solution)/shard_map/ppermute | solution.py:33
  105.5 2.9 %ladder.2 = (f32[256,512]{1,0:T(8,128)S(1)}, bf16[256,512]{1,0:T(8,128)(2,1)S(1)}, bf16[256,512]{1,0:T(8,128)(2,1)S(1)}, bf16[256,512]{1,0:T(8,128)(2,1)S(1)}) custom-call(s32[5]{0:T(128)S(1)} %stack.28.at, bf16[1024,2048]{1,0:T(8,128)(2,1)S(1)} %bitcast.10, bf16[256,2048]{1,0:T(8,128)(2,1)S(1)} %stack.32.mine, ...), custom_call_target="tpu_custom_call" | custom-call | flops 2147483648 | bytes 8388608 | tf_op jit(solution)/shard_map/ladder/pallas_call | solution.py:43
  108.5 3.0 %collective-permute-start.33 = (bf16[256,512]{1,0:T(8,128)(2,1)S(1)}, bf16[256,512]{1,0:T(8,128)(2,1)S(1)}, u32[]{:S(2)}, u32[]{:S(2)}) collective-permute-start(bf16[256,512]{1,0:T(8,128)(2,1)S(1)} %get-tuple-element.40), channel_id=1, source_target_pairs={{0,3},{1,2},{2,1},{3,0},{4,7},{5,6},{6,5},{7,4},{8,11},{9,10},{10,... | collective-permute-start | bytes 786440 | tf_op jit(solution)/shard_map/ppermute | solution.py:33
  111.5 4.5 %collective-permute-done.20.refs_1_ = bf16[64,2048]{1,0:T(8,128)(2,1)S(1)} collective-permute-done((bf16[64,2048]{1,0:T(8,128)(2,1)S(1)}, bf16[64,2048]{1,0:T(8,128)(2,1)S(1)}, u32[]{:S(2)}, u32[]{:S(2)}) %collective-permute-start.20) | collective-permute-done | bytes 262176 | tf_op jit(solution)/shard_map/ppermute | solution.py:33
  116.1 1.5 %collective-permute-done.22.refs_3_ = bf16[64,2048]{1,0:T(8,128)(2,1)S(1)} collective-permute-done((bf16[64,2048]{1,0:T(8,128)(2,1)S(1)}, bf16[64,2048]{1,0:T(8,128)(2,1)S(1)}, u32[]{:S(2)}, u32[]{:S(2)}) %collective-permute-start.22) | collective-permute-done | bytes 262176 | tf_op jit(solution)/shard_map/ppermute | solution.py:33
  117.7 1.3 collective-permute-start.34
  119.0 2.6 %collective-permute-start.38 = (bf16[256,512]{1,0:T(8,128)(2,1)S(1)}, bf16[256,512]{1,0:T(8,128)(2,1)S(1)}, u32[]{:S(2)}, u32[]{:S(2)}) collective-permute-start(bf16[256,512]{1,0:T(8,128)(2,1)S(1)} %get-tuple-element.48), channel_id=1, source_target_pairs={{0,2},{1,3},{2,0},{3,1},{4,6},{5,7},{6,4},{7,5},{8,10},{9,11},{10,... | collective-permute-start | bytes 786440 | tf_op jit(solution)/shard_map/ppermute | solution.py:33
  121.6 3.4 %ladder.3 = (f32[256,512]{1,0:T(8,128)S(1)}, bf16[256,512]{1,0:T(8,128)(2,1)}, bf16[256,512]{1,0:T(8,128)(2,1)}, bf16[256,512]{1,0:T(8,128)(2,1)S(1)}) custom-call(s32[5]{0:T(128)S(1)} %stack.28.at, bf16[1024,2048]{1,0:T(8,128)(2,1)S(1)} %bitcast.11, bf16[256,2048]{1,0:T(8,128)(2,1)S(1)} %stack.33.mine, bf16[256,2048]{1,0:T(8,128)(2,1)S(1)} %collective-permute-done.34.peer), custom_call_target="tpu_custom_call" | custom-call | flops 2147483648 | bytes 8388608 | tf_op jit(solution)/shard_map/ladder/pallas_call | solution.py:43
  125.7 2.9 %collective-permute-start.36 = (bf16[256,512]{1,0:T(8,128)(2,1)}, bf16[256,512]{1,0:T(8,128)(2,1)S(1)}, u32[]{:S(2)}, u32[]{:S(2)}) collective-permute-start(bf16[256,512]{1,0:T(8,128)(2,1)} %get-tuple-element.43), channel_id=1, source_target_pairs={{0,2},{1,3},{2,0},{3,1},{4,6},{5,7},{6,4},{7,5},{8,10},{9,11},{10,... | collective-permute-start | bytes 786440 | tf_op jit(solution)/shard_map/ppermute | solution.py:33
  129.0 1.6 %prepare.1 = (bf16[512,512]{1,0:T(8,128)(2,1)S(1)}, f32[256,1024]{1,0:T(8,128)S(1)}) custom-call(s32[5]{0:T(128)S(1)} %stack.28.at, s32[2]{0:T(128)S(1)} %copy-done.2, f32[1400]{0:T(1024)S(1)} %copy-done.1, s32[256,2]{1,0:T(8,128)S(1)} %copy.9.pairs, f32[1,120]{1,0:T(1,128)S(1)} %bitcast.9), custom_call_target="tpu_custom_call" | custom-call | bytes 1048576 | tf_op jit(solution)/shard_map/prepare/pallas_call | solution.py:43
  130.6 1.4 finish.2.refs_0_
  132.0 2.0 %collective-permute-done.35.r1 = bf16[256,512]{1,0:T(8,128)(2,1)S(1)} collective-permute-done((bf16[256,512]{1,0:T(8,128)(2,1)}, bf16[256,512]{1,0:T(8,128)(2,1)S(1)}, u32[]{:S(2)}, u32[]{:S(2)}) %collective-permute-start.35) | collective-permute-done | bytes 262176 | tf_op jit(solution)/shard_map/ppermute | solution.py:33
  134.0 6.5 %collective-permute-done.36.r2 = bf16[256,512]{1,0:T(8,128)(2,1)S(1)} collective-permute-done((bf16[256,512]{1,0:T(8,128)(2,1)}, bf16[256,512]{1,0:T(8,128)(2,1)S(1)}, u32[]{:S(2)}, u32[]{:S(2)}) %collective-permute-start.36) | collective-permute-done | bytes 262176 | tf_op jit(solution)/shard_map/ppermute | solution.py:33
  140.5 1.8 %collective-permute-done.37.r3 = bf16[256,512]{1,0:T(8,128)(2,1)S(1)} collective-permute-done((bf16[256,512]{1,0:T(8,128)(2,1)S(1)}, bf16[256,512]{1,0:T(8,128)(2,1)S(1)}, u32[]{:S(2)}, u32[]{:S(2)}) %collective-permute-start.37) | collective-permute-done | bytes 262176 | tf_op jit(solution)/shard_map/ppermute | solution.py:33
  142.3 1.4 finish.3
  (69 shorter events, 11.1 us)
Async XLA Ops:
  1.8 7.1 %collective-permute-start = (bf16[64,1280]{1,0:T(8,128)(2,1)S(1)}, bf16[64,1280]{1,0:T(8,128)(2,1)S(1)}, u32[]{:S(2)}, u32[]{:S(2)}) collective-permute-start(bf16[64,1280]{1,0:T(8,128)(2,1)S(1)} %get-tuple-element.28), channel_id=1, source_target_pairs={{0,64},{1,65},{2,66},{3,67},{4,68},{5,69},{6,70},{7,71},{8,72},{9,... | collective-permute-start | bytes 491528 | tf_op jit(solution)/shard_map/ppermute | solution.py:33
  8.9 9.3 %collective-permute-start.1 = (bf16[64,1280]{1,0:T(8,128)(2,1)S(1)}, bf16[64,1280]{1,0:T(8,128)(2,1)S(1)}, u32[]{:S(2)}, u32[]{:S(2)}) collective-permute-start(bf16[64,1280]{1,0:T(8,128)(2,1)S(1)} %stack.29.refs_0_), channel_id=1, source_target_pairs={{0,8},{1,9},{2,10},{3,11},{4,12},{5,13},{6,14},{7,15},{8,0},{9,1},... | collective-permute-start | bytes 491528 | tf_op jit(solution)/shard_map/ppermute | solution.py:33
  10.6 9.0 %collective-permute-start.2 = (bf16[64,1280]{1,0:T(8,128)(2,1)S(1)}, bf16[64,1280]{1,0:T(8,128)(2,1)S(1)}, u32[]{:S(2)}, u32[]{:S(2)}) collective-permute-start(bf16[64,1280]{1,0:T(8,128)(2,1)S(1)} %stack.29.refs_0_), channel_id=1, source_target_pairs={{0,16},{1,17},{2,18},{3,19},{4,20},{5,21},{6,22},{7,23},{8,24},{9,... | collective-permute-start | bytes 491528 | tf_op jit(solution)/shard_map/ppermute | solution.py:33
  13.3 8.8 %collective-permute-start.3 = (bf16[64,1280]{1,0:T(8,128)(2,1)S(1)}, bf16[64,1280]{1,0:T(8,128)(2,1)S(1)}, u32[]{:S(2)}, u32[]{:S(2)}) collective-permute-start(bf16[64,1280]{1,0:T(8,128)(2,1)S(1)} %stack.29.refs_0_), channel_id=1, source_target_pairs={{0,24},{1,25},{2,26},{3,27},{4,28},{5,29},{6,30},{7,31},{8,16},{9,... | collective-permute-start | bytes 491528 | tf_op jit(solution)/shard_map/ppermute | solution.py:33
  13.3 8.8 %collective-permute-start.4 = (bf16[64,1280]{1,0:T(8,128)(2,1)S(1)}, bf16[64,1280]{1,0:T(8,128)(2,1)S(1)}, u32[]{:S(2)}, u32[]{:S(2)}) collective-permute-start(bf16[64,1280]{1,0:T(8,128)(2,1)S(1)} %collective-permute-done.refs_1_.refs_0_), channel_id=1, source_target_pairs={{0,1},{1,0},{2,3},{3,2},{4,5},{5,4},{6,7},{7,6},{8,9},{9,8},{10,11... | collective-permute-start | bytes 491528 | tf_op jit(solution)/shard_map/ppermute | solution.py:33
  14.9 8.4 %collective-permute-start.5 = (bf16[64,1280]{1,0:T(8,128)(2,1)S(1)}, bf16[64,1280]{1,0:T(8,128)(2,1)S(1)}, u32[]{:S(2)}, u32[]{:S(2)}) collective-permute-start(bf16[64,1280]{1,0:T(8,128)(2,1)S(1)} %collective-permute-done.refs_1_.refs_0_), channel_id=1, source_target_pairs={{0,2},{1,3},{2,0},{3,1},{4,6},{5,7},{6,4},{7,5},{8,10},{9,11},{10,... | collective-permute-start | bytes 491528 | tf_op jit(solution)/shard_map/ppermute | solution.py:33
  18.2 6.2 %collective-permute-start.6 = (bf16[64,1280]{1,0:T(8,128)(2,1)S(1)}, bf16[64,1280]{1,0:T(8,128)(2,1)S(1)}, u32[]{:S(2)}, u32[]{:S(2)}) collective-permute-start(bf16[64,1280]{1,0:T(8,128)(2,1)S(1)} %collective-permute-done.refs_1_.refs_0_), channel_id=1, source_target_pairs={{0,3},{1,2},{2,1},{3,0},{4,7},{5,6},{6,5},{7,4},{8,11},{9,10},{10,... | collective-permute-start | bytes 491528 | tf_op jit(solution)/shard_map/ppermute | solution.py:33
  18.2 1.3 copy-start
  19.6 13.3 %collective-permute-start.23 = (bf16[1250,256]{1,0:T(8,128)(2,1)S(1)}, bf16[1250,256]{1,0:T(8,128)(2,1)S(1)}, u32[]{:S(2)}, u32[]{:S(2)}) collective-permute-start(bf16[1250,256]{1,0:T(8,128)(2,1)S(1)} %get-tuple-element.34.refs_10_), channel_id=1, source_target_pairs={{0,4},{1,5},{2,6},{3,7},{4,0},{5,1},{6,2},{7,3},{8,12},{9,13},{10,... | collective-permute-start | bytes 1920008 | tf_op jit(solution)/shard_map/ppermute | solution.py:33
  24.5 12.9 %collective-permute-start.11 = (bf16[256,1280]{1,0:T(8,128)(2,1)S(1)}, bf16[256,1280]{1,0:T(8,128)(2,1)S(1)}, u32[]{:S(2)}, u32[]{:S(2)}) collective-permute-start(bf16[256,1280]{1,0:T(8,128)(2,1)S(1)} %stack.31.refs_5_), channel_id=1, source_target_pairs={{0,8},{1,9},{2,10},{3,11},{4,12},{5,13},{6,14},{7,15},{8,0},{9,1},... | collective-permute-start | bytes 1966088 | tf_op jit(solution)/shard_map/ppermute | solution.py:33
  24.6 12.8 %collective-permute-start.24 = (bf16[1250,256]{1,0:T(8,128)(2,1)S(1)}, bf16[1250,256]{1,0:T(8,128)(2,1)S(1)}, u32[]{:S(2)}, u32[]{:S(2)}) collective-permute-start(bf16[1250,256]{1,0:T(8,128)(2,1)S(1)} %get-tuple-element.34.refs_10_), channel_id=1, source_target_pairs={{0,68},{1,69},{2,70},{3,71},{4,64},{5,65},{6,66},{7,67},{8,76},{9,... | collective-permute-start | bytes 1920008 | tf_op jit(solution)/shard_map/ppermute | solution.py:33
  27.1 12.8 %collective-permute-start.12 = (bf16[256,1280]{1,0:T(8,128)(2,1)S(1)}, bf16[256,1280]{1,0:T(8,128)(2,1)S(1)}, u32[]{:S(2)}, u32[]{:S(2)}) collective-permute-start(bf16[256,1280]{1,0:T(8,128)(2,1)S(1)} %stack.31.refs_5_), channel_id=1, source_target_pairs={{0,24},{1,25},{2,26},{3,27},{4,28},{5,29},{6,30},{7,31},{8,16},{9,... | collective-permute-start | bytes 1966088 | tf_op jit(solution)/shard_map/ppermute | solution.py:33
  29.8 14.7 %collective-permute-start.8 = (bf16[256,1280]{1,0:T(8,128)(2,1)S(1)}, bf16[256,1280]{1,0:T(8,128)(2,1)S(1)}, u32[]{:S(2)}, u32[]{:S(2)}) collective-permute-start(bf16[256,1280]{1,0:T(8,128)(2,1)S(1)} %stack.30.refs_0_), channel_id=1, source_target_pairs={{0,3},{1,2},{2,1},{3,0},{4,7},{5,6},{6,5},{7,4},{8,11},{9,10},{10,... | collective-permute-start | bytes 1966088 | tf_op jit(solution)/shard_map/ppermute | solution.py:33
  32.9 12.5 %collective-permute-start.7 = (bf16[256,1280]{1,0:T(8,128)(2,1)S(1)}, bf16[256,1280]{1,0:T(8,128)(2,1)S(1)}, u32[]{:S(2)}, u32[]{:S(2)}) collective-permute-start(bf16[256,1280]{1,0:T(8,128)(2,1)S(1)} %stack.30.refs_0_), channel_id=1, source_target_pairs={{0,1},{1,0},{2,3},{3,2},{4,5},{5,4},{6,7},{7,6},{8,9},{9,8},{10,11... | collective-permute-start | bytes 1966088 | tf_op jit(solution)/shard_map/ppermute | solution.py:33
  37.4 9.7 %collective-permute-start.15 = (bf16[1250,256]{1,0:T(8,128)(2,1)S(1)}, bf16[1250,256]{1,0:T(8,128)(2,1)S(1)}, u32[]{:S(2)}, u32[]{:S(2)}) collective-permute-start(bf16[1250,256]{1,0:T(8,128)(2,1)S(1)} %get-tuple-element.29.refs_10_), channel_id=1, source_target_pairs={{0,4},{1,5},{2,6},{3,7},{4,0},{5,1},{6,2},{7,3},{8,12},{9,13},{10,... | collective-permute-start | bytes 1920008 | tf_op jit(solution)/shard_map/ppermute | solution.py:33
  37.4 12.9 %collective-permute-start.16 = (bf16[1250,256]{1,0:T(8,128)(2,1)S(1)}, bf16[1250,256]{1,0:T(8,128)(2,1)S(1)}, u32[]{:S(2)}, u32[]{:S(2)}) collective-permute-start(bf16[1250,256]{1,0:T(8,128)(2,1)S(1)} %get-tuple-element.29.refs_10_), channel_id=1, source_target_pairs={{0,68},{1,69},{2,70},{3,71},{4,64},{5,65},{6,66},{7,67},{8,76},{9,... | collective-permute-start | bytes 1920008 | tf_op jit(solution)/shard_map/ppermute | solution.py:33
  40.0 17.3 %collective-permute-start.25 = (bf16[1250,128]{1,0:T(8,128)(2,1)S(1)}, bf16[1250,128]{1,0:T(8,128)(2,1)S(1)}, u32[]{:S(2)}, u32[]{:S(2)}) collective-permute-start(bf16[1250,128]{1,0:T(8,128)(2,1)S(1)} %cut.16), channel_id=1, source_target_pairs={{0,68},{1,69},{2,70},{3,71},{4,64},{5,65},{6,66},{7,67},{8,76},{9,... | collective-permute-start | bytes 960008 | tf_op jit(solution)/shard_map/ppermute | solution.py:33
  44.6 21.9 %collective-permute-start.13 = (bf16[128,1280]{1,0:T(8,128)(2,1)S(1)}, bf16[128,1280]{1,0:T(8,128)(2,1)S(1)}, u32[]{:S(2)}, u32[]{:S(2)}) collective-permute-start(bf16[128,1280]{1,0:T(8,128)(2,1)S(1)} %cut.11), channel_id=1, source_target_pairs={{0,24},{1,25},{2,26},{3,27},{4,28},{5,29},{6,30},{7,31},{8,16},{9,... | collective-permute-start | bytes 983048 | tf_op jit(solution)/shard_map/ppermute | solution.py:33
  45.4 18.6 %collective-permute-start.26 = (bf16[1250,128]{1,0:T(8,128)(2,1)S(1)}, bf16[1250,128]{1,0:T(8,128)(2,1)S(1)}, u32[]{:S(2)}, u32[]{:S(2)}) collective-permute-start(bf16[1250,128]{1,0:T(8,128)(2,1)S(1)} %cut.17), channel_id=1, source_target_pairs={{0,4},{1,5},{2,6},{3,7},{4,0},{5,1},{6,2},{7,3},{8,12},{9,13},{10,... | collective-permute-start | bytes 960008 | tf_op jit(solution)/shard_map/ppermute | solution.py:33
  47.1 19.4 %collective-permute-start.14 = (bf16[128,1280]{1,0:T(8,128)(2,1)S(1)}, bf16[128,1280]{1,0:T(8,128)(2,1)S(1)}, u32[]{:S(2)}, u32[]{:S(2)}) collective-permute-start(bf16[128,1280]{1,0:T(8,128)(2,1)S(1)} %cut.12), channel_id=1, source_target_pairs={{0,8},{1,9},{2,10},{3,11},{4,12},{5,13},{6,14},{7,15},{8,0},{9,1},... | collective-permute-start | bytes 983048 | tf_op jit(solution)/shard_map/ppermute | solution.py:33
  50.3 16.2 %collective-permute-start.10 = (bf16[128,1280]{1,0:T(8,128)(2,1)S(1)}, bf16[128,1280]{1,0:T(8,128)(2,1)S(1)}, u32[]{:S(2)}, u32[]{:S(2)}) collective-permute-start(bf16[128,1280]{1,0:T(8,128)(2,1)S(1)} %cut.10), channel_id=1, source_target_pairs={{0,1},{1,0},{2,3},{3,2},{4,5},{5,4},{6,7},{7,6},{8,9},{9,8},{10,11... | collective-permute-start | bytes 983048 | tf_op jit(solution)/shard_map/ppermute | solution.py:33
  57.2 11.2 %collective-permute-start.9 = (bf16[128,1280]{1,0:T(8,128)(2,1)S(1)}, bf16[128,1280]{1,0:T(8,128)(2,1)S(1)}, u32[]{:S(2)}, u32[]{:S(2)}) collective-permute-start(bf16[128,1280]{1,0:T(8,128)(2,1)S(1)} %cut.9), channel_id=1, source_target_pairs={{0,3},{1,2},{2,1},{3,0},{4,7},{5,6},{6,5},{7,4},{8,11},{9,10},{10,... | collective-permute-start | bytes 983048 | tf_op jit(solution)/shard_map/ppermute | solution.py:33
  64.1 13.1 %collective-permute-start.17 = (bf16[1250,128]{1,0:T(8,128)(2,1)S(1)}, bf16[1250,128]{1,0:T(8,128)(2,1)S(1)}, u32[]{:S(2)}, u32[]{:S(2)}) collective-permute-start(bf16[1250,128]{1,0:T(8,128)(2,1)S(1)} %cut.14), channel_id=1, source_target_pairs={{0,68},{1,69},{2,70},{3,71},{4,64},{5,65},{6,66},{7,67},{8,76},{9,... | collective-permute-start | bytes 960008 | tf_op jit(solution)/shard_map/ppermute | solution.py:33
  66.5 10.7 %collective-permute-start.18 = (bf16[1250,128]{1,0:T(8,128)(2,1)S(1)}, bf16[1250,128]{1,0:T(8,128)(2,1)S(1)}, u32[]{:S(2)}, u32[]{:S(2)}) collective-permute-start(bf16[1250,128]{1,0:T(8,128)(2,1)S(1)} %cut.15), channel_id=1, source_target_pairs={{0,4},{1,5},{2,6},{3,7},{4,0},{5,1},{6,2},{7,3},{8,12},{9,13},{10,... | collective-permute-start | bytes 960008 | tf_op jit(solution)/shard_map/ppermute | solution.py:33
  72.0 9.7 %collective-permute-start.27 = (f32[2,1024,128]{2,1,0:T(8,128)S(1)}, f32[2,1024,128]{2,1,0:T(8,128)S(1)}, u32[]{:S(2)}, u32[]{:S(2)}) collective-permute-start(f32[2,1024,128]{2,1,0:T(8,128)S(1)} %get-tuple-element.36), channel_id=1, source_target_pairs={{0,32},{1,33},{2,34},{3,35},{4,36},{5,37},{6,38},{7,39},{8,40},{9,... | collective-permute-start | bytes 3145736 | tf_op jit(solution)/shard_map/ppermute | solution.py:33
  80.8 24.7 %copy-start.4 = (bf16[1024,1,2048]{2,0,1:T(8,128)(2,1)S(1)}, bf16[1024,1,2048]{2,0,1:T(8,128)(2,1)}, u32[]{:S(2)}) copy-start(bf16[1024,1,2048]{2,0,1:T(8,128)(2,1)} %param.9) | copy-start | bytes 12582916
  80.8 6.9 %collective-permute-start.19 = (f32[2,1024,128]{2,1,0:T(8,128)S(1)}, f32[2,1024,128]{2,1,0:T(8,128)S(1)}, u32[]{:S(2)}, u32[]{:S(2)}) collective-permute-start(f32[2,1024,128]{2,1,0:T(8,128)S(1)} %get-tuple-element.31), channel_id=1, source_target_pairs={{0,32},{1,33},{2,34},{3,35},{4,36},{5,37},{6,38},{7,39},{8,40},{9,... | collective-permute-start | bytes 3145736 | tf_op jit(solution)/shard_map/ppermute | solution.py:33
  83.8 8.0 %collective-permute-start.28 = (bf16[64,2048]{1,0:T(8,128)(2,1)S(1)}, bf16[64,2048]{1,0:T(8,128)(2,1)S(1)}, u32[]{:S(2)}, u32[]{:S(2)}) collective-permute-start(bf16[64,2048]{1,0:T(8,128)(2,1)S(1)} %get-tuple-element.38), channel_id=1, source_target_pairs={{0,4},{1,5},{2,6},{3,7},{4,0},{5,1},{6,2},{7,3},{8,12},{9,13},{10,... | collective-permute-start | bytes 786440 | tf_op jit(solution)/shard_map/ppermute | solution.py:33
  84.3 13.8 %collective-permute-start.29 = (bf16[64,2048]{1,0:T(8,128)(2,1)S(1)}, bf16[64,2048]{1,0:T(8,128)(2,1)S(1)}, u32[]{:S(2)}, u32[]{:S(2)}) collective-permute-start(bf16[64,2048]{1,0:T(8,128)(2,1)S(1)} %get-tuple-element.37.refs_0_), channel_id=1, source_target_pairs={{0,64},{1,65},{2,66},{3,67},{4,68},{5,69},{6,70},{7,71},{8,72},{9,... | collective-permute-start | bytes 786440 | tf_op jit(solution)/shard_map/ppermute | solution.py:33
  86.5 13.6 %collective-permute-start.30 = (bf16[64,2048]{1,0:T(8,128)(2,1)S(1)}, bf16[64,2048]{1,0:T(8,128)(2,1)S(1)}, u32[]{:S(2)}, u32[]{:S(2)}) collective-permute-start(bf16[64,2048]{1,0:T(8,128)(2,1)S(1)} %get-tuple-element.38), channel_id=1, source_target_pairs={{0,68},{1,69},{2,70},{3,71},{4,64},{5,65},{6,66},{7,67},{8,76},{9,... | collective-permute-start | bytes 786440 | tf_op jit(solution)/shard_map/ppermute | solution.py:33
  100.2 5.3 %collective-permute-start.31 = (bf16[256,2048]{1,0:T(8,128)(2,1)S(1)}, bf16[256,2048]{1,0:T(8,128)(2,1)S(1)}, u32[]{:S(2)}, u32[]{:S(2)}) collective-permute-start(bf16[256,2048]{1,0:T(8,128)(2,1)S(1)} %stack.32.mine), channel_id=1, source_target_pairs={{0,32},{1,33},{2,34},{3,35},{4,36},{5,37},{6,38},{7,39},{8,40},{9,... | collective-permute-start | bytes 3145736 | tf_op jit(solution)/shard_map/ppermute | solution.py:33
  102.2 13.8 %collective-permute-start.21 = (bf16[64,2048]{1,0:T(8,128)(2,1)S(1)}, bf16[64,2048]{1,0:T(8,128)(2,1)S(1)}, u32[]{:S(2)}, u32[]{:S(2)}) collective-permute-start(bf16[64,2048]{1,0:T(8,128)(2,1)S(1)} %get-tuple-element.32.refs_4_.refs_0_), channel_id=1, source_target_pairs={{0,64},{1,65},{2,66},{3,67},{4,68},{5,69},{6,70},{7,71},{8,72},{9,... | collective-permute-start | bytes 786440 | tf_op jit(solution)/shard_map/ppermute | solution.py:33
  102.2 13.8 %collective-permute-start.20 = (bf16[64,2048]{1,0:T(8,128)(2,1)S(1)}, bf16[64,2048]{1,0:T(8,128)(2,1)S(1)}, u32[]{:S(2)}, u32[]{:S(2)}) collective-permute-start(bf16[64,2048]{1,0:T(8,128)(2,1)S(1)} %get-tuple-element.33), channel_id=1, source_target_pairs={{0,4},{1,5},{2,6},{3,7},{4,0},{5,1},{6,2},{7,3},{8,12},{9,13},{10,... | collective-permute-start | bytes 786440 | tf_op jit(solution)/shard_map/ppermute | solution.py:33
  104.0 13.6 %collective-permute-start.22 = (bf16[64,2048]{1,0:T(8,128)(2,1)S(1)}, bf16[64,2048]{1,0:T(8,128)(2,1)S(1)}, u32[]{:S(2)}, u32[]{:S(2)}) collective-permute-start(bf16[64,2048]{1,0:T(8,128)(2,1)S(1)} %get-tuple-element.33), channel_id=1, source_target_pairs={{0,68},{1,69},{2,70},{3,71},{4,64},{5,65},{6,66},{7,67},{8,76},{9,... | collective-permute-start | bytes 786440 | tf_op jit(solution)/shard_map/ppermute | solution.py:33
  108.4 9.2 %collective-permute-start.32 = (bf16[256,512]{1,0:T(8,128)(2,1)S(1)}, bf16[256,512]{1,0:T(8,128)(2,1)S(1)}, u32[]{:S(2)}, u32[]{:S(2)}) collective-permute-start(bf16[256,512]{1,0:T(8,128)(2,1)S(1)} %get-tuple-element.39), channel_id=1, source_target_pairs={{0,1},{1,0},{2,3},{3,2},{4,5},{5,4},{6,7},{7,6},{8,9},{9,8},{10,11... | collective-permute-start | bytes 786440 | tf_op jit(solution)/shard_map/ppermute | solution.py:33
  108.5 9.1 %collective-permute-start.33 = (bf16[256,512]{1,0:T(8,128)(2,1)S(1)}, bf16[256,512]{1,0:T(8,128)(2,1)S(1)}, u32[]{:S(2)}, u32[]{:S(2)}) collective-permute-start(bf16[256,512]{1,0:T(8,128)(2,1)S(1)} %get-tuple-element.40), channel_id=1, source_target_pairs={{0,3},{1,2},{2,1},{3,0},{4,7},{5,6},{6,5},{7,4},{8,11},{9,10},{10,... | collective-permute-start | bytes 786440 | tf_op jit(solution)/shard_map/ppermute | solution.py:33
  117.7 11.2 %copy-start.5 = (s32[256,2]{0,1:T(2,128)S(1)}, s32[256,2]{0,1:T(2,128)}, u32[]{:S(2)}) copy-start(s32[256,2]{0,1:T(2,128)} %param.10) | copy-start | bytes 6148
  117.7 11.3 %copy-start.1 = (f32[1400]{0:T(1024)S(1)}, f32[1400]{0:T(1024)}, u32[]{:S(2)}) copy-start(f32[1400]{0:T(1024)} %virt.1) | copy-start | bytes 16804
  117.7 11.3 %copy-start.2 = (s32[2]{0:T(128)S(1)}, s32[2]{0:T(128)}, u32[]{:S(2)}) copy-start(s32[2]{0:T(128)} %offsets.1) | copy-start | bytes 28
  117.7 11.3 %copy-start.3 = (f32[120]{0:T(128)S(1)}, f32[120]{0:T(128)}, u32[]{:S(2)}) copy-start(f32[120]{0:T(128)} %param.12) | copy-start | bytes 1444
  117.7 3.8 %collective-permute-start.34 = (bf16[256,2048]{1,0:T(8,128)(2,1)S(1)}, bf16[256,2048]{1,0:T(8,128)(2,1)S(1)}, u32[]{:S(2)}, u32[]{:S(2)}) collective-permute-start(bf16[256,2048]{1,0:T(8,128)(2,1)S(1)} %stack.33.mine), channel_id=1, source_target_pairs={{0,32},{1,33},{2,34},{3,35},{4,36},{5,37},{6,38},{7,39},{8,40},{9,... | collective-permute-start | bytes 3145736 | tf_op jit(solution)/shard_map/ppermute | solution.py:33
  119.0 11.6 %collective-permute-start.38 = (bf16[256,512]{1,0:T(8,128)(2,1)S(1)}, bf16[256,512]{1,0:T(8,128)(2,1)S(1)}, u32[]{:S(2)}, u32[]{:S(2)}) collective-permute-start(bf16[256,512]{1,0:T(8,128)(2,1)S(1)} %get-tuple-element.48), channel_id=1, source_target_pairs={{0,2},{1,3},{2,0},{3,1},{4,6},{5,7},{6,4},{7,5},{8,10},{9,11},{10,... | collective-permute-start | bytes 786440 | tf_op jit(solution)/shard_map/ppermute | solution.py:33
  125.0 9.0 %collective-permute-start.35 = (bf16[256,512]{1,0:T(8,128)(2,1)}, bf16[256,512]{1,0:T(8,128)(2,1)S(1)}, u32[]{:S(2)}, u32[]{:S(2)}) collective-permute-start(bf16[256,512]{1,0:T(8,128)(2,1)} %get-tuple-element.42), channel_id=1, source_target_pairs={{0,1},{1,0},{2,3},{3,2},{4,5},{5,4},{6,7},{7,6},{8,9},{9,8},{10,11... | collective-permute-start | bytes 786440 | tf_op jit(solution)/shard_map/ppermute | solution.py:33
  125.7 14.8 %collective-permute-start.36 = (bf16[256,512]{1,0:T(8,128)(2,1)}, bf16[256,512]{1,0:T(8,128)(2,1)S(1)}, u32[]{:S(2)}, u32[]{:S(2)}) collective-permute-start(bf16[256,512]{1,0:T(8,128)(2,1)} %get-tuple-element.43), channel_id=1, source_target_pairs={{0,2},{1,3},{2,0},{3,1},{4,6},{5,7},{6,4},{7,5},{8,10},{9,11},{10,... | collective-permute-start | bytes 786440 | tf_op jit(solution)/shard_map/ppermute | solution.py:33
  128.6 13.7 %collective-permute-start.37 = (bf16[256,512]{1,0:T(8,128)(2,1)S(1)}, bf16[256,512]{1,0:T(8,128)(2,1)S(1)}, u32[]{:S(2)}, u32[]{:S(2)}) collective-permute-start(bf16[256,512]{1,0:T(8,128)(2,1)S(1)} %get-tuple-element.44), channel_id=1, source_target_pairs={{0,3},{1,2},{2,1},{3,0},{4,7},{5,6},{6,5},{7,4},{8,11},{9,10},{10,... | collective-permute-start | bytes 786440 | tf_op jit(solution)/shard_map/ppermute | solution.py:33

commit v3 on v2

--- a/solution.py
+++ b/solution.py
@@ -86,10 +86,11 @@
     return call(functools.partial(stack_kernel, n), shape, (*pieces, *after), [VMEM] * n + [HBM] * len(after), "stack")
 
 
-def tile_kernel(at, *refs):
+def tile_kernel(j, at, *refs):
     la, lb, r = refs[0:5], refs[5:10], refs[10:15]
     keep, send, acc = refs[-3:]
     first = at[CORE] == 0
+    lanes = slice(j * 128, (j + 1) * 128)
     place = ((0, 0, 4), (1, 0, 4), (3, 0, 4), (2, 0, 2), (2, 2, 2))
     for part in range(2):
         right = r[part][...]
@@ -98,7 +99,7 @@
             for i in range(count):
                 acc[part, start + i, at[Z] ^ zr] = out[i * 64:(i + 1) * 64]
     for part in range(2):
-        right = jnp.concatenate([r[3][...], r[4][...]], axis=1) if part == 0 else r[2][...]
+        right = jnp.concatenate([r[3][:, lanes], r[4][:, lanes]], axis=1) if part == 0 else r[2][...]
         for k, (yr, start, count) in enumerate(place):
             out = jnp.dot(lb[k][:, :1250], right, preferred_element_type=jnp.float32)
             for i in range(count):
@@ -109,9 +110,9 @@
                 send[part, rows, :] = jnp.where(first, total[:, 128:], total[:, :128])
 
 
-def tile(at, la, lb, r, after=()):
+def tile(j, at, la, lb, r, after=()):
     return call(
-        tile_kernel,
+        functools.partial(tile_kernel, j),
         [((2, 1024, 128), F32)] * 2,
         (at, *la, *lb, *r, *after),
         [SMEM] + [VMEM] * 15 + [HBM] * len(after),
@@ -123,16 +124,17 @@
     )
 
 
-def turn_kernel(keep, got, own, other):
+def turn_kernel(keep, got, own, other, total):
     lane = lax.broadcasted_iota(jnp.int32, (16, 128), 1)
     odd = (lane // 32) % 2 == 1
     high = lane // 64 == 1
+    total[...] = keep[...] + got[...]
     for part, out in ((0, own), (1, other)):
         for group in range(16):
             v = []
             for c in range(4):
                 rows = pl.ds(group * 4 + c, 16, stride=64)
-                v.append(keep[part, rows, :] + got[part, rows, :])
+                v.append(total[part, rows, :])
             w = [
                 jnp.where(odd, pltpu.roll(v[1], 32, 1), v[0]),
                 jnp.where(odd, v[1], pltpu.roll(v[0], 96, 1)),
@@ -150,25 +152,32 @@
 
 
 def turn(keep, got):
-    return call(turn_kernel, [((64, 2048), BF16)] * 2, (keep, got), [VMEM] * 2, "turn", size=3 * MIB)
-
-
-def ladder_kernel(at, amp, mine, peer, own, *out):
-    for s in range(4):
+    return call(turn_kernel, [((64, 2048), BF16)] * 2, (keep, got), [VMEM] * 2, "turn", scratch=[pltpu.VMEM((2, 1024, 128), F32)], size=3 * MIB)
+
+
+def ladder_kernel(at, amp, part, *refs):
+    halves, outs = refs[:-4], refs[-4:]
+    for s, out in enumerate(outs):
         rows = pl.ds(pl.multiple_of((at[Z] ^ s) * 256, 256), 256)
-        for k, part in enumerate((mine, peer)):
-            lanes = slice(k * 256, (k + 1) * 256)
-            total = dot_nt(amp[rows, :], part[...])
-            if s == 0:
-                own[:, lanes] = total
-            else:
-                out[s - 1][:, lanes] = total.astype(BF16)
-
-
-def ladder(at, amp, mine, peer):
-    shapes = [((256, 512), F32)] + [((256, 512), BF16)] * 3
-    inputs = (at, amp, mine, peer)
-    return call(ladder_kernel, shapes, inputs, [SMEM] + [VMEM] * 3, "ladder", flops=2 * 1024 * 2048 * 512, size=8 * MIB)
+        total = dot_nt(amp[rows, :], part[...]).astype(out.dtype)
+        if halves:
+            out[:, :256] = halves[s][...]
+            out[:, 256:] = total
+        else:
+            out[...] = total
+
+
+def ladder(at, amp, part, halves=()):
+    shape = (256, 512 if halves else 256)
+    return call(
+        ladder_kernel,
+        [(shape, F32)] + [(shape, BF16)] * 3,
+        (at, amp, part, *halves),
+        [SMEM] + [VMEM] * (2 + len(halves)),
+        "ladder",
+        flops=2 * 1024 * 2048 * 256,
+        size=6 * MIB,
+    )
 
 
 def finish_kernel(j, own, r1, r2, r3, order, scale, *refs):
@@ -236,16 +245,19 @@
     )
 
 
-def spread(x, axis):
+def join_kernel(lanes, *refs):
+    refs[-1][...] = jnp.concatenate([v[:, lanes] for v in refs[:-1]], axis=1)
+
+
+def join(parts, lanes):
+    shape = ((parts[0].shape[0], 128 * len(parts)), BF16)
+    return call(functools.partial(join_kernel, lanes), shape, parts, [VMEM] * len(parts), "join")
+
+
+def spread(x, axis, after):
     one, three = swap(x, **{axis: 1}), swap(x, **{axis: 3})
-    (upper,), (lower,) = cut(one, [np.s_[:128, :]]), cut(three, [np.s_[128:, :]])
+    (upper,), (lower,) = cut(one, [np.s_[:128, :]], after), cut(three, [np.s_[128:, :]], after)
     return [x, one, three, swap(upper, **{axis: 3}), swap(lower, **{axis: 1})]
-
-
-def around(x):
-    one, three = swap(x, xl=1), swap(x, xl=1, xh=1)
-    (near,), (far,) = cut(one, [np.s_[:, :128]]), cut(three, [np.s_[:, 128:]])
-    return [x, one, three, swap(near, xl=1, xh=1), swap(far, xl=1)]
 
 
 def per_device(left, right, amplitudes, pair_list, offsets, occ_energy, virt_energy):
@@ -255,26 +267,31 @@
 
     mine, theirs = split(at, jnp.pad(left, ((0, 30), (0, 0))))
     far = swap(theirs, xh=1)
-    mine = stack([mine], (far,))
+    r0 = cut(right, [np.s_[:, :256]], (theirs,))
+    mine = stack([mine], r0)
     far4 = [far] + [swap(far, z=s) for s in (1, 2, 3)]
     mine4 = [mine] + [swap(mine, y=s) for s in (1, 2, 3)]
-    la = spread(stack(mine4, tuple(far4[1:])), "z")
-    lb = spread(stack(far4, tuple(mine4[1:])), "y")
-
-    r = [around(v) for v in cut(right, [np.s_[:, :256], np.s_[:, 256:]], (far,))]
+    r0 += cut(right, [np.s_[:, 256:]], (mine4[3], far4[1]))
+    r1, r3 = [swap(v, xl=1) for v in r0], [swap(v, xl=1, xh=1) for v in r0]
+
+    la = stack(mine4, (*far4[1:], r1[0], r3[0]))
+    lb = stack(far4, (*mine4[1:], r1[0], r3[0]))
+    la, lb = spread(la, "z", (r1[1], r3[1])), spread(lb, "y", (r1[1], r3[1]))
+    r2 = swap(join(r1, np.s_[:128]), xl=1, xh=1), swap(join(r3, np.s_[128:]), xl=1)
     order, scale = prepare(at, offsets, virt_energy, pair_list, occ_energy)
 
-    turned, after = [], ()
+    parts = []
     for j in range(CHUNKS):
-        keep, send = tile(at, la, lb, r[j], after)
-        turned.append(turn(keep, swap(send, core=1)))
-    out, after = None, (turned[1][0],)
+        keep, send = tile(j, at, la, lb, (r0[j], r1[j], r3[j], *r2))
+        own, other = turn(keep, swap(send, core=1))
+        parts.append([own, swap(other, xl=1), swap(own, xh=1), swap(other, xl=1, xh=1)])
+    out, after = None, (parts[1][1], parts[1][3])
     for j in range(CHUNKS):
-        own, other = turned[j]
-        held = stack([own, swap(other, xl=1), swap(own, xh=1), swap(other, xl=1, xh=1)], after)
-        l0, l1, l2, l3 = ladder(at, amp, held, swap(held, core=1))
-        got = [swap(l1, z=1), swap(l2, z=2), swap(l3, z=3)]
-        after = (got[0], got[2])
+        held = stack(parts[j], after)
+        peer = swap(held, core=1)
+        l0, l1, l2, l3 = ladder(at, amp, peer, ladder(at, amp, held))
+        got = [swap(l1, z=1), swap(l3, z=3), swap(l2, z=2)]
+        after = (got[0], got[1])
         out = finish(j, l0, got, order, scale, out)
     return out
 

time: 145 us -> 135 us (0.931)
  starting transfers between devices: 63.2 us -> 54.1 us
  waiting for transfers between devices: 54.2 us -> 51.4 us
    ppermute x39 -> x37, starting transfers between devices: 63.2 us -> 54.1 us  [swap(): return lax.ppermute(x, AXES, swap_table(**by))]
    ppermute x39 -> x37, waiting for transfers between devices: 54.2 us -> 51.4 us  [swap(): return lax.ppermute(x, AXES, swap_table(**by))]
    pallas_call x24 -> x25, Pallas kernels: 23.4 us -> 24.7 us  [call(): pl.pallas_call(body, out_shape=[jax.ShapeDtypeStruct(*v) for v in shapes]...]
  transfers between devices with their start and end apart: 39 -> 37, of which waited for: 19 -> 18; matrix products, arithmetic and copies ran while one was open for 0% -> 0% of each run, Pallas kernels for 15% -> 14%
where the time goes in v3:
time: 135 us
  starting transfers between devices  54.1 us (40%)
  waiting for transfers between devices  51.4 us (38%)
  Pallas kernels  24.7 us (18%)
  local copies, waits for them, and re-layouts  3.86 us (3%)
    ppermute x37, starting transfers between devices, swap(): return lax.ppermute(x, AXES, swap_table(**by))  54.1 us
    ppermute x37, waiting for transfers between devices, swap(): return lax.ppermute(x, AXES, swap_table(**by))  51.4 us
    pallas_call x25, Pallas kernels, call(): pl.pallas_call(body, out_shape=[jax.ShapeDtypeStruct(*v) for v in shapes]...  24.7 us
    unnamed x15, local copies, waits for them, and re-layouts  2.78 us
  transfers between devices with their start and end apart: 37, of which 18 were waited for; matrix products, arithmetic and copies ran while one was open for 0% of the time, Pallas kernels for 14%

profile of v3, /device:TPU:1, one launch (start us, length us, event | category | flops | bytes accessed | tf_op | source)
XLA Modules:
  0.0 134.5 jit_solution(11190703144827188885)
XLA Ops:
  1.8 3.7 %collective-permute-start.3 = (bf16[64,1280]{1,0:T(8,128)(2,1)S(1)}, bf16[64,1280]{1,0:T(8,128)(2,1)S(1)}, u32[]{:S(2)}, u32[]{:S(2)}) collective-permute-start(bf16[64,1280]{1,0:T(8,128)(2,1)S(1)} %get-tuple-element.34.refs_0_), channel_id=1, source_target_pairs={{0,64},{1,65},{2,66},{3,67},{4,68},{5,69},{6,70},{7,71},{8,72},{9,... | collective-permute-start | bytes 491528 | tf_op jit(solution)/shard_map/ppermute | solution.py:33
  5.4 1.3 copy-done.1
  7.8 2.8 %collective-permute-start.2 = (bf16[64,1280]{1,0:T(8,128)(2,1)S(1)}, bf16[64,1280]{1,0:T(8,128)(2,1)S(1)}, u32[]{:S(2)}, u32[]{:S(2)}) collective-permute-start(bf16[64,1280]{1,0:T(8,128)(2,1)S(1)} %stack.29.refs_0_), channel_id=1, source_target_pairs={{0,24},{1,25},{2,26},{3,27},{4,28},{5,29},{6,30},{7,31},{8,16},{9,... | collective-permute-start | bytes 491528 | tf_op jit(solution)/shard_map/ppermute | solution.py:33
  10.6 1.6 %collective-permute-start.4 = (bf16[64,1280]{1,0:T(8,128)(2,1)S(1)}, bf16[64,1280]{1,0:T(8,128)(2,1)S(1)}, u32[]{:S(2)}, u32[]{:S(2)}) collective-permute-start(bf16[64,1280]{1,0:T(8,128)(2,1)S(1)} %collective-permute-done.3.refs_0_), channel_id=1, source_target_pairs={{0,1},{1,0},{2,3},{3,2},{4,5},{5,4},{6,7},{7,6},{8,9},{9,8},{10,11... | collective-permute-start | bytes 491528 | tf_op jit(solution)/shard_map/ppermute | solution.py:33
  12.3 1.4 %collective-permute-done.2.refs_3_.refs_0_.refs_6_ = bf16[64,1280]{1,0:T(8,128)(2,1)S(1)} collective-permute-done((bf16[64,1280]{1,0:T(8,128)(2,1)S(1)}, bf16[64,1280]{1,0:T(8,128)(2,1)S(1)}, u32[]{:S(2)}, u32[]{:S(2)}) %collective-permute-start.2) | collective-permute-done | bytes 163872 | tf_op jit(solution)/shard_map/ppermute | solution.py:33
  13.7 1.6 %collective-permute-start.1 = (bf16[64,1280]{1,0:T(8,128)(2,1)S(1)}, bf16[64,1280]{1,0:T(8,128)(2,1)S(1)}, u32[]{:S(2)}, u32[]{:S(2)}) collective-permute-start(bf16[64,1280]{1,0:T(8,128)(2,1)S(1)} %stack.29.refs_0_), channel_id=1, source_target_pairs={{0,16},{1,17},{2,18},{3,19},{4,20},{5,21},{6,22},{7,23},{8,24},{9,... | collective-permute-start | bytes 491528 | tf_op jit(solution)/shard_map/ppermute | solution.py:33
  15.3 3.6 %collective-permute-start.5 = (bf16[64,1280]{1,0:T(8,128)(2,1)S(1)}, bf16[64,1280]{1,0:T(8,128)(2,1)S(1)}, u32[]{:S(2)}, u32[]{:S(2)}) collective-permute-start(bf16[64,1280]{1,0:T(8,128)(2,1)S(1)} %collective-permute-done.3.refs_0_), channel_id=1, source_target_pairs={{0,2},{1,3},{2,0},{3,1},{4,6},{5,7},{6,4},{7,5},{8,10},{9,11},{10,... | collective-permute-start | bytes 491528 | tf_op jit(solution)/shard_map/ppermute | solution.py:33
  18.9 1.3 copy-done.2
  21.1 1.8 %collective-permute-start.12 = (bf16[1250,256]{1,0:T(8,128)(2,1)S(1)}, bf16[1250,256]{1,0:T(8,128)(2,1)S(1)}, u32[]{:S(2)}, u32[]{:S(2)}) collective-permute-start(bf16[1250,256]{1,0:T(8,128)(2,1)S(1)} %cut.7.refs_10_), channel_id=1, source_target_pairs={{0,68},{1,69},{2,70},{3,71},{4,64},{5,65},{6,66},{7,67},{8,76},{9,... | collective-permute-start | bytes 1920008 | tf_op jit(solution)/shard_map/ppermute | solution.py:33
  22.9 3.7 %collective-permute-start.6 = (bf16[64,1280]{1,0:T(8,128)(2,1)S(1)}, bf16[64,1280]{1,0:T(8,128)(2,1)S(1)}, u32[]{:S(2)}, u32[]{:S(2)}) collective-permute-start(bf16[64,1280]{1,0:T(8,128)(2,1)S(1)} %collective-permute-done.3.refs_0_), channel_id=1, source_target_pairs={{0,3},{1,2},{2,1},{3,0},{4,7},{5,6},{6,5},{7,4},{8,11},{9,10},{10,... | collective-permute-start | bytes 491528 | tf_op jit(solution)/shard_map/ppermute | solution.py:33
  26.6 3.0 %collective-permute-done.6.refs_6_.refs_3_ = bf16[64,1280]{1,0:T(8,128)(2,1)S(1)} collective-permute-done((bf16[64,1280]{1,0:T(8,128)(2,1)S(1)}, bf16[64,1280]{1,0:T(8,128)(2,1)S(1)}, u32[]{:S(2)}, u32[]{:S(2)}) %collective-permute-start.6) | collective-permute-done | bytes 163872 | tf_op jit(solution)/shard_map/ppermute | solution.py:33
  29.7 1.3 collective-permute-start.16
  31.0 2.4 %collective-permute-start.10 = (bf16[256,1280]{1,0:T(8,128)(2,1)S(1)}, bf16[256,1280]{1,0:T(8,128)(2,1)S(1)}, u32[]{:S(2)}, u32[]{:S(2)}) collective-permute-start(bf16[256,1280]{1,0:T(8,128)(2,1)S(1)} %stack.30.refs_0_), channel_id=1, source_target_pairs={{0,3},{1,2},{2,1},{3,0},{4,7},{5,6},{6,5},{7,4},{8,11},{9,10},{10,... | collective-permute-start | bytes 1966088 | tf_op jit(solution)/shard_map/ppermute | solution.py:33
  33.5 2.6 %collective-permute-done.11.refs_0_.refs_1_.refs_11_ = bf16[1250,256]{1,0:T(8,128)(2,1)S(1)} collective-permute-done((bf16[1250,256]{1,0:T(8,128)(2,1)S(1)}, bf16[1250,256]{1,0:T(8,128)(2,1)S(1)}, u32[]{:S(2)}, u32[]{:S(2)}) %collective-permute-start.11) | collective-permute-done | bytes 640032 | tf_op jit(solution)/shard_map/ppermute | solution.py:33
  36.0 2.4 %collective-permute-start.9 = (bf16[256,1280]{1,0:T(8,128)(2,1)S(1)}, bf16[256,1280]{1,0:T(8,128)(2,1)S(1)}, u32[]{:S(2)}, u32[]{:S(2)}) collective-permute-start(bf16[256,1280]{1,0:T(8,128)(2,1)S(1)} %stack.30.refs_0_), channel_id=1, source_target_pairs={{0,1},{1,0},{2,3},{3,2},{4,5},{5,4},{6,7},{7,6},{8,9},{9,8},{10,11... | collective-permute-start | bytes 1966088 | tf_op jit(solution)/shard_map/ppermute | solution.py:33
  38.7 4.5 %collective-permute-done.16.source.refs_7_ = bf16[256,1280]{1,0:T(8,128)(2,1)S(1)} collective-permute-done((bf16[256,1280]{1,0:T(8,128)(2,1)S(1)}, bf16[256,1280]{1,0:T(8,128)(2,1)S(1)}, u32[]{:S(2)}, u32[]{:S(2)}) %collective-permute-start.16) | collective-permute-done | bytes 655392 | tf_op jit(solution)/shard_map/ppermute | solution.py:33
  43.4 2.1 %collective-permute-start.17 = (bf16[128,1280]{1,0:T(8,128)(2,1)S(1)}, bf16[128,1280]{1,0:T(8,128)(2,1)S(1)}, u32[]{:S(2)}, u32[]{:S(2)}) collective-permute-start(bf16[128,1280]{1,0:T(8,128)(2,1)S(1)} %cut.10), channel_id=1, source_target_pairs={{0,24},{1,25},{2,26},{3,27},{4,28},{5,29},{6,30},{7,31},{8,16},{9,... | collective-permute-start | bytes 983048 | tf_op jit(solution)/shard_map/ppermute | solution.py:33
  45.6 5.6 %collective-permute-done.9.source.refs_1_ = bf16[256,1280]{1,0:T(8,128)(2,1)S(1)} collective-permute-done((bf16[256,1280]{1,0:T(8,128)(2,1)S(1)}, bf16[256,1280]{1,0:T(8,128)(2,1)S(1)}, u32[]{:S(2)}, u32[]{:S(2)}) %collective-permute-start.9) | collective-permute-done | bytes 655392 | tf_op jit(solution)/shard_map/ppermute | solution.py:33
  51.2 1.8 %collective-permute-start.14 = (bf16[128,1280]{1,0:T(8,128)(2,1)S(1)}, bf16[128,1280]{1,0:T(8,128)(2,1)S(1)}, u32[]{:S(2)}, u32[]{:S(2)}) collective-permute-start(bf16[128,1280]{1,0:T(8,128)(2,1)S(1)} %cut.9), channel_id=1, source_target_pairs={{0,1},{1,0},{2,3},{3,2},{4,5},{5,4},{6,7},{7,6},{8,9},{9,8},{10,11... | collective-permute-start | bytes 983048 | tf_op jit(solution)/shard_map/ppermute | solution.py:33
  53.9 3.0 %collective-permute-start.13 = (bf16[128,1280]{1,0:T(8,128)(2,1)S(1)}, bf16[128,1280]{1,0:T(8,128)(2,1)S(1)}, u32[]{:S(2)}, u32[]{:S(2)}) collective-permute-start(bf16[128,1280]{1,0:T(8,128)(2,1)S(1)} %cut.8), channel_id=1, source_target_pairs={{0,3},{1,2},{2,1},{3,0},{4,7},{5,6},{6,5},{7,4},{8,11},{9,10},{10,... | collective-permute-start | bytes 983048 | tf_op jit(solution)/shard_map/ppermute | solution.py:33
  56.9 1.3 collective-permute-done.14.refs_4_
  58.2 3.9 %collective-permute-done.13.refs_3_ = bf16[128,1280]{1,0:T(8,128)(2,1)S(1)} collective-permute-done((bf16[128,1280]{1,0:T(8,128)(2,1)S(1)}, bf16[128,1280]{1,0:T(8,128)(2,1)S(1)}, u32[]{:S(2)}, u32[]{:S(2)}) %collective-permute-start.13) | collective-permute-done | bytes 327712 | tf_op jit(solution)/shard_map/ppermute | solution.py:33
  62.1 3.6 %tile.3 = (f32[2,1024,128]{2,1,0:T(8,128)S(1)}, f32[2,1024,128]{2,1,0:T(8,128)S(1)}) custom-call(s32[5]{0:T(128)S(1)} %stack.28.at, bf16[256,1280]{1,0:T(8,128)(2,1)S(1)} %stack.30.refs_0_, bf16[256,1280]{1,0:T(8,128)(2,1)S(1)} %collective-permute-done.9.source.refs_1_, bf16[256,1280]{1,0:T(8,128)(2,1)S(1)} %collective-permute-done.10.source.refs_2_, ...), custom_call_target="tpu_custom_call" | custom-call | flops 2621440000 | bytes 10485760 | tf_op jit(solution)/shard_map/tile/pallas_call | solution.py:43
  65.7 3.5 %collective-permute-start.25 = (f32[2,1024,128]{2,1,0:T(8,128)S(1)}, f32[2,1024,128]{2,1,0:T(8,128)S(1)}, u32[]{:S(2)}, u32[]{:S(2)}) collective-permute-start(f32[2,1024,128]{2,1,0:T(8,128)S(1)} %get-tuple-element.40), channel_id=1, source_target_pairs={{0,32},{1,33},{2,34},{3,35},{4,36},{5,37},{6,38},{7,39},{8,40},{9,... | collective-permute-start | bytes 3145736 | tf_op jit(solution)/shard_map/ppermute | solution.py:33
  69.2 3.6 %tile.2 = (f32[2,1024,128]{2,1,0:T(8,128)S(1)}, f32[2,1024,128]{2,1,0:T(8,128)S(1)}) custom-call(s32[5]{0:T(128)S(1)} %stack.28.at, bf16[256,1280]{1,0:T(8,128)(2,1)S(1)} %stack.30.refs_0_, bf16[256,1280]{1,0:T(8,128)(2,1)S(1)} %collective-permute-done.9.source.refs_1_, bf16[256,1280]{1,0:T(8,128)(2,1)S(1)} %collective-permute-done.10.source.refs_2_, ...), custom_call_target="tpu_custom_call" | custom-call | flops 2621440000 | bytes 10485760 | tf_op jit(solution)/shard_map/tile/pallas_call | solution.py:43
  73.1 1.9 %turn.3 = (bf16[64,2048]{1,0:T(8,128)(2,1)S(1)}, bf16[64,2048]{1,0:T(8,128)(2,1)S(1)}) custom-call(f32[2,1024,128]{2,1,0:T(8,128)S(1)} %get-tuple-element.39.keep, f32[2,1024,128]{2,1,0:T(8,128)S(1)} %collective-permute-done.25.got), custom_call_target="tpu_custom_call" | custom-call | bytes 3145728 | tf_op jit(solution)/shard_map/turn/pallas_call | solution.py:43
  75.1 1.4 %collective-permute-start.28 = (bf16[64,2048]{1,0:T(8,128)(2,1)S(1)}, bf16[64,2048]{1,0:T(8,128)(2,1)S(1)}, u32[]{:S(2)}, u32[]{:S(2)}) collective-permute-start(bf16[64,2048]{1,0:T(8,128)(2,1)S(1)} %get-tuple-element.42), channel_id=1, source_target_pairs={{0,68},{1,69},{2,70},{3,71},{4,64},{5,65},{6,66},{7,67},{8,76},{9,... | collective-permute-start | bytes 786440 | tf_op jit(solution)/shard_map/ppermute | solution.py:33
  76.4 1.9 %collective-permute-start.27 = (bf16[64,2048]{1,0:T(8,128)(2,1)S(1)}, bf16[64,2048]{1,0:T(8,128)(2,1)S(1)}, u32[]{:S(2)}, u32[]{:S(2)}) collective-permute-start(bf16[64,2048]{1,0:T(8,128)(2,1)S(1)} %get-tuple-element.41.refs_0_), channel_id=1, source_target_pairs={{0,64},{1,65},{2,66},{3,67},{4,68},{5,69},{6,70},{7,71},{8,72},{9,... | collective-permute-start | bytes 786440 | tf_op jit(solution)/shard_map/ppermute | solution.py:33
  78.3 1.9 %turn.2 = (bf16[64,2048]{1,0:T(8,128)(2,1)S(1)}, bf16[64,2048]{1,0:T(8,128)(2,1)S(1)}) custom-call(f32[2,1024,128]{2,1,0:T(8,128)S(1)} %get-tuple-element.35.keep, f32[2,1024,128]{2,1,0:T(8,128)S(1)} %collective-permute-done.21.got), custom_call_target="tpu_custom_call" | custom-call | bytes 3145728 | tf_op jit(solution)/shard_map/turn/pallas_call | solution.py:43
  82.5 5.6 %collective-permute-done.27.refs_2_ = bf16[64,2048]{1,0:T(8,128)(2,1)S(1)} collective-permute-done((bf16[64,2048]{1,0:T(8,128)(2,1)S(1)}, bf16[64,2048]{1,0:T(8,128)(2,1)S(1)}, u32[]{:S(2)}, u32[]{:S(2)}) %collective-permute-start.27) | collective-permute-done | bytes 262176 | tf_op jit(solution)/shard_map/ppermute | solution.py:33
  89.3 4.4 %collective-permute-done.22.refs_4_.refs_1_ = bf16[64,2048]{1,0:T(8,128)(2,1)S(1)} collective-permute-done((bf16[64,2048]{1,0:T(8,128)(2,1)S(1)}, bf16[64,2048]{1,0:T(8,128)(2,1)S(1)}, u32[]{:S(2)}, u32[]{:S(2)}) %collective-permute-start.22) | collective-permute-done | bytes 262176 | tf_op jit(solution)/shard_map/ppermute | solution.py:33
  95.0 1.5 %collective-permute-start.29 = (bf16[256,2048]{1,0:T(8,128)(2,1)S(1)}, bf16[256,2048]{1,0:T(8,128)(2,1)S(1)}, u32[]{:S(2)}, u32[]{:S(2)}) collective-permute-start(bf16[256,2048]{1,0:T(8,128)(2,1)S(1)} %stack.32.part), channel_id=1, source_target_pairs={{0,32},{1,33},{2,34},{3,35},{4,36},{5,37},{6,38},{7,39},{8,40},{9,... | collective-permute-start | bytes 3145736 | tf_op jit(solution)/shard_map/ppermute | solution.py:33
  97.0 1.8 %ladder.4 = (f32[256,256]{1,0:T(8,128)S(1)}, bf16[256,256]{1,0:T(8,128)(2,1)S(1)}, bf16[256,256]{1,0:T(8,128)(2,1)S(1)}, bf16[256,256]{1,0:T(8,128)(2,1)S(1)}) custom-call(s32[5]{0:T(128)S(1)} %stack.28.at, bf16[1024,2048]{1,0:T(8,128)(2,1)S(1)} %bitcast.8, bf16[256,2048]{1,0:T(8,128)(2,1)S(1)} %stack.32.part), custom_call_target="tpu_custom_call" | custom-call | flops 1073741824 | bytes 6291456 | tf_op jit(solution)/shard_map/ladder/pallas_call | solution.py:43
  98.8 1.8 %ladder.5 = (f32[256,512]{1,0:T(8,128)S(1)}, bf16[256,512]{1,0:T(8,128)(2,1)S(1)}, bf16[256,512]{1,0:T(8,128)(2,1)S(1)}, bf16[256,512]{1,0:T(8,128)(2,1)S(1)}) custom-call(s32[5]{0:T(128)S(1)} %stack.28.at, bf16[1024,2048]{1,0:T(8,128)(2,1)S(1)} %bitcast.9, bf16[256,2048]{1,0:T(8,128)(2,1)S(1)} %collective-permute-done.29.part, ...), custom_call_target="tpu_custom_call" | custom-call | flops 1073741824 | bytes 6291456 | tf_op jit(solution)/shard_map/ladder/pallas_call | solution.py:43
  101.5 2.1 %collective-permute-start.31 = (bf16[256,512]{1,0:T(8,128)(2,1)S(1)}, bf16[256,512]{1,0:T(8,128)(2,1)S(1)}, u32[]{:S(2)}, u32[]{:S(2)}) collective-permute-start(bf16[256,512]{1,0:T(8,128)(2,1)S(1)} %get-tuple-element.48), channel_id=1, source_target_pairs={{0,3},{1,2},{2,1},{3,0},{4,7},{5,6},{6,5},{7,4},{8,11},{9,10},{10,... | collective-permute-start | bytes 786440 | tf_op jit(solution)/shard_map/ppermute | solution.py:33
  103.6 2.3 %collective-permute-done.23.refs_2_ = bf16[64,2048]{1,0:T(8,128)(2,1)S(1)} collective-permute-done((bf16[64,2048]{1,0:T(8,128)(2,1)S(1)}, bf16[64,2048]{1,0:T(8,128)(2,1)S(1)}, u32[]{:S(2)}, u32[]{:S(2)}) %collective-permute-start.23) | collective-permute-done | bytes 262176 | tf_op jit(solution)/shard_map/ppermute | solution.py:33
  105.9 2.5 %collective-permute-done.30.refs_4_.r1 = bf16[256,512]{1,0:T(8,128)(2,1)S(1)} collective-permute-done((bf16[256,512]{1,0:T(8,128)(2,1)S(1)}, bf16[256,512]{1,0:T(8,128)(2,1)S(1)}, u32[]{:S(2)}, u32[]{:S(2)}) %collective-permute-start.30) | collective-permute-done | bytes 262176 | tf_op jit(solution)/shard_map/ppermute | solution.py:33
  108.3 1.6 %collective-permute-done.31.refs_5_.r2 = bf16[256,512]{1,0:T(8,128)(2,1)S(1)} collective-permute-done((bf16[256,512]{1,0:T(8,128)(2,1)S(1)}, bf16[256,512]{1,0:T(8,128)(2,1)S(1)}, u32[]{:S(2)}, u32[]{:S(2)}) %collective-permute-start.31) | collective-permute-done | bytes 262176 | tf_op jit(solution)/shard_map/ppermute | solution.py:33
  110.0 1.6 %collective-permute-start.32 = (bf16[256,2048]{1,0:T(8,128)(2,1)S(1)}, bf16[256,2048]{1,0:T(8,128)(2,1)S(1)}, u32[]{:S(2)}, u32[]{:S(2)}) collective-permute-start(bf16[256,2048]{1,0:T(8,128)(2,1)S(1)} %stack.33.part), channel_id=1, source_target_pairs={{0,32},{1,33},{2,34},{3,35},{4,36},{5,37},{6,38},{7,39},{8,40},{9,... | collective-permute-start | bytes 3145736 | tf_op jit(solution)/shard_map/ppermute | solution.py:33
  111.6 1.9 %collective-permute-start.36 = (bf16[256,512]{1,0:T(8,128)(2,1)S(1)}, bf16[256,512]{1,0:T(8,128)(2,1)S(1)}, u32[]{:S(2)}, u32[]{:S(2)}) collective-permute-start(bf16[256,512]{1,0:T(8,128)(2,1)S(1)} %get-tuple-element.60), channel_id=1, source_target_pairs={{0,2},{1,3},{2,0},{3,1},{4,6},{5,7},{6,4},{7,5},{8,10},{9,11},{10,... | collective-permute-start | bytes 786440 | tf_op jit(solution)/shard_map/ppermute | solution.py:33
  113.5 1.8 %ladder.6 = (f32[256,256]{1,0:T(8,128)S(1)}, bf16[256,256]{1,0:T(8,128)(2,1)S(1)}, bf16[256,256]{1,0:T(8,128)(2,1)S(1)}, bf16[256,256]{1,0:T(8,128)(2,1)S(1)}) custom-call(s32[5]{0:T(128)S(1)} %stack.28.at, bf16[1024,2048]{1,0:T(8,128)(2,1)S(1)} %bitcast.10, bf16[256,2048]{1,0:T(8,128)(2,1)S(1)} %stack.33.part), custom_call_target="tpu_custom_call" | custom-call | flops 1073741824 | bytes 6291456 | tf_op jit(solution)/shard_map/ladder/pallas_call | solution.py:43
  115.4 2.5 %ladder.7 = (f32[256,512]{1,0:T(8,128)S(1)}, bf16[256,512]{1,0:T(8,128)(2,1)}, bf16[256,512]{1,0:T(8,128)(2,1)S(1)}, bf16[256,512]{1,0:T(8,128)(2,1)}) custom-call(s32[5]{0:T(128)S(1)} %stack.28.at, bf16[1024,2048]{1,0:T(8,128)(2,1)S(1)} %bitcast.11, bf16[256,2048]{1,0:T(8,128)(2,1)S(1)} %collective-permute-done.32.part, ...), custom_call_target="tpu_custom_call" | custom-call | flops 1073741824 | bytes 6291456 | tf_op jit(solution)/shard_map/ladder/pallas_call | solution.py:43
  119.3 1.9 %collective-permute-start.35 = (bf16[256,512]{1,0:T(8,128)(2,1)S(1)}, bf16[256,512]{1,0:T(8,128)(2,1)S(1)}, u32[]{:S(2)}, u32[]{:S(2)}) collective-permute-start(bf16[256,512]{1,0:T(8,128)(2,1)S(1)} %get-tuple-element.56), channel_id=1, source_target_pairs={{0,2},{1,3},{2,0},{3,1},{4,6},{5,7},{6,4},{7,5},{8,10},{9,11},{10,... | collective-permute-start | bytes 786440 | tf_op jit(solution)/shard_map/ppermute | solution.py:33
  121.4 1.6 %prepare.1 = (bf16[512,512]{1,0:T(8,128)(2,1)S(1)}, f32[256,1024]{1,0:T(8,128)S(1)}) custom-call(s32[5]{0:T(128)S(1)} %stack.28.at, s32[2]{0:T(128)S(1)} %copy-done.4, f32[1400]{0:T(1024)S(1)} %copy-done.3, s32[256,2]{1,0:T(8,128)S(1)} %copy.9.pairs, f32[1,120]{1,0:T(1,128)S(1)} %bitcast.14), custom_call_target="tpu_custom_call" | custom-call | bytes 1048576 | tf_op jit(solution)/shard_map/prepare/pallas_call | solution.py:43
  123.0 1.4 %finish.2.refs_0_ = f32[256,1024]{1,0:T(8,128)} custom-call(f32[256,512]{1,0:T(8,128)S(1)} %get-tuple-element.59.own, bf16[256,512]{1,0:T(8,128)(2,1)S(1)} %collective-permute-done.30.refs_4_.r1, bf16[256,512]{1,0:T(8,128)(2,1)S(1)} %collective-permute-done.31.refs_5_.r2, bf16[256,512]{1,0:T(8,128)(2,1)S(1)} %collective-permute-done.36.r3, ...), custom_call_target="tpu_custom_call" | custom-call | flops 402653184 | bytes 4194304 | tf_op jit(solution)/shard_map/finish/pallas_call | solution.py:43
  124.4 1.8 %collective-permute-done.33.r1 = bf16[256,512]{1,0:T(8,128)(2,1)S(1)} collective-permute-done((bf16[256,512]{1,0:T(8,128)(2,1)}, bf16[256,512]{1,0:T(8,128)(2,1)S(1)}, u32[]{:S(2)}, u32[]{:S(2)}) %collective-permute-start.33) | collective-permute-done | bytes 262176 | tf_op jit(solution)/shard_map/ppermute | solution.py:33
  126.2 6.7 %collective-permute-done.34.r2 = bf16[256,512]{1,0:T(8,128)(2,1)S(1)} collective-permute-done((bf16[256,512]{1,0:T(8,128)(2,1)}, bf16[256,512]{1,0:T(8,128)(2,1)S(1)}, u32[]{:S(2)}, u32[]{:S(2)}) %collective-permute-start.34) | collective-permute-done | bytes 262176 | tf_op jit(solution)/shard_map/ppermute | solution.py:33
  132.9 1.4 %finish.3 = f32[256,1024]{1,0:T(8,128)} custom-call(f32[256,512]{1,0:T(8,128)S(1)} %get-tuple-element.53.own, bf16[256,512]{1,0:T(8,128)(2,1)S(1)} %collective-permute-done.33.r1, bf16[256,512]{1,0:T(8,128)(2,1)S(1)} %collective-permute-done.34.r2, bf16[256,512]{1,0:T(8,128)(2,1)S(1)} %collective-permute-done.35.r3, ...), custom_call_target="tpu_custom_call", output_to_operand_aliasing={{}: (6, {})} | custom-call | flops 402653184 | bytes 4194304 | tf_op jit(solution)/shard_map/finish/pallas_call | solution.py:43
  (68 shorter events, 13.2 us)
Async XLA Ops:
  1.8 8.9 %collective-permute-start.3 = (bf16[64,1280]{1,0:T(8,128)(2,1)S(1)}, bf16[64,1280]{1,0:T(8,128)(2,1)S(1)}, u32[]{:S(2)}, u32[]{:S(2)}) collective-permute-start(bf16[64,1280]{1,0:T(8,128)(2,1)S(1)} %get-tuple-element.34.refs_0_), channel_id=1, source_target_pairs={{0,64},{1,65},{2,66},{3,67},{4,68},{5,69},{6,70},{7,71},{8,72},{9,... | collective-permute-start | bytes 491528 | tf_op jit(solution)/shard_map/ppermute | solution.py:33
  5.4 1.3 copy-start.1
  6.8 22.8 %collective-permute-start.7 = (bf16[1250,256]{1,0:T(8,128)(2,1)S(1)}, bf16[1250,256]{1,0:T(8,128)(2,1)S(1)}, u32[]{:S(2)}, u32[]{:S(2)}) collective-permute-start(bf16[1250,256]{1,0:T(8,128)(2,1)S(1)} %cut.6.refs_1_.refs_10_), channel_id=1, source_target_pairs={{0,4},{1,5},{2,6},{3,7},{4,0},{5,1},{6,2},{7,3},{8,12},{9,13},{10,... | collective-permute-start | bytes 1920008 | tf_op jit(solution)/shard_map/ppermute | solution.py:33
  7.2 22.4 %collective-permute-start.8 = (bf16[1250,256]{1,0:T(8,128)(2,1)S(1)}, bf16[1250,256]{1,0:T(8,128)(2,1)S(1)}, u32[]{:S(2)}, u32[]{:S(2)}) collective-permute-start(bf16[1250,256]{1,0:T(8,128)(2,1)S(1)} %cut.6.refs_1_.refs_10_), channel_id=1, source_target_pairs={{0,68},{1,69},{2,70},{3,71},{4,64},{5,65},{6,66},{7,67},{8,76},{9,... | collective-permute-start | bytes 1920008 | tf_op jit(solution)/shard_map/ppermute | solution.py:33
  7.8 5.9 %collective-permute-start.2 = (bf16[64,1280]{1,0:T(8,128)(2,1)S(1)}, bf16[64,1280]{1,0:T(8,128)(2,1)S(1)}, u32[]{:S(2)}, u32[]{:S(2)}) collective-permute-start(bf16[64,1280]{1,0:T(8,128)(2,1)S(1)} %stack.29.refs_0_), channel_id=1, source_target_pairs={{0,24},{1,25},{2,26},{3,27},{4,28},{5,29},{6,30},{7,31},{8,16},{9,... | collective-permute-start | bytes 491528 | tf_op jit(solution)/shard_map/ppermute | solution.py:33
  10.6 4.6 %collective-permute-start.4 = (bf16[64,1280]{1,0:T(8,128)(2,1)S(1)}, bf16[64,1280]{1,0:T(8,128)(2,1)S(1)}, u32[]{:S(2)}, u32[]{:S(2)}) collective-permute-start(bf16[64,1280]{1,0:T(8,128)(2,1)S(1)} %collective-permute-done.3.refs_0_), channel_id=1, source_target_pairs={{0,1},{1,0},{2,3},{3,2},{4,5},{5,4},{6,7},{7,6},{8,9},{9,8},{10,11... | collective-permute-start | bytes 491528 | tf_op jit(solution)/shard_map/ppermute | solution.py:33
  12.3 8.0 %collective-permute-start = (bf16[64,1280]{1,0:T(8,128)(2,1)S(1)}, bf16[64,1280]{1,0:T(8,128)(2,1)S(1)}, u32[]{:S(2)}, u32[]{:S(2)}) collective-permute-start(bf16[64,1280]{1,0:T(8,128)(2,1)S(1)} %stack.29.refs_0_), channel_id=1, source_target_pairs={{0,8},{1,9},{2,10},{3,11},{4,12},{5,13},{6,14},{7,15},{8,0},{9,1},... | collective-permute-start | bytes 491528 | tf_op jit(solution)/shard_map/ppermute | solution.py:33
  13.7 7.4 %collective-permute-start.1 = (bf16[64,1280]{1,0:T(8,128)(2,1)S(1)}, bf16[64,1280]{1,0:T(8,128)(2,1)S(1)}, u32[]{:S(2)}, u32[]{:S(2)}) collective-permute-start(bf16[64,1280]{1,0:T(8,128)(2,1)S(1)} %stack.29.refs_0_), channel_id=1, source_target_pairs={{0,16},{1,17},{2,18},{3,19},{4,20},{5,21},{6,22},{7,23},{8,24},{9,... | collective-permute-start | bytes 491528 | tf_op jit(solution)/shard_map/ppermute | solution.py:33
  15.3 7.6 %collective-permute-start.5 = (bf16[64,1280]{1,0:T(8,128)(2,1)S(1)}, bf16[64,1280]{1,0:T(8,128)(2,1)S(1)}, u32[]{:S(2)}, u32[]{:S(2)}) collective-permute-start(bf16[64,1280]{1,0:T(8,128)(2,1)S(1)} %collective-permute-done.3.refs_0_), channel_id=1, source_target_pairs={{0,2},{1,3},{2,0},{3,1},{4,6},{5,7},{6,4},{7,5},{8,10},{9,11},{10,... | collective-permute-start | bytes 491528 | tf_op jit(solution)/shard_map/ppermute | solution.py:33
  18.9 1.3 copy-start.2
  20.3 15.8 %collective-permute-start.11 = (bf16[1250,256]{1,0:T(8,128)(2,1)S(1)}, bf16[1250,256]{1,0:T(8,128)(2,1)S(1)}, u32[]{:S(2)}, u32[]{:S(2)}) collective-permute-start(bf16[1250,256]{1,0:T(8,128)(2,1)S(1)} %cut.7.refs_10_), channel_id=1, source_target_pairs={{0,4},{1,5},{2,6},{3,7},{4,0},{5,1},{6,2},{7,3},{8,12},{9,13},{10,... | collective-permute-start | bytes 1920008 | tf_op jit(solution)/shard_map/ppermute | solution.py:33
  21.1 17.4 %collective-permute-start.12 = (bf16[1250,256]{1,0:T(8,128)(2,1)S(1)}, bf16[1250,256]{1,0:T(8,128)(2,1)S(1)}, u32[]{:S(2)}, u32[]{:S(2)}) collective-permute-start(bf16[1250,256]{1,0:T(8,128)(2,1)S(1)} %cut.7.refs_10_), channel_id=1, source_target_pairs={{0,68},{1,69},{2,70},{3,71},{4,64},{5,65},{6,66},{7,67},{8,76},{9,... | collective-permute-start | bytes 1920008 | tf_op jit(solution)/shard_map/ppermute | solution.py:33
  22.9 6.7 %collective-permute-start.6 = (bf16[64,1280]{1,0:T(8,128)(2,1)S(1)}, bf16[64,1280]{1,0:T(8,128)(2,1)S(1)}, u32[]{:S(2)}, u32[]{:S(2)}) collective-permute-start(bf16[64,1280]{1,0:T(8,128)(2,1)S(1)} %collective-permute-done.3.refs_0_), channel_id=1, source_target_pairs={{0,3},{1,2},{2,1},{3,0},{4,7},{5,6},{6,5},{7,4},{8,11},{9,10},{10,... | collective-permute-start | bytes 491528 | tf_op jit(solution)/shard_map/ppermute | solution.py:33
  29.7 13.6 %collective-permute-start.16 = (bf16[256,1280]{1,0:T(8,128)(2,1)S(1)}, bf16[256,1280]{1,0:T(8,128)(2,1)S(1)}, u32[]{:S(2)}, u32[]{:S(2)}) collective-permute-start(bf16[256,1280]{1,0:T(8,128)(2,1)S(1)} %stack.31.refs_5_), channel_id=1, source_target_pairs={{0,24},{1,25},{2,26},{3,27},{4,28},{5,29},{6,30},{7,31},{8,16},{9,... | collective-permute-start | bytes 1966088 | tf_op jit(solution)/shard_map/ppermute | solution.py:33
  31.0 12.3 %collective-permute-start.15 = (bf16[256,1280]{1,0:T(8,128)(2,1)S(1)}, bf16[256,1280]{1,0:T(8,128)(2,1)S(1)}, u32[]{:S(2)}, u32[]{:S(2)}) collective-permute-start(bf16[256,1280]{1,0:T(8,128)(2,1)S(1)} %stack.31.refs_5_), channel_id=1, source_target_pairs={{0,8},{1,9},{2,10},{3,11},{4,12},{5,13},{6,14},{7,15},{8,0},{9,1},... | collective-permute-start | bytes 1966088 | tf_op jit(solution)/shard_map/ppermute | solution.py:33
  31.0 12.4 %collective-permute-start.10 = (bf16[256,1280]{1,0:T(8,128)(2,1)S(1)}, bf16[256,1280]{1,0:T(8,128)(2,1)S(1)}, u32[]{:S(2)}, u32[]{:S(2)}) collective-permute-start(bf16[256,1280]{1,0:T(8,128)(2,1)S(1)} %stack.30.refs_0_), channel_id=1, source_target_pairs={{0,3},{1,2},{2,1},{3,0},{4,7},{5,6},{6,5},{7,4},{8,11},{9,10},{10,... | collective-permute-start | bytes 1966088 | tf_op jit(solution)/shard_map/ppermute | solution.py:33
  36.0 15.2 %collective-permute-start.9 = (bf16[256,1280]{1,0:T(8,128)(2,1)S(1)}, bf16[256,1280]{1,0:T(8,128)(2,1)S(1)}, u32[]{:S(2)}, u32[]{:S(2)}) collective-permute-start(bf16[256,1280]{1,0:T(8,128)(2,1)S(1)} %stack.30.refs_0_), channel_id=1, source_target_pairs={{0,1},{1,0},{2,3},{3,2},{4,5},{5,4},{6,7},{7,6},{8,9},{9,8},{10,11... | collective-permute-start | bytes 1966088 | tf_op jit(solution)/shard_map/ppermute | solution.py:33
  38.5 15.3 %collective-permute-start.19 = (bf16[1250,256]{1,0:T(8,128)(2,1)S(1)}, bf16[1250,256]{1,0:T(8,128)(2,1)S(1)}, u32[]{:S(2)}, u32[]{:S(2)}) collective-permute-start(bf16[1250,256]{1,0:T(8,128)(2,1)S(1)} %join.2), channel_id=1, source_target_pairs={{0,68},{1,69},{2,70},{3,71},{4,64},{5,65},{6,66},{7,67},{8,76},{9,... | collective-permute-start | bytes 1920008 | tf_op jit(solution)/shard_map/ppermute | solution.py:33
  43.3 13.6 %collective-permute-start.20 = (bf16[1250,256]{1,0:T(8,128)(2,1)S(1)}, bf16[1250,256]{1,0:T(8,128)(2,1)S(1)}, u32[]{:S(2)}, u32[]{:S(2)}) collective-permute-start(bf16[1250,256]{1,0:T(8,128)(2,1)S(1)} %join.3), channel_id=1, source_target_pairs={{0,4},{1,5},{2,6},{3,7},{4,0},{5,1},{6,2},{7,3},{8,12},{9,13},{10,... | collective-permute-start | bytes 1920008 | tf_op jit(solution)/shard_map/ppermute | solution.py:33
  43.3 13.6 %collective-permute-start.18 = (bf16[128,1280]{1,0:T(8,128)(2,1)S(1)}, bf16[128,1280]{1,0:T(8,128)(2,1)S(1)}, u32[]{:S(2)}, u32[]{:S(2)}) collective-permute-start(bf16[128,1280]{1,0:T(8,128)(2,1)S(1)} %cut.11), channel_id=1, source_target_pairs={{0,8},{1,9},{2,10},{3,11},{4,12},{5,13},{6,14},{7,15},{8,0},{9,1},... | collective-permute-start | bytes 983048 | tf_op jit(solution)/shard_map/ppermute | solution.py:33
  43.4 13.4 %collective-permute-start.17 = (bf16[128,1280]{1,0:T(8,128)(2,1)S(1)}, bf16[128,1280]{1,0:T(8,128)(2,1)S(1)}, u32[]{:S(2)}, u32[]{:S(2)}) collective-permute-start(bf16[128,1280]{1,0:T(8,128)(2,1)S(1)} %cut.10), channel_id=1, source_target_pairs={{0,24},{1,25},{2,26},{3,27},{4,28},{5,29},{6,30},{7,31},{8,16},{9,... | collective-permute-start | bytes 983048 | tf_op jit(solution)/shard_map/ppermute | solution.py:33
  51.2 7.0 %collective-permute-start.14 = (bf16[128,1280]{1,0:T(8,128)(2,1)S(1)}, bf16[128,1280]{1,0:T(8,128)(2,1)S(1)}, u32[]{:S(2)}, u32[]{:S(2)}) collective-permute-start(bf16[128,1280]{1,0:T(8,128)(2,1)S(1)} %cut.9), channel_id=1, source_target_pairs={{0,1},{1,0},{2,3},{3,2},{4,5},{5,4},{6,7},{7,6},{8,9},{9,8},{10,11... | collective-permute-start | bytes 983048 | tf_op jit(solution)/shard_map/ppermute | solution.py:33
  53.9 8.2 %collective-permute-start.13 = (bf16[128,1280]{1,0:T(8,128)(2,1)S(1)}, bf16[128,1280]{1,0:T(8,128)(2,1)S(1)}, u32[]{:S(2)}, u32[]{:S(2)}) collective-permute-start(bf16[128,1280]{1,0:T(8,128)(2,1)S(1)} %cut.8), channel_id=1, source_target_pairs={{0,3},{1,2},{2,1},{3,0},{4,7},{5,6},{6,5},{7,4},{8,11},{9,10},{10,... | collective-permute-start | bytes 983048 | tf_op jit(solution)/shard_map/ppermute | solution.py:33
  65.7 7.4 %collective-permute-start.25 = (f32[2,1024,128]{2,1,0:T(8,128)S(1)}, f32[2,1024,128]{2,1,0:T(8,128)S(1)}, u32[]{:S(2)}, u32[]{:S(2)}) collective-permute-start(f32[2,1024,128]{2,1,0:T(8,128)S(1)} %get-tuple-element.40), channel_id=1, source_target_pairs={{0,32},{1,33},{2,34},{3,35},{4,36},{5,37},{6,38},{7,39},{8,40},{9,... | collective-permute-start | bytes 3145736 | tf_op jit(solution)/shard_map/ppermute | solution.py:33
  72.8 24.2 %copy-start = (bf16[1024,1,2048]{2,0,1:T(8,128)(2,1)S(1)}, bf16[1024,1,2048]{2,0,1:T(8,128)(2,1)}, u32[]{:S(2)}) copy-start(bf16[1024,1,2048]{2,0,1:T(8,128)(2,1)} %param.9) | copy-start | bytes 12582916
  72.8 5.5 %collective-permute-start.21 = (f32[2,1024,128]{2,1,0:T(8,128)S(1)}, f32[2,1024,128]{2,1,0:T(8,128)S(1)}, u32[]{:S(2)}, u32[]{:S(2)}) collective-permute-start(f32[2,1024,128]{2,1,0:T(8,128)S(1)} %get-tuple-element.36), channel_id=1, source_target_pairs={{0,32},{1,33},{2,34},{3,35},{4,36},{5,37},{6,38},{7,39},{8,40},{9,... | collective-permute-start | bytes 3145736 | tf_op jit(solution)/shard_map/ppermute | solution.py:33
  75.0 7.5 %collective-permute-start.26 = (bf16[64,2048]{1,0:T(8,128)(2,1)S(1)}, bf16[64,2048]{1,0:T(8,128)(2,1)S(1)}, u32[]{:S(2)}, u32[]{:S(2)}) collective-permute-start(bf16[64,2048]{1,0:T(8,128)(2,1)S(1)} %get-tuple-element.42), channel_id=1, source_target_pairs={{0,4},{1,5},{2,6},{3,7},{4,0},{5,1},{6,2},{7,3},{8,12},{9,13},{10,... | collective-permute-start | bytes 786440 | tf_op jit(solution)/shard_map/ppermute | solution.py:33
  75.1 14.2 %collective-permute-start.28 = (bf16[64,2048]{1,0:T(8,128)(2,1)S(1)}, bf16[64,2048]{1,0:T(8,128)(2,1)S(1)}, u32[]{:S(2)}, u32[]{:S(2)}) collective-permute-start(bf16[64,2048]{1,0:T(8,128)(2,1)S(1)} %get-tuple-element.42), channel_id=1, source_target_pairs={{0,68},{1,69},{2,70},{3,71},{4,64},{5,65},{6,66},{7,67},{8,76},{9,... | collective-permute-start | bytes 786440 | tf_op jit(solution)/shard_map/ppermute | solution.py:33
  76.4 11.6 %collective-permute-start.27 = (bf16[64,2048]{1,0:T(8,128)(2,1)S(1)}, bf16[64,2048]{1,0:T(8,128)(2,1)S(1)}, u32[]{:S(2)}, u32[]{:S(2)}) collective-permute-start(bf16[64,2048]{1,0:T(8,128)(2,1)S(1)} %get-tuple-element.41.refs_0_), channel_id=1, source_target_pairs={{0,64},{1,65},{2,66},{3,67},{4,68},{5,69},{6,70},{7,71},{8,72},{9,... | collective-permute-start | bytes 786440 | tf_op jit(solution)/shard_map/ppermute | solution.py:33
  80.3 13.5 %collective-permute-start.22 = (bf16[64,2048]{1,0:T(8,128)(2,1)S(1)}, bf16[64,2048]{1,0:T(8,128)(2,1)S(1)}, u32[]{:S(2)}, u32[]{:S(2)}) collective-permute-start(bf16[64,2048]{1,0:T(8,128)(2,1)S(1)} %get-tuple-element.38), channel_id=1, source_target_pairs={{0,4},{1,5},{2,6},{3,7},{4,0},{5,1},{6,2},{7,3},{8,12},{9,13},{10,... | collective-permute-start | bytes 786440 | tf_op jit(solution)/shard_map/ppermute | solution.py:33
  80.4 14.5 %collective-permute-start.24 = (bf16[64,2048]{1,0:T(8,128)(2,1)S(1)}, bf16[64,2048]{1,0:T(8,128)(2,1)S(1)}, u32[]{:S(2)}, u32[]{:S(2)}) collective-permute-start(bf16[64,2048]{1,0:T(8,128)(2,1)S(1)} %get-tuple-element.38), channel_id=1, source_target_pairs={{0,68},{1,69},{2,70},{3,71},{4,64},{5,65},{6,66},{7,67},{8,76},{9,... | collective-permute-start | bytes 786440 | tf_op jit(solution)/shard_map/ppermute | solution.py:33
  95.0 3.8 %collective-permute-start.29 = (bf16[256,2048]{1,0:T(8,128)(2,1)S(1)}, bf16[256,2048]{1,0:T(8,128)(2,1)S(1)}, u32[]{:S(2)}, u32[]{:S(2)}) collective-permute-start(bf16[256,2048]{1,0:T(8,128)(2,1)S(1)} %stack.32.part), channel_id=1, source_target_pairs={{0,32},{1,33},{2,34},{3,35},{4,36},{5,37},{6,38},{7,39},{8,40},{9,... | collective-permute-start | bytes 3145736 | tf_op jit(solution)/shard_map/ppermute | solution.py:33
  96.5 9.4 %collective-permute-start.23 = (bf16[64,2048]{1,0:T(8,128)(2,1)S(1)}, bf16[64,2048]{1,0:T(8,128)(2,1)S(1)}, u32[]{:S(2)}, u32[]{:S(2)}) collective-permute-start(bf16[64,2048]{1,0:T(8,128)(2,1)S(1)} %get-tuple-element.37.refs_0_), channel_id=1, source_target_pairs={{0,64},{1,65},{2,66},{3,67},{4,68},{5,69},{6,70},{7,71},{8,72},{9,... | collective-permute-start | bytes 786440 | tf_op jit(solution)/shard_map/ppermute | solution.py:33
  100.7 7.6 %collective-permute-start.30 = (bf16[256,512]{1,0:T(8,128)(2,1)S(1)}, bf16[256,512]{1,0:T(8,128)(2,1)S(1)}, u32[]{:S(2)}, u32[]{:S(2)}) collective-permute-start(bf16[256,512]{1,0:T(8,128)(2,1)S(1)} %get-tuple-element.47), channel_id=1, source_target_pairs={{0,1},{1,0},{2,3},{3,2},{4,5},{5,4},{6,7},{7,6},{8,9},{9,8},{10,11... | collective-permute-start | bytes 786440 | tf_op jit(solution)/shard_map/ppermute | solution.py:33
  101.5 8.4 %collective-permute-start.31 = (bf16[256,512]{1,0:T(8,128)(2,1)S(1)}, bf16[256,512]{1,0:T(8,128)(2,1)S(1)}, u32[]{:S(2)}, u32[]{:S(2)}) collective-permute-start(bf16[256,512]{1,0:T(8,128)(2,1)S(1)} %get-tuple-element.48), channel_id=1, source_target_pairs={{0,3},{1,2},{2,1},{3,0},{4,7},{5,6},{6,5},{7,4},{8,11},{9,10},{10,... | collective-permute-start | bytes 786440 | tf_op jit(solution)/shard_map/ppermute | solution.py:33
  110.0 5.4 %collective-permute-start.32 = (bf16[256,2048]{1,0:T(8,128)(2,1)S(1)}, bf16[256,2048]{1,0:T(8,128)(2,1)S(1)}, u32[]{:S(2)}, u32[]{:S(2)}) collective-permute-start(bf16[256,2048]{1,0:T(8,128)(2,1)S(1)} %stack.33.part), channel_id=1, source_target_pairs={{0,32},{1,33},{2,34},{3,35},{4,36},{5,37},{6,38},{7,39},{8,40},{9,... | collective-permute-start | bytes 3145736 | tf_op jit(solution)/shard_map/ppermute | solution.py:33
  111.6 11.4 %collective-permute-start.36 = (bf16[256,512]{1,0:T(8,128)(2,1)S(1)}, bf16[256,512]{1,0:T(8,128)(2,1)S(1)}, u32[]{:S(2)}, u32[]{:S(2)}) collective-permute-start(bf16[256,512]{1,0:T(8,128)(2,1)S(1)} %get-tuple-element.60), channel_id=1, source_target_pairs={{0,2},{1,3},{2,0},{3,1},{4,6},{5,7},{6,4},{7,5},{8,10},{9,11},{10,... | collective-permute-start | bytes 786440 | tf_op jit(solution)/shard_map/ppermute | solution.py:33
  115.3 5.9 %copy-start.6 = (s32[256,2]{0,1:T(2,128)S(1)}, s32[256,2]{0,1:T(2,128)}, u32[]{:S(2)}) copy-start(s32[256,2]{0,1:T(2,128)} %param.10) | copy-start | bytes 6148
  115.4 6.0 %copy-start.3 = (f32[1400]{0:T(1024)S(1)}, f32[1400]{0:T(1024)}, u32[]{:S(2)}) copy-start(f32[1400]{0:T(1024)} %virt.1) | copy-start | bytes 16804
  115.4 6.0 %copy-start.4 = (s32[2]{0:T(128)S(1)}, s32[2]{0:T(128)}, u32[]{:S(2)}) copy-start(s32[2]{0:T(128)} %offsets.1) | copy-start | bytes 28
  115.4 6.0 %copy-start.5 = (f32[120]{0:T(128)S(1)}, f32[120]{0:T(128)}, u32[]{:S(2)}) copy-start(f32[120]{0:T(128)} %param.12) | copy-start | bytes 1444
  117.9 8.3 %collective-permute-start.33 = (bf16[256,512]{1,0:T(8,128)(2,1)}, bf16[256,512]{1,0:T(8,128)(2,1)S(1)}, u32[]{:S(2)}, u32[]{:S(2)}) collective-permute-start(bf16[256,512]{1,0:T(8,128)(2,1)} %get-tuple-element.54), channel_id=1, source_target_pairs={{0,1},{1,0},{2,3},{3,2},{4,5},{5,4},{6,7},{7,6},{8,9},{9,8},{10,11... | collective-permute-start | bytes 786440 | tf_op jit(solution)/shard_map/ppermute | solution.py:33
  118.7 14.2 %collective-permute-start.34 = (bf16[256,512]{1,0:T(8,128)(2,1)}, bf16[256,512]{1,0:T(8,128)(2,1)S(1)}, u32[]{:S(2)}, u32[]{:S(2)}) collective-permute-start(bf16[256,512]{1,0:T(8,128)(2,1)} %get-tuple-element.55), channel_id=1, source_target_pairs={{0,3},{1,2},{2,1},{3,0},{4,7},{5,6},{6,5},{7,4},{8,11},{9,10},{10,... | collective-permute-start | bytes 786440 | tf_op jit(solution)/shard_map/ppermute | solution.py:33
  119.3 13.6 %collective-permute-start.35 = (bf16[256,512]{1,0:T(8,128)(2,1)S(1)}, bf16[256,512]{1,0:T(8,128)(2,1)S(1)}, u32[]{:S(2)}, u32[]{:S(2)}) collective-permute-start(bf16[256,512]{1,0:T(8,128)(2,1)S(1)} %get-tuple-element.56), channel_id=1, source_target_pairs={{0,2},{1,3},{2,0},{3,1},{4,6},{5,7},{6,4},{7,5},{8,10},{9,11},{10,... | collective-permute-start | bytes 786440 | tf_op jit(solution)/shard_map/ppermute | solution.py:33

commit v4 on v3

--- a/solution.py
+++ b/solution.py
@@ -156,10 +156,10 @@
 
 
 def ladder_kernel(at, amp, part, *refs):
-    halves, outs = refs[:-4], refs[-4:]
+    halves, outs = refs[:-3], refs[-3:]
     for s, out in enumerate(outs):
-        rows = pl.ds(pl.multiple_of((at[Z] ^ s) * 256, 256), 256)
-        total = dot_nt(amp[rows, :], part[...]).astype(out.dtype)
+        rows = pl.ds(pl.multiple_of((at[Z] ^ (s + 1)) * 256, 256), 256)
+        total = dot_nt(amp[rows, :], part[...]).astype(BF16)
         if halves:
             out[:, :256] = halves[s][...]
             out[:, 256:] = total
@@ -171,13 +171,25 @@
     shape = (256, 512 if halves else 256)
     return call(
         ladder_kernel,
-        [(shape, F32)] + [(shape, BF16)] * 3,
+        [(shape, BF16)] * 3,
         (at, amp, part, *halves),
         [SMEM] + [VMEM] * (2 + len(halves)),
         "ladder",
-        flops=2 * 1024 * 2048 * 256,
-        size=6 * MIB,
-    )
+        flops=2 * 768 * 2048 * 256,
+        size=4 * MIB,
+    )
+
+
+def own_kernel(at, amp, mine, peer, *refs):
+    rows = pl.ds(pl.multiple_of(at[Z] * 256, 256), 256)
+    for k, part in enumerate((mine, peer)):
+        refs[-1][:, k * 256:(k + 1) * 256] = dot_nt(amp[rows, :], part[...])
+
+
+def own_ladder(at, amp, mine, peer, after):
+    inputs = (at, amp, mine, peer, *after)
+    places = [SMEM] + [VMEM] * 3 + [HBM] * len(after)
+    return call(own_kernel, ((256, 512), F32), inputs, places, "own", flops=2 * 256 * 2048 * 512, size=4 * MIB)
 
 
 def finish_kernel(j, own, r1, r2, r3, order, scale, *refs):
@@ -225,7 +237,7 @@
     for a in range(64):
         ea = jnp.where(lane % 64 == a, virt[offsets[0] + a], ea)
     b_start = offsets[1] + (at[Y] * 2 + at[XL]) * 16
-    first, second = pairs[:, 0:1], pairs[:, 1:2]
+    first, second = (jnp.broadcast_to(pairs[i:i + 1, :], (8, 256)).T[:, 0:1] for i in (0, 1))
     levels = lax.broadcasted_iota(jnp.int32, (256, 120), 1)
     occupied = jnp.sum(jnp.where(levels == first, occ[...], 0.0), axis=1, keepdims=True)
     occupied += jnp.sum(jnp.where(levels == second, occ[...], 0.0), axis=1, keepdims=True)
@@ -239,7 +251,7 @@
     return call(
         prepare_kernel,
         [((512, 512), BF16), ((256, 1024), F32)],
-        (at, offsets, virt, pairs, occ.reshape(1, -1)),
+        (at, offsets, virt, pairs.T, occ.reshape(1, -1)),
         [SMEM] * 3 + [VMEM] * 2,
         "prepare",
     )
@@ -289,7 +301,8 @@
     for j in range(CHUNKS):
         held = stack(parts[j], after)
         peer = swap(held, core=1)
-        l0, l1, l2, l3 = ladder(at, amp, peer, ladder(at, amp, held))
+        l1, l2, l3 = ladder(at, amp, peer, ladder(at, amp, held))
+        l0 = own_ladder(at, amp, held, peer, (l1,))
         got = [swap(l1, z=1), swap(l3, z=3), swap(l2, z=2)]
         after = (got[0], got[1])
         out = finish(j, l0, got, order, scale, out)

time: 135 us -> 134 us (level)
  waiting for transfers between devices: 51.4 us -> 49.6 us
    ppermute x37, waiting for transfers between devices: 51.4 us -> 49.6 us  [swap(): return lax.ppermute(x, AXES, swap_table(**by))]
    pallas_call x25 -> x27, Pallas kernels: 24.7 us -> 25.5 us  [call(): pl.pallas_call(body, out_shape=[jax.ShapeDtypeStruct(*v) for v in shapes]...]
    unnamed x15 -> x14, local copies, waits for them, and re-layouts: 2.78 us -> 2.63 us
  transfers between devices with their start and end apart: 37 -> 37, of which waited for: 18 -> 20; matrix products, arithmetic and copies ran while one was open for 0% -> 0% of each run, Pallas kernels for 14% -> 15%
where the time goes in v4:
time: 134 us
  starting transfers between devices  54.3 us (41%)
  waiting for transfers between devices  49.6 us (37%)
  Pallas kernels  25.5 us (19%)
  local copies, waits for them, and re-layouts  3.72 us (3%)
    ppermute x37, starting transfers between devices, swap(): return lax.ppermute(x, AXES, swap_table(**by))  54.3 us
    ppermute x37, waiting for transfers between devices, swap(): return lax.ppermute(x, AXES, swap_table(**by))  49.6 us
    pallas_call x27, Pallas kernels, call(): pl.pallas_call(body, out_shape=[jax.ShapeDtypeStruct(*v) for v in shapes]...  25.5 us
  transfers between devices with their start and end apart: 37, of which 20 were waited for; matrix products, arithmetic and copies ran while one was open for 0% of the time, Pallas kernels for 15%

profile of v4, /device:TPU:1, one launch (start us, length us, event | category | flops | bytes accessed | tf_op | source)
XLA Modules:
  0.0 133.6 jit_solution(15573381833592090566)
XLA Ops:
  1.8 3.7 %collective-permute-start.3 = (bf16[64,1280]{1,0:T(8,128)(2,1)S(1)}, bf16[64,1280]{1,0:T(8,128)(2,1)S(1)}, u32[]{:S(2)}, u32[]{:S(2)}) collective-permute-start(bf16[64,1280]{1,0:T(8,128)(2,1)S(1)} %get-tuple-element.30.refs_0_), channel_id=1, source_target_pairs={{0,64},{1,65},{2,66},{3,67},{4,68},{5,69},{6,70},{7,71},{8,72},{9,... | collective-permute-start | bytes 491528 | tf_op jit(solution)/shard_map/ppermute | solution.py:33
  5.4 1.3 copy-done.1
  7.8 2.8 %collective-permute-start.2 = (bf16[64,1280]{1,0:T(8,128)(2,1)S(1)}, bf16[64,1280]{1,0:T(8,128)(2,1)S(1)}, u32[]{:S(2)}, u32[]{:S(2)}) collective-permute-start(bf16[64,1280]{1,0:T(8,128)(2,1)S(1)} %stack.29.refs_0_), channel_id=1, source_target_pairs={{0,24},{1,25},{2,26},{3,27},{4,28},{5,29},{6,30},{7,31},{8,16},{9,... | collective-permute-start | bytes 491528 | tf_op jit(solution)/shard_map/ppermute | solution.py:33
  10.6 1.6 %collective-permute-start.4 = (bf16[64,1280]{1,0:T(8,128)(2,1)S(1)}, bf16[64,1280]{1,0:T(8,128)(2,1)S(1)}, u32[]{:S(2)}, u32[]{:S(2)}) collective-permute-start(bf16[64,1280]{1,0:T(8,128)(2,1)S(1)} %collective-permute-done.3.refs_0_), channel_id=1, source_target_pairs={{0,1},{1,0},{2,3},{3,2},{4,5},{5,4},{6,7},{7,6},{8,9},{9,8},{10,11... | collective-permute-start | bytes 491528 | tf_op jit(solution)/shard_map/ppermute | solution.py:33
  12.3 1.4 %collective-permute-done.2.refs_3_.refs_0_.refs_6_ = bf16[64,1280]{1,0:T(8,128)(2,1)S(1)} collective-permute-done((bf16[64,1280]{1,0:T(8,128)(2,1)S(1)}, bf16[64,1280]{1,0:T(8,128)(2,1)S(1)}, u32[]{:S(2)}, u32[]{:S(2)}) %collective-permute-start.2) | collective-permute-done | bytes 163872 | tf_op jit(solution)/shard_map/ppermute | solution.py:33
  13.7 1.6 %collective-permute-start.1 = (bf16[64,1280]{1,0:T(8,128)(2,1)S(1)}, bf16[64,1280]{1,0:T(8,128)(2,1)S(1)}, u32[]{:S(2)}, u32[]{:S(2)}) collective-permute-start(bf16[64,1280]{1,0:T(8,128)(2,1)S(1)} %stack.29.refs_0_), channel_id=1, source_target_pairs={{0,16},{1,17},{2,18},{3,19},{4,20},{5,21},{6,22},{7,23},{8,24},{9,... | collective-permute-start | bytes 491528 | tf_op jit(solution)/shard_map/ppermute | solution.py:33
  15.3 3.6 %collective-permute-start.5 = (bf16[64,1280]{1,0:T(8,128)(2,1)S(1)}, bf16[64,1280]{1,0:T(8,128)(2,1)S(1)}, u32[]{:S(2)}, u32[]{:S(2)}) collective-permute-start(bf16[64,1280]{1,0:T(8,128)(2,1)S(1)} %collective-permute-done.3.refs_0_), channel_id=1, source_target_pairs={{0,2},{1,3},{2,0},{3,1},{4,6},{5,7},{6,4},{7,5},{8,10},{9,11},{10,... | collective-permute-start | bytes 491528 | tf_op jit(solution)/shard_map/ppermute | solution.py:33
  18.9 1.3 copy-done.2
  21.1 1.8 %collective-permute-start.12 = (bf16[1250,256]{1,0:T(8,128)(2,1)S(1)}, bf16[1250,256]{1,0:T(8,128)(2,1)S(1)}, u32[]{:S(2)}, u32[]{:S(2)}) collective-permute-start(bf16[1250,256]{1,0:T(8,128)(2,1)S(1)} %cut.7.refs_10_), channel_id=1, source_target_pairs={{0,68},{1,69},{2,70},{3,71},{4,64},{5,65},{6,66},{7,67},{8,76},{9,... | collective-permute-start | bytes 1920008 | tf_op jit(solution)/shard_map/ppermute | solution.py:33
  22.9 3.7 %collective-permute-start.6 = (bf16[64,1280]{1,0:T(8,128)(2,1)S(1)}, bf16[64,1280]{1,0:T(8,128)(2,1)S(1)}, u32[]{:S(2)}, u32[]{:S(2)}) collective-permute-start(bf16[64,1280]{1,0:T(8,128)(2,1)S(1)} %collective-permute-done.3.refs_0_), channel_id=1, source_target_pairs={{0,3},{1,2},{2,1},{3,0},{4,7},{5,6},{6,5},{7,4},{8,11},{9,10},{10,... | collective-permute-start | bytes 491528 | tf_op jit(solution)/shard_map/ppermute | solution.py:33
  26.6 3.0 %collective-permute-done.6.refs_6_.refs_3_ = bf16[64,1280]{1,0:T(8,128)(2,1)S(1)} collective-permute-done((bf16[64,1280]{1,0:T(8,128)(2,1)S(1)}, bf16[64,1280]{1,0:T(8,128)(2,1)S(1)}, u32[]{:S(2)}, u32[]{:S(2)}) %collective-permute-start.6) | collective-permute-done | bytes 163872 | tf_op jit(solution)/shard_map/ppermute | solution.py:33
  29.7 1.3 %collective-permute-start.16 = (bf16[256,1280]{1,0:T(8,128)(2,1)S(1)}, bf16[256,1280]{1,0:T(8,128)(2,1)S(1)}, u32[]{:S(2)}, u32[]{:S(2)}) collective-permute-start(bf16[256,1280]{1,0:T(8,128)(2,1)S(1)} %stack.31.refs_5_), channel_id=1, source_target_pairs={{0,24},{1,25},{2,26},{3,27},{4,28},{5,29},{6,30},{7,31},{8,16},{9,... | collective-permute-start | bytes 1966088 | tf_op jit(solution)/shard_map/ppermute | solution.py:33
  31.0 2.4 %collective-permute-start.10 = (bf16[256,1280]{1,0:T(8,128)(2,1)S(1)}, bf16[256,1280]{1,0:T(8,128)(2,1)S(1)}, u32[]{:S(2)}, u32[]{:S(2)}) collective-permute-start(bf16[256,1280]{1,0:T(8,128)(2,1)S(1)} %stack.30.refs_0_), channel_id=1, source_target_pairs={{0,3},{1,2},{2,1},{3,0},{4,7},{5,6},{6,5},{7,4},{8,11},{9,10},{10,... | collective-permute-start | bytes 1966088 | tf_op jit(solution)/shard_map/ppermute | solution.py:33
  33.5 2.6 %collective-permute-done.11.refs_0_.refs_1_.refs_11_ = bf16[1250,256]{1,0:T(8,128)(2,1)S(1)} collective-permute-done((bf16[1250,256]{1,0:T(8,128)(2,1)S(1)}, bf16[1250,256]{1,0:T(8,128)(2,1)S(1)}, u32[]{:S(2)}, u32[]{:S(2)}) %collective-permute-start.11) | collective-permute-done | bytes 640032 | tf_op jit(solution)/shard_map/ppermute | solution.py:33
  36.0 2.4 %collective-permute-start.9 = (bf16[256,1280]{1,0:T(8,128)(2,1)S(1)}, bf16[256,1280]{1,0:T(8,128)(2,1)S(1)}, u32[]{:S(2)}, u32[]{:S(2)}) collective-permute-start(bf16[256,1280]{1,0:T(8,128)(2,1)S(1)} %stack.30.refs_0_), channel_id=1, source_target_pairs={{0,1},{1,0},{2,3},{3,2},{4,5},{5,4},{6,7},{7,6},{8,9},{9,8},{10,11... | collective-permute-start | bytes 1966088 | tf_op jit(solution)/shard_map/ppermute | solution.py:33
  38.7 4.5 %collective-permute-done.16.source.refs_7_ = bf16[256,1280]{1,0:T(8,128)(2,1)S(1)} collective-permute-done((bf16[256,1280]{1,0:T(8,128)(2,1)S(1)}, bf16[256,1280]{1,0:T(8,128)(2,1)S(1)}, u32[]{:S(2)}, u32[]{:S(2)}) %collective-permute-start.16) | collective-permute-done | bytes 655392 | tf_op jit(solution)/shard_map/ppermute | solution.py:33
  43.4 2.1 %collective-permute-start.17 = (bf16[128,1280]{1,0:T(8,128)(2,1)S(1)}, bf16[128,1280]{1,0:T(8,128)(2,1)S(1)}, u32[]{:S(2)}, u32[]{:S(2)}) collective-permute-start(bf16[128,1280]{1,0:T(8,128)(2,1)S(1)} %cut.10), channel_id=1, source_target_pairs={{0,24},{1,25},{2,26},{3,27},{4,28},{5,29},{6,30},{7,31},{8,16},{9,... | collective-permute-start | bytes 983048 | tf_op jit(solution)/shard_map/ppermute | solution.py:33
  45.6 5.6 %collective-permute-done.9.source.refs_1_ = bf16[256,1280]{1,0:T(8,128)(2,1)S(1)} collective-permute-done((bf16[256,1280]{1,0:T(8,128)(2,1)S(1)}, bf16[256,1280]{1,0:T(8,128)(2,1)S(1)}, u32[]{:S(2)}, u32[]{:S(2)}) %collective-permute-start.9) | collective-permute-done | bytes 655392 | tf_op jit(solution)/shard_map/ppermute | solution.py:33
  51.2 1.8 %collective-permute-start.14 = (bf16[128,1280]{1,0:T(8,128)(2,1)S(1)}, bf16[128,1280]{1,0:T(8,128)(2,1)S(1)}, u32[]{:S(2)}, u32[]{:S(2)}) collective-permute-start(bf16[128,1280]{1,0:T(8,128)(2,1)S(1)} %cut.9), channel_id=1, source_target_pairs={{0,1},{1,0},{2,3},{3,2},{4,5},{5,4},{6,7},{7,6},{8,9},{9,8},{10,11... | collective-permute-start | bytes 983048 | tf_op jit(solution)/shard_map/ppermute | solution.py:33
  53.9 3.0 %collective-permute-start.13 = (bf16[128,1280]{1,0:T(8,128)(2,1)S(1)}, bf16[128,1280]{1,0:T(8,128)(2,1)S(1)}, u32[]{:S(2)}, u32[]{:S(2)}) collective-permute-start(bf16[128,1280]{1,0:T(8,128)(2,1)S(1)} %cut.8), channel_id=1, source_target_pairs={{0,3},{1,2},{2,1},{3,0},{4,7},{5,6},{6,5},{7,4},{8,11},{9,10},{10,... | collective-permute-start | bytes 983048 | tf_op jit(solution)/shard_map/ppermute | solution.py:33
  56.9 1.3 collective-permute-done.14.refs_4_
  58.2 3.9 %collective-permute-done.13.refs_3_ = bf16[128,1280]{1,0:T(8,128)(2,1)S(1)} collective-permute-done((bf16[128,1280]{1,0:T(8,128)(2,1)S(1)}, bf16[128,1280]{1,0:T(8,128)(2,1)S(1)}, u32[]{:S(2)}, u32[]{:S(2)}) %collective-permute-start.13) | collective-permute-done | bytes 327712 | tf_op jit(solution)/shard_map/ppermute | solution.py:33
  62.1 3.6 %tile.3 = (f32[2,1024,128]{2,1,0:T(8,128)S(1)}, f32[2,1024,128]{2,1,0:T(8,128)S(1)}) custom-call(s32[5]{0:T(128)S(1)} %stack.28.at, bf16[256,1280]{1,0:T(8,128)(2,1)S(1)} %stack.30.refs_0_, bf16[256,1280]{1,0:T(8,128)(2,1)S(1)} %collective-permute-done.9.source.refs_1_, bf16[256,1280]{1,0:T(8,128)(2,1)S(1)} %collective-permute-done.10.source.refs_2_, ...), custom_call_target="tpu_custom_call" | custom-call | flops 2621440000 | bytes 10485760 | tf_op jit(solution)/shard_map/tile/pallas_call | solution.py:43
  65.7 3.5 %collective-permute-start.25 = (f32[2,1024,128]{2,1,0:T(8,128)S(1)}, f32[2,1024,128]{2,1,0:T(8,128)S(1)}, u32[]{:S(2)}, u32[]{:S(2)}) collective-permute-start(f32[2,1024,128]{2,1,0:T(8,128)S(1)} %get-tuple-element.36), channel_id=1, source_target_pairs={{0,32},{1,33},{2,34},{3,35},{4,36},{5,37},{6,38},{7,39},{8,40},{9,... | collective-permute-start | bytes 3145736 | tf_op jit(solution)/shard_map/ppermute | solution.py:33
  69.2 3.6 %tile.2 = (f32[2,1024,128]{2,1,0:T(8,128)S(1)}, f32[2,1024,128]{2,1,0:T(8,128)S(1)}) custom-call(s32[5]{0:T(128)S(1)} %stack.28.at, bf16[256,1280]{1,0:T(8,128)(2,1)S(1)} %stack.30.refs_0_, bf16[256,1280]{1,0:T(8,128)(2,1)S(1)} %collective-permute-done.9.source.refs_1_, bf16[256,1280]{1,0:T(8,128)(2,1)S(1)} %collective-permute-done.10.source.refs_2_, ...), custom_call_target="tpu_custom_call" | custom-call | flops 2621440000 | bytes 10485760 | tf_op jit(solution)/shard_map/tile/pallas_call | solution.py:43
  73.1 1.9 %turn.3 = (bf16[64,2048]{1,0:T(8,128)(2,1)S(1)}, bf16[64,2048]{1,0:T(8,128)(2,1)S(1)}) custom-call(f32[2,1024,128]{2,1,0:T(8,128)S(1)} %get-tuple-element.35.keep, f32[2,1024,128]{2,1,0:T(8,128)S(1)} %collective-permute-done.25.got), custom_call_target="tpu_custom_call" | custom-call | bytes 3145728 | tf_op jit(solution)/shard_map/turn/pallas_call | solution.py:43
  75.1 1.4 %collective-permute-start.28 = (bf16[64,2048]{1,0:T(8,128)(2,1)S(1)}, bf16[64,2048]{1,0:T(8,128)(2,1)S(1)}, u32[]{:S(2)}, u32[]{:S(2)}) collective-permute-start(bf16[64,2048]{1,0:T(8,128)(2,1)S(1)} %get-tuple-element.38), channel_id=1, source_target_pairs={{0,68},{1,69},{2,70},{3,71},{4,64},{5,65},{6,66},{7,67},{8,76},{9,... | collective-permute-start | bytes 786440 | tf_op jit(solution)/shard_map/ppermute | solution.py:33
  76.4 1.9 %collective-permute-start.27 = (bf16[64,2048]{1,0:T(8,128)(2,1)S(1)}, bf16[64,2048]{1,0:T(8,128)(2,1)S(1)}, u32[]{:S(2)}, u32[]{:S(2)}) collective-permute-start(bf16[64,2048]{1,0:T(8,128)(2,1)S(1)} %get-tuple-element.37.refs_0_), channel_id=1, source_target_pairs={{0,64},{1,65},{2,66},{3,67},{4,68},{5,69},{6,70},{7,71},{8,72},{9,... | collective-permute-start | bytes 786440 | tf_op jit(solution)/shard_map/ppermute | solution.py:33
  78.3 1.9 %turn.2 = (bf16[64,2048]{1,0:T(8,128)(2,1)S(1)}, bf16[64,2048]{1,0:T(8,128)(2,1)S(1)}) custom-call(f32[2,1024,128]{2,1,0:T(8,128)S(1)} %get-tuple-element.31.keep, f32[2,1024,128]{2,1,0:T(8,128)S(1)} %collective-permute-done.21.got), custom_call_target="tpu_custom_call" | custom-call | bytes 3145728 | tf_op jit(solution)/shard_map/turn/pallas_call | solution.py:43
  82.5 5.6 %collective-permute-done.27.refs_2_ = bf16[64,2048]{1,0:T(8,128)(2,1)S(1)} collective-permute-done((bf16[64,2048]{1,0:T(8,128)(2,1)S(1)}, bf16[64,2048]{1,0:T(8,128)(2,1)S(1)}, u32[]{:S(2)}, u32[]{:S(2)}) %collective-permute-start.27) | collective-permute-done | bytes 262176 | tf_op jit(solution)/shard_map/ppermute | solution.py:33
  89.3 4.4 %collective-permute-done.22.refs_4_.refs_1_ = bf16[64,2048]{1,0:T(8,128)(2,1)S(1)} collective-permute-done((bf16[64,2048]{1,0:T(8,128)(2,1)S(1)}, bf16[64,2048]{1,0:T(8,128)(2,1)S(1)}, u32[]{:S(2)}, u32[]{:S(2)}) %collective-permute-start.22) | collective-permute-done | bytes 262176 | tf_op jit(solution)/shard_map/ppermute | solution.py:33
  95.0 1.5 %collective-permute-start.29 = (bf16[256,2048]{1,0:T(8,128)(2,1)S(1)}, bf16[256,2048]{1,0:T(8,128)(2,1)S(1)}, u32[]{:S(2)}, u32[]{:S(2)}) collective-permute-start(bf16[256,2048]{1,0:T(8,128)(2,1)S(1)} %stack.32.part.mine), channel_id=1, source_target_pairs={{0,32},{1,33},{2,34},{3,35},{4,36},{5,37},{6,38},{7,39},{8,40},{9,... | collective-permute-start | bytes 3145736 | tf_op jit(solution)/shard_map/ppermute | solution.py:33
  97.0 1.6 %ladder.4 = (bf16[256,256]{1,0:T(8,128)(2,1)S(1)}, bf16[256,256]{1,0:T(8,128)(2,1)S(1)}, bf16[256,256]{1,0:T(8,128)(2,1)S(1)}) custom-call(s32[5]{0:T(128)S(1)} %stack.28.at, bf16[1024,2048]{1,0:T(8,128)(2,1)S(1)} %bitcast.9, bf16[256,2048]{1,0:T(8,128)(2,1)S(1)} %stack.32.part.mine), custom_call_target="tpu_custom_call" | custom-call | flops 805306368 | bytes 4194304 | tf_op jit(solution)/shard_map/ladder/pallas_call | solution.py:43
  98.8 1.5 %ladder.5 = (bf16[256,512]{1,0:T(8,128)(2,1)S(1)}, bf16[256,512]{1,0:T(8,128)(2,1)S(1)}, bf16[256,512]{1,0:T(8,128)(2,1)S(1)}) custom-call(s32[5]{0:T(128)S(1)} %stack.28.at, bf16[1024,2048]{1,0:T(8,128)(2,1)S(1)} %bitcast.10, bf16[256,2048]{1,0:T(8,128)(2,1)S(1)} %collective-permute-done.29.part.peer, bf16[256,256]{1,0:T(8,128)(2,1)S(1)} %get-tuple-element.39.refs_0_, ...), custom_call_target="tpu_custom_call" | custom-call | flops 805306368 | bytes 4194304 | tf_op jit(solution)/shard_map/ladder/pallas_call | solution.py:43
  101.2 2.1 %collective-permute-start.31 = (bf16[256,512]{1,0:T(8,128)(2,1)S(1)}, bf16[256,512]{1,0:T(8,128)(2,1)S(1)}, u32[]{:S(2)}, u32[]{:S(2)}) collective-permute-start(bf16[256,512]{1,0:T(8,128)(2,1)S(1)} %get-tuple-element.43), channel_id=1, source_target_pairs={{0,3},{1,2},{2,1},{3,0},{4,7},{5,6},{6,5},{7,4},{8,11},{9,10},{10,... | collective-permute-start | bytes 786440 | tf_op jit(solution)/shard_map/ppermute | solution.py:33
  103.2 2.6 %collective-permute-done.23.refs_2_ = bf16[64,2048]{1,0:T(8,128)(2,1)S(1)} collective-permute-done((bf16[64,2048]{1,0:T(8,128)(2,1)S(1)}, bf16[64,2048]{1,0:T(8,128)(2,1)S(1)}, u32[]{:S(2)}, u32[]{:S(2)}) %collective-permute-start.23) | collective-permute-done | bytes 262176 | tf_op jit(solution)/shard_map/ppermute | solution.py:33
  105.9 2.1 %collective-permute-done.30.refs_4_.r1 = bf16[256,512]{1,0:T(8,128)(2,1)S(1)} collective-permute-done((bf16[256,512]{1,0:T(8,128)(2,1)S(1)}, bf16[256,512]{1,0:T(8,128)(2,1)S(1)}, u32[]{:S(2)}, u32[]{:S(2)}) %collective-permute-start.30) | collective-permute-done | bytes 262176 | tf_op jit(solution)/shard_map/ppermute | solution.py:33
  107.9 1.6 %collective-permute-done.31.refs_5_.r2 = bf16[256,512]{1,0:T(8,128)(2,1)S(1)} collective-permute-done((bf16[256,512]{1,0:T(8,128)(2,1)S(1)}, bf16[256,512]{1,0:T(8,128)(2,1)S(1)}, u32[]{:S(2)}, u32[]{:S(2)}) %collective-permute-start.31) | collective-permute-done | bytes 262176 | tf_op jit(solution)/shard_map/ppermute | solution.py:33
  109.6 1.6 %collective-permute-start.32 = (bf16[256,2048]{1,0:T(8,128)(2,1)S(1)}, bf16[256,2048]{1,0:T(8,128)(2,1)S(1)}, u32[]{:S(2)}, u32[]{:S(2)}) collective-permute-start(bf16[256,2048]{1,0:T(8,128)(2,1)S(1)} %stack.33.part.mine), channel_id=1, source_target_pairs={{0,32},{1,33},{2,34},{3,35},{4,36},{5,37},{6,38},{7,39},{8,40},{9,... | collective-permute-start | bytes 3145736 | tf_op jit(solution)/shard_map/ppermute | solution.py:33
  111.3 2.0 %collective-permute-start.36 = (bf16[256,512]{1,0:T(8,128)(2,1)S(1)}, bf16[256,512]{1,0:T(8,128)(2,1)S(1)}, u32[]{:S(2)}, u32[]{:S(2)}) collective-permute-start(bf16[256,512]{1,0:T(8,128)(2,1)S(1)} %get-tuple-element.52), channel_id=1, source_target_pairs={{0,2},{1,3},{2,0},{3,1},{4,6},{5,7},{6,4},{7,5},{8,10},{9,11},{10,... | collective-permute-start | bytes 786440 | tf_op jit(solution)/shard_map/ppermute | solution.py:33
  113.2 1.5 %ladder.6 = (bf16[256,256]{1,0:T(8,128)(2,1)S(1)}, bf16[256,256]{1,0:T(8,128)(2,1)S(1)}, bf16[256,256]{1,0:T(8,128)(2,1)S(1)}) custom-call(s32[5]{0:T(128)S(1)} %stack.28.at, bf16[1024,2048]{1,0:T(8,128)(2,1)S(1)} %bitcast.11, bf16[256,2048]{1,0:T(8,128)(2,1)S(1)} %stack.33.part.mine), custom_call_target="tpu_custom_call" | custom-call | flops 805306368 | bytes 4194304 | tf_op jit(solution)/shard_map/ladder/pallas_call | solution.py:43
  114.8 1.5 %ladder.7 = (bf16[256,512]{1,0:T(8,128)(2,1)S(1)}, bf16[256,512]{1,0:T(8,128)(2,1)S(1)}, bf16[256,512]{1,0:T(8,128)(2,1)S(1)}) custom-call(s32[5]{0:T(128)S(1)} %stack.28.at, bf16[1024,2048]{1,0:T(8,128)(2,1)S(1)} %bitcast.12, bf16[256,2048]{1,0:T(8,128)(2,1)S(1)} %collective-permute-done.32.part.peer, bf16[256,256]{1,0:T(8,128)(2,1)S(1)} %get-tuple-element.44.refs_0_, ...), custom_call_target="tpu_custom_call" | custom-call | flops 805306368 | bytes 4194304 | tf_op jit(solution)/shard_map/ladder/pallas_call | solution.py:43
  117.8 1.9 %collective-permute-start.35 = (bf16[256,512]{1,0:T(8,128)(2,1)S(1)}, bf16[256,512]{1,0:T(8,128)(2,1)S(1)}, u32[]{:S(2)}, u32[]{:S(2)}) collective-permute-start(bf16[256,512]{1,0:T(8,128)(2,1)S(1)} %get-tuple-element.49), channel_id=1, source_target_pairs={{0,2},{1,3},{2,0},{3,1},{4,6},{5,7},{6,4},{7,5},{8,10},{9,11},{10,... | collective-permute-start | bytes 786440 | tf_op jit(solution)/shard_map/ppermute | solution.py:33
  119.7 1.6 %prepare.1 = (bf16[512,512]{1,0:T(8,128)(2,1)S(1)}, f32[256,1024]{1,0:T(8,128)S(1)}) custom-call(s32[5]{0:T(128)S(1)} %stack.28.at, s32[2]{0:T(128)S(1)} %copy-done.5, f32[1400]{0:T(1024)S(1)} %copy-done.3, s32[2,256]{1,0:T(2,128)S(1)} %bitcast.17, f32[1,120]{1,0:T(1,128)S(1)} %bitcast.18), custom_call_target="tpu_custom_call" | custom-call | bytes 1048576 | tf_op jit(solution)/shard_map/prepare/pallas_call | solution.py:43
  121.3 1.3 own.3
  122.7 1.4 %finish.2.refs_0_ = f32[256,1024]{1,0:T(8,128)} custom-call(f32[256,512]{1,0:T(8,128)S(1)} %own.3, bf16[256,512]{1,0:T(8,128)(2,1)S(1)} %collective-permute-done.30.refs_4_.r1, bf16[256,512]{1,0:T(8,128)(2,1)S(1)} %collective-permute-done.31.refs_5_.r2, bf16[256,512]{1,0:T(8,128)(2,1)S(1)} %collective-permute-done.36.r3, ...), custom_call_target="tpu_custom_call" | custom-call | flops 402653184 | bytes 4194304 | tf_op jit(solution)/shard_map/finish/pallas_call | solution.py:43
  126.1 5.9 %collective-permute-done.35.r3 = bf16[256,512]{1,0:T(8,128)(2,1)S(1)} collective-permute-done((bf16[256,512]{1,0:T(8,128)(2,1)S(1)}, bf16[256,512]{1,0:T(8,128)(2,1)S(1)}, u32[]{:S(2)}, u32[]{:S(2)}) %collective-permute-start.35) | collective-permute-done | bytes 262176 | tf_op jit(solution)/shard_map/ppermute | solution.py:33
  132.0 1.4 %finish.3 = f32[256,1024]{1,0:T(8,128)} custom-call(f32[256,512]{1,0:T(8,128)S(1)} %own.2, bf16[256,512]{1,0:T(8,128)(2,1)S(1)} %collective-permute-done.33.r1, bf16[256,512]{1,0:T(8,128)(2,1)S(1)} %collective-permute-done.34.r2, bf16[256,512]{1,0:T(8,128)(2,1)S(1)} %collective-permute-done.35.r3, ...), custom_call_target="tpu_custom_call", output_to_operand_aliasing={{}: (6, {})} | custom-call | flops 402653184 | bytes 4194304 | tf_op jit(solution)/shard_map/finish/pallas_call | solution.py:43
  (69 shorter events, 15.4 us)
Async XLA Ops:
  1.8 8.9 %collective-permute-start.3 = (bf16[64,1280]{1,0:T(8,128)(2,1)S(1)}, bf16[64,1280]{1,0:T(8,128)(2,1)S(1)}, u32[]{:S(2)}, u32[]{:S(2)}) collective-permute-start(bf16[64,1280]{1,0:T(8,128)(2,1)S(1)} %get-tuple-element.30.refs_0_), channel_id=1, source_target_pairs={{0,64},{1,65},{2,66},{3,67},{4,68},{5,69},{6,70},{7,71},{8,72},{9,... | collective-permute-start | bytes 491528 | tf_op jit(solution)/shard_map/ppermute | solution.py:33
  5.4 1.3 copy-start.1
  6.8 22.8 %collective-permute-start.7 = (bf16[1250,256]{1,0:T(8,128)(2,1)S(1)}, bf16[1250,256]{1,0:T(8,128)(2,1)S(1)}, u32[]{:S(2)}, u32[]{:S(2)}) collective-permute-start(bf16[1250,256]{1,0:T(8,128)(2,1)S(1)} %cut.6.refs_1_.refs_10_), channel_id=1, source_target_pairs={{0,4},{1,5},{2,6},{3,7},{4,0},{5,1},{6,2},{7,3},{8,12},{9,13},{10,... | collective-permute-start | bytes 1920008 | tf_op jit(solution)/shard_map/ppermute | solution.py:33
  7.2 22.4 %collective-permute-start.8 = (bf16[1250,256]{1,0:T(8,128)(2,1)S(1)}, bf16[1250,256]{1,0:T(8,128)(2,1)S(1)}, u32[]{:S(2)}, u32[]{:S(2)}) collective-permute-start(bf16[1250,256]{1,0:T(8,128)(2,1)S(1)} %cut.6.refs_1_.refs_10_), channel_id=1, source_target_pairs={{0,68},{1,69},{2,70},{3,71},{4,64},{5,65},{6,66},{7,67},{8,76},{9,... | collective-permute-start | bytes 1920008 | tf_op jit(solution)/shard_map/ppermute | solution.py:33
  7.8 5.9 %collective-permute-start.2 = (bf16[64,1280]{1,0:T(8,128)(2,1)S(1)}, bf16[64,1280]{1,0:T(8,128)(2,1)S(1)}, u32[]{:S(2)}, u32[]{:S(2)}) collective-permute-start(bf16[64,1280]{1,0:T(8,128)(2,1)S(1)} %stack.29.refs_0_), channel_id=1, source_target_pairs={{0,24},{1,25},{2,26},{3,27},{4,28},{5,29},{6,30},{7,31},{8,16},{9,... | collective-permute-start | bytes 491528 | tf_op jit(solution)/shard_map/ppermute | solution.py:33
  10.6 4.6 %collective-permute-start.4 = (bf16[64,1280]{1,0:T(8,128)(2,1)S(1)}, bf16[64,1280]{1,0:T(8,128)(2,1)S(1)}, u32[]{:S(2)}, u32[]{:S(2)}) collective-permute-start(bf16[64,1280]{1,0:T(8,128)(2,1)S(1)} %collective-permute-done.3.refs_0_), channel_id=1, source_target_pairs={{0,1},{1,0},{2,3},{3,2},{4,5},{5,4},{6,7},{7,6},{8,9},{9,8},{10,11... | collective-permute-start | bytes 491528 | tf_op jit(solution)/shard_map/ppermute | solution.py:33
  12.3 8.0 %collective-permute-start = (bf16[64,1280]{1,0:T(8,128)(2,1)S(1)}, bf16[64,1280]{1,0:T(8,128)(2,1)S(1)}, u32[]{:S(2)}, u32[]{:S(2)}) collective-permute-start(bf16[64,1280]{1,0:T(8,128)(2,1)S(1)} %stack.29.refs_0_), channel_id=1, source_target_pairs={{0,8},{1,9},{2,10},{3,11},{4,12},{5,13},{6,14},{7,15},{8,0},{9,1},... | collective-permute-start | bytes 491528 | tf_op jit(solution)/shard_map/ppermute | solution.py:33
  13.7 7.4 %collective-permute-start.1 = (bf16[64,1280]{1,0:T(8,128)(2,1)S(1)}, bf16[64,1280]{1,0:T(8,128)(2,1)S(1)}, u32[]{:S(2)}, u32[]{:S(2)}) collective-permute-start(bf16[64,1280]{1,0:T(8,128)(2,1)S(1)} %stack.29.refs_0_), channel_id=1, source_target_pairs={{0,16},{1,17},{2,18},{3,19},{4,20},{5,21},{6,22},{7,23},{8,24},{9,... | collective-permute-start | bytes 491528 | tf_op jit(solution)/shard_map/ppermute | solution.py:33
  15.3 7.6 %collective-permute-start.5 = (bf16[64,1280]{1,0:T(8,128)(2,1)S(1)}, bf16[64,1280]{1,0:T(8,128)(2,1)S(1)}, u32[]{:S(2)}, u32[]{:S(2)}) collective-permute-start(bf16[64,1280]{1,0:T(8,128)(2,1)S(1)} %collective-permute-done.3.refs_0_), channel_id=1, source_target_pairs={{0,2},{1,3},{2,0},{3,1},{4,6},{5,7},{6,4},{7,5},{8,10},{9,11},{10,... | collective-permute-start | bytes 491528 | tf_op jit(solution)/shard_map/ppermute | solution.py:33
  18.9 1.3 copy-start.2
  20.3 15.8 %collective-permute-start.11 = (bf16[1250,256]{1,0:T(8,128)(2,1)S(1)}, bf16[1250,256]{1,0:T(8,128)(2,1)S(1)}, u32[]{:S(2)}, u32[]{:S(2)}) collective-permute-start(bf16[1250,256]{1,0:T(8,128)(2,1)S(1)} %cut.7.refs_10_), channel_id=1, source_target_pairs={{0,4},{1,5},{2,6},{3,7},{4,0},{5,1},{6,2},{7,3},{8,12},{9,13},{10,... | collective-permute-start | bytes 1920008 | tf_op jit(solution)/shard_map/ppermute | solution.py:33
  21.1 17.4 %collective-permute-start.12 = (bf16[1250,256]{1,0:T(8,128)(2,1)S(1)}, bf16[1250,256]{1,0:T(8,128)(2,1)S(1)}, u32[]{:S(2)}, u32[]{:S(2)}) collective-permute-start(bf16[1250,256]{1,0:T(8,128)(2,1)S(1)} %cut.7.refs_10_), channel_id=1, source_target_pairs={{0,68},{1,69},{2,70},{3,71},{4,64},{5,65},{6,66},{7,67},{8,76},{9,... | collective-permute-start | bytes 1920008 | tf_op jit(solution)/shard_map/ppermute | solution.py:33
  22.9 6.7 %collective-permute-start.6 = (bf16[64,1280]{1,0:T(8,128)(2,1)S(1)}, bf16[64,1280]{1,0:T(8,128)(2,1)S(1)}, u32[]{:S(2)}, u32[]{:S(2)}) collective-permute-start(bf16[64,1280]{1,0:T(8,128)(2,1)S(1)} %collective-permute-done.3.refs_0_), channel_id=1, source_target_pairs={{0,3},{1,2},{2,1},{3,0},{4,7},{5,6},{6,5},{7,4},{8,11},{9,10},{10,... | collective-permute-start | bytes 491528 | tf_op jit(solution)/shard_map/ppermute | solution.py:33
  29.7 13.6 %collective-permute-start.16 = (bf16[256,1280]{1,0:T(8,128)(2,1)S(1)}, bf16[256,1280]{1,0:T(8,128)(2,1)S(1)}, u32[]{:S(2)}, u32[]{:S(2)}) collective-permute-start(bf16[256,1280]{1,0:T(8,128)(2,1)S(1)} %stack.31.refs_5_), channel_id=1, source_target_pairs={{0,24},{1,25},{2,26},{3,27},{4,28},{5,29},{6,30},{7,31},{8,16},{9,... | collective-permute-start | bytes 1966088 | tf_op jit(solution)/shard_map/ppermute | solution.py:33
  31.0 12.3 %collective-permute-start.15 = (bf16[256,1280]{1,0:T(8,128)(2,1)S(1)}, bf16[256,1280]{1,0:T(8,128)(2,1)S(1)}, u32[]{:S(2)}, u32[]{:S(2)}) collective-permute-start(bf16[256,1280]{1,0:T(8,128)(2,1)S(1)} %stack.31.refs_5_), channel_id=1, source_target_pairs={{0,8},{1,9},{2,10},{3,11},{4,12},{5,13},{6,14},{7,15},{8,0},{9,1},... | collective-permute-start | bytes 1966088 | tf_op jit(solution)/shard_map/ppermute | solution.py:33
  31.0 12.4 %collective-permute-start.10 = (bf16[256,1280]{1,0:T(8,128)(2,1)S(1)}, bf16[256,1280]{1,0:T(8,128)(2,1)S(1)}, u32[]{:S(2)}, u32[]{:S(2)}) collective-permute-start(bf16[256,1280]{1,0:T(8,128)(2,1)S(1)} %stack.30.refs_0_), channel_id=1, source_target_pairs={{0,3},{1,2},{2,1},{3,0},{4,7},{5,6},{6,5},{7,4},{8,11},{9,10},{10,... | collective-permute-start | bytes 1966088 | tf_op jit(solution)/shard_map/ppermute | solution.py:33
  36.0 15.2 %collective-permute-start.9 = (bf16[256,1280]{1,0:T(8,128)(2,1)S(1)}, bf16[256,1280]{1,0:T(8,128)(2,1)S(1)}, u32[]{:S(2)}, u32[]{:S(2)}) collective-permute-start(bf16[256,1280]{1,0:T(8,128)(2,1)S(1)} %stack.30.refs_0_), channel_id=1, source_target_pairs={{0,1},{1,0},{2,3},{3,2},{4,5},{5,4},{6,7},{7,6},{8,9},{9,8},{10,11... | collective-permute-start | bytes 1966088 | tf_op jit(solution)/shard_map/ppermute | solution.py:33
  38.5 15.3 %collective-permute-start.19 = (bf16[1250,256]{1,0:T(8,128)(2,1)S(1)}, bf16[1250,256]{1,0:T(8,128)(2,1)S(1)}, u32[]{:S(2)}, u32[]{:S(2)}) collective-permute-start(bf16[1250,256]{1,0:T(8,128)(2,1)S(1)} %join.2), channel_id=1, source_target_pairs={{0,68},{1,69},{2,70},{3,71},{4,64},{5,65},{6,66},{7,67},{8,76},{9,... | collective-permute-start | bytes 1920008 | tf_op jit(solution)/shard_map/ppermute | solution.py:33
  43.3 13.6 %collective-permute-start.20 = (bf16[1250,256]{1,0:T(8,128)(2,1)S(1)}, bf16[1250,256]{1,0:T(8,128)(2,1)S(1)}, u32[]{:S(2)}, u32[]{:S(2)}) collective-permute-start(bf16[1250,256]{1,0:T(8,128)(2,1)S(1)} %join.3), channel_id=1, source_target_pairs={{0,4},{1,5},{2,6},{3,7},{4,0},{5,1},{6,2},{7,3},{8,12},{9,13},{10,... | collective-permute-start | bytes 1920008 | tf_op jit(solution)/shard_map/ppermute | solution.py:33
  43.3 13.6 %collective-permute-start.18 = (bf16[128,1280]{1,0:T(8,128)(2,1)S(1)}, bf16[128,1280]{1,0:T(8,128)(2,1)S(1)}, u32[]{:S(2)}, u32[]{:S(2)}) collective-permute-start(bf16[128,1280]{1,0:T(8,128)(2,1)S(1)} %cut.11), channel_id=1, source_target_pairs={{0,8},{1,9},{2,10},{3,11},{4,12},{5,13},{6,14},{7,15},{8,0},{9,1},... | collective-permute-start | bytes 983048 | tf_op jit(solution)/shard_map/ppermute | solution.py:33
  43.4 13.4 %collective-permute-start.17 = (bf16[128,1280]{1,0:T(8,128)(2,1)S(1)}, bf16[128,1280]{1,0:T(8,128)(2,1)S(1)}, u32[]{:S(2)}, u32[]{:S(2)}) collective-permute-start(bf16[128,1280]{1,0:T(8,128)(2,1)S(1)} %cut.10), channel_id=1, source_target_pairs={{0,24},{1,25},{2,26},{3,27},{4,28},{5,29},{6,30},{7,31},{8,16},{9,... | collective-permute-start | bytes 983048 | tf_op jit(solution)/shard_map/ppermute | solution.py:33
  51.2 7.0 %collective-permute-start.14 = (bf16[128,1280]{1,0:T(8,128)(2,1)S(1)}, bf16[128,1280]{1,0:T(8,128)(2,1)S(1)}, u32[]{:S(2)}, u32[]{:S(2)}) collective-permute-start(bf16[128,1280]{1,0:T(8,128)(2,1)S(1)} %cut.9), channel_id=1, source_target_pairs={{0,1},{1,0},{2,3},{3,2},{4,5},{5,4},{6,7},{7,6},{8,9},{9,8},{10,11... | collective-permute-start | bytes 983048 | tf_op jit(solution)/shard_map/ppermute | solution.py:33
  53.9 8.2 %collective-permute-start.13 = (bf16[128,1280]{1,0:T(8,128)(2,1)S(1)}, bf16[128,1280]{1,0:T(8,128)(2,1)S(1)}, u32[]{:S(2)}, u32[]{:S(2)}) collective-permute-start(bf16[128,1280]{1,0:T(8,128)(2,1)S(1)} %cut.8), channel_id=1, source_target_pairs={{0,3},{1,2},{2,1},{3,0},{4,7},{5,6},{6,5},{7,4},{8,11},{9,10},{10,... | collective-permute-start | bytes 983048 | tf_op jit(solution)/shard_map/ppermute | solution.py:33
  65.7 7.4 %collective-permute-start.25 = (f32[2,1024,128]{2,1,0:T(8,128)S(1)}, f32[2,1024,128]{2,1,0:T(8,128)S(1)}, u32[]{:S(2)}, u32[]{:S(2)}) collective-permute-start(f32[2,1024,128]{2,1,0:T(8,128)S(1)} %get-tuple-element.36), channel_id=1, source_target_pairs={{0,32},{1,33},{2,34},{3,35},{4,36},{5,37},{6,38},{7,39},{8,40},{9,... | collective-permute-start | bytes 3145736 | tf_op jit(solution)/shard_map/ppermute | solution.py:33
  72.8 24.2 %copy-start = (bf16[1024,1,2048]{2,0,1:T(8,128)(2,1)S(1)}, bf16[1024,1,2048]{2,0,1:T(8,128)(2,1)}, u32[]{:S(2)}) copy-start(bf16[1024,1,2048]{2,0,1:T(8,128)(2,1)} %param.9) | copy-start | bytes 12582916
  72.8 5.5 %collective-permute-start.21 = (f32[2,1024,128]{2,1,0:T(8,128)S(1)}, f32[2,1024,128]{2,1,0:T(8,128)S(1)}, u32[]{:S(2)}, u32[]{:S(2)}) collective-permute-start(f32[2,1024,128]{2,1,0:T(8,128)S(1)} %get-tuple-element.32), channel_id=1, source_target_pairs={{0,32},{1,33},{2,34},{3,35},{4,36},{5,37},{6,38},{7,39},{8,40},{9,... | collective-permute-start | bytes 3145736 | tf_op jit(solution)/shard_map/ppermute | solution.py:33
  75.0 7.5 %collective-permute-start.26 = (bf16[64,2048]{1,0:T(8,128)(2,1)S(1)}, bf16[64,2048]{1,0:T(8,128)(2,1)S(1)}, u32[]{:S(2)}, u32[]{:S(2)}) collective-permute-start(bf16[64,2048]{1,0:T(8,128)(2,1)S(1)} %get-tuple-element.38), channel_id=1, source_target_pairs={{0,4},{1,5},{2,6},{3,7},{4,0},{5,1},{6,2},{7,3},{8,12},{9,13},{10,... | collective-permute-start | bytes 786440 | tf_op jit(solution)/shard_map/ppermute | solution.py:33
  75.1 14.2 %collective-permute-start.28 = (bf16[64,2048]{1,0:T(8,128)(2,1)S(1)}, bf16[64,2048]{1,0:T(8,128)(2,1)S(1)}, u32[]{:S(2)}, u32[]{:S(2)}) collective-permute-start(bf16[64,2048]{1,0:T(8,128)(2,1)S(1)} %get-tuple-element.38), channel_id=1, source_target_pairs={{0,68},{1,69},{2,70},{3,71},{4,64},{5,65},{6,66},{7,67},{8,76},{9,... | collective-permute-start | bytes 786440 | tf_op jit(solution)/shard_map/ppermute | solution.py:33
  76.4 11.6 %collective-permute-start.27 = (bf16[64,2048]{1,0:T(8,128)(2,1)S(1)}, bf16[64,2048]{1,0:T(8,128)(2,1)S(1)}, u32[]{:S(2)}, u32[]{:S(2)}) collective-permute-start(bf16[64,2048]{1,0:T(8,128)(2,1)S(1)} %get-tuple-element.37.refs_0_), channel_id=1, source_target_pairs={{0,64},{1,65},{2,66},{3,67},{4,68},{5,69},{6,70},{7,71},{8,72},{9,... | collective-permute-start | bytes 786440 | tf_op jit(solution)/shard_map/ppermute | solution.py:33
  80.3 13.5 %collective-permute-start.22 = (bf16[64,2048]{1,0:T(8,128)(2,1)S(1)}, bf16[64,2048]{1,0:T(8,128)(2,1)S(1)}, u32[]{:S(2)}, u32[]{:S(2)}) collective-permute-start(bf16[64,2048]{1,0:T(8,128)(2,1)S(1)} %get-tuple-element.34), channel_id=1, source_target_pairs={{0,4},{1,5},{2,6},{3,7},{4,0},{5,1},{6,2},{7,3},{8,12},{9,13},{10,... | collective-permute-start | bytes 786440 | tf_op jit(solution)/shard_map/ppermute | solution.py:33
  80.4 14.5 %collective-permute-start.24 = (bf16[64,2048]{1,0:T(8,128)(2,1)S(1)}, bf16[64,2048]{1,0:T(8,128)(2,1)S(1)}, u32[]{:S(2)}, u32[]{:S(2)}) collective-permute-start(bf16[64,2048]{1,0:T(8,128)(2,1)S(1)} %get-tuple-element.34), channel_id=1, source_target_pairs={{0,68},{1,69},{2,70},{3,71},{4,64},{5,65},{6,66},{7,67},{8,76},{9,... | collective-permute-start | bytes 786440 | tf_op jit(solution)/shard_map/ppermute | solution.py:33
  95.0 3.7 %collective-permute-start.29 = (bf16[256,2048]{1,0:T(8,128)(2,1)S(1)}, bf16[256,2048]{1,0:T(8,128)(2,1)S(1)}, u32[]{:S(2)}, u32[]{:S(2)}) collective-permute-start(bf16[256,2048]{1,0:T(8,128)(2,1)S(1)} %stack.32.part.mine), channel_id=1, source_target_pairs={{0,32},{1,33},{2,34},{3,35},{4,36},{5,37},{6,38},{7,39},{8,40},{9,... | collective-permute-start | bytes 3145736 | tf_op jit(solution)/shard_map/ppermute | solution.py:33
  96.5 9.4 %collective-permute-start.23 = (bf16[64,2048]{1,0:T(8,128)(2,1)S(1)}, bf16[64,2048]{1,0:T(8,128)(2,1)S(1)}, u32[]{:S(2)}, u32[]{:S(2)}) collective-permute-start(bf16[64,2048]{1,0:T(8,128)(2,1)S(1)} %get-tuple-element.33.refs_0_), channel_id=1, source_target_pairs={{0,64},{1,65},{2,66},{3,67},{4,68},{5,69},{6,70},{7,71},{8,72},{9,... | collective-permute-start | bytes 786440 | tf_op jit(solution)/shard_map/ppermute | solution.py:33
  100.3 7.6 %collective-permute-start.30 = (bf16[256,512]{1,0:T(8,128)(2,1)S(1)}, bf16[256,512]{1,0:T(8,128)(2,1)S(1)}, u32[]{:S(2)}, u32[]{:S(2)}) collective-permute-start(bf16[256,512]{1,0:T(8,128)(2,1)S(1)} %get-tuple-element.42.refs_0_), channel_id=1, source_target_pairs={{0,1},{1,0},{2,3},{3,2},{4,5},{5,4},{6,7},{7,6},{8,9},{9,8},{10,11... | collective-permute-start | bytes 786440 | tf_op jit(solution)/shard_map/ppermute | solution.py:33
  101.2 8.4 %collective-permute-start.31 = (bf16[256,512]{1,0:T(8,128)(2,1)S(1)}, bf16[256,512]{1,0:T(8,128)(2,1)S(1)}, u32[]{:S(2)}, u32[]{:S(2)}) collective-permute-start(bf16[256,512]{1,0:T(8,128)(2,1)S(1)} %get-tuple-element.43), channel_id=1, source_target_pairs={{0,3},{1,2},{2,1},{3,0},{4,7},{5,6},{6,5},{7,4},{8,11},{9,10},{10,... | collective-permute-start | bytes 786440 | tf_op jit(solution)/shard_map/ppermute | solution.py:33
  109.6 5.1 %collective-permute-start.32 = (bf16[256,2048]{1,0:T(8,128)(2,1)S(1)}, bf16[256,2048]{1,0:T(8,128)(2,1)S(1)}, u32[]{:S(2)}, u32[]{:S(2)}) collective-permute-start(bf16[256,2048]{1,0:T(8,128)(2,1)S(1)} %stack.33.part.mine), channel_id=1, source_target_pairs={{0,32},{1,33},{2,34},{3,35},{4,36},{5,37},{6,38},{7,39},{8,40},{9,... | collective-permute-start | bytes 3145736 | tf_op jit(solution)/shard_map/ppermute | solution.py:33
  111.2 8.4 %copy-start.3 = (f32[1400]{0:T(1024)S(1)}, f32[1400]{0:T(1024)}, u32[]{:S(2)}) copy-start(f32[1400]{0:T(1024)} %virt.1) | copy-start | bytes 16804
  111.3 8.4 %copy-start.4 = (s32[256,2]{0,1:T(2,128)S(1)}, s32[256,2]{0,1:T(2,128)}, u32[]{:S(2)}) copy-start(s32[256,2]{0,1:T(2,128)} %param.10) | copy-start | bytes 6148
  111.3 8.4 %copy-start.5 = (s32[2]{0:T(128)S(1)}, s32[2]{0:T(128)}, u32[]{:S(2)}) copy-start(s32[2]{0:T(128)} %offsets.1) | copy-start | bytes 28
  111.3 8.4 %copy-start.6 = (f32[120]{0:T(128)S(1)}, f32[120]{0:T(128)}, u32[]{:S(2)}) copy-start(f32[120]{0:T(128)} %param.12) | copy-start | bytes 1444
  111.3 11.4 %collective-permute-start.36 = (bf16[256,512]{1,0:T(8,128)(2,1)S(1)}, bf16[256,512]{1,0:T(8,128)(2,1)S(1)}, u32[]{:S(2)}, u32[]{:S(2)}) collective-permute-start(bf16[256,512]{1,0:T(8,128)(2,1)S(1)} %get-tuple-element.52), channel_id=1, source_target_pairs={{0,2},{1,3},{2,0},{3,1},{4,6},{5,7},{6,4},{7,5},{8,10},{9,11},{10,... | collective-permute-start | bytes 786440 | tf_op jit(solution)/shard_map/ppermute | solution.py:33
  116.4 9.7 %collective-permute-start.33 = (bf16[256,512]{1,0:T(8,128)(2,1)S(1)}, bf16[256,512]{1,0:T(8,128)(2,1)S(1)}, u32[]{:S(2)}, u32[]{:S(2)}) collective-permute-start(bf16[256,512]{1,0:T(8,128)(2,1)S(1)} %get-tuple-element.47.refs_0_), channel_id=1, source_target_pairs={{0,1},{1,0},{2,3},{3,2},{4,5},{5,4},{6,7},{7,6},{8,9},{9,8},{10,11... | collective-permute-start | bytes 786440 | tf_op jit(solution)/shard_map/ppermute | solution.py:33
  117.2 9.0 %collective-permute-start.34 = (bf16[256,512]{1,0:T(8,128)(2,1)S(1)}, bf16[256,512]{1,0:T(8,128)(2,1)S(1)}, u32[]{:S(2)}, u32[]{:S(2)}) collective-permute-start(bf16[256,512]{1,0:T(8,128)(2,1)S(1)} %get-tuple-element.48), channel_id=1, source_target_pairs={{0,3},{1,2},{2,1},{3,0},{4,7},{5,6},{6,5},{7,4},{8,11},{9,10},{10,... | collective-permute-start | bytes 786440 | tf_op jit(solution)/shard_map/ppermute | solution.py:33
  117.8 14.2 %collective-permute-start.35 = (bf16[256,512]{1,0:T(8,128)(2,1)S(1)}, bf16[256,512]{1,0:T(8,128)(2,1)S(1)}, u32[]{:S(2)}, u32[]{:S(2)}) collective-permute-start(bf16[256,512]{1,0:T(8,128)(2,1)S(1)} %get-tuple-element.49), channel_id=1, source_target_pairs={{0,2},{1,3},{2,0},{3,1},{4,6},{5,7},{6,4},{7,5},{8,10},{9,11},{10,... | collective-permute-start | bytes 786440 | tf_op jit(solution)/shard_map/ppermute | solution.py:33

commit v5 on v4

--- a/solution.py
+++ b/solution.py
@@ -283,7 +283,7 @@
     mine = stack([mine], r0)
     far4 = [far] + [swap(far, z=s) for s in (1, 2, 3)]
     mine4 = [mine] + [swap(mine, y=s) for s in (1, 2, 3)]
-    r0 += cut(right, [np.s_[:, 256:]], (mine4[3], far4[1]))
+    r0 += cut(right, [np.s_[:, 256:]], (mine4[1], mine4[3], far4[1], far4[3]))
     r1, r3 = [swap(v, xl=1) for v in r0], [swap(v, xl=1, xh=1) for v in r0]
 
     la = stack(mine4, (*far4[1:], r1[0], r3[0]))

time: 134 us -> 133 us (level)
  waiting for transfers between devices: 49.6 us -> 46.3 us
  starting transfers between devices: 54.3 us -> 57.1 us
    ppermute x37, waiting for transfers between devices: 49.6 us -> 46.3 us  [swap(): return lax.ppermute(x, AXES, swap_table(**by))]
    ppermute x37, starting transfers between devices: 54.3 us -> 57.1 us  [swap(): return lax.ppermute(x, AXES, swap_table(**by))]
  transfers between devices with their start and end apart: 37 -> 37, of which waited for: 20 -> 18; matrix products, arithmetic and copies ran while one was open for 0% -> 0% of each run, Pallas kernels for 15% -> 15%
where the time goes in v5:
time: 133 us
  starting transfers between devices  57.1 us (43%)
  waiting for transfers between devices  46.3 us (35%)
  Pallas kernels  25.5 us (19%)
  local copies, waits for them, and re-layouts  3.72 us (3%)
    ppermute x37, starting transfers between devices, swap(): return lax.ppermute(x, AXES, swap_table(**by))  57.1 us
    ppermute x37, waiting for transfers between devices, swap(): return lax.ppermute(x, AXES, swap_table(**by))  46.3 us
    pallas_call x27, Pallas kernels, call(): pl.pallas_call(body, out_shape=[jax.ShapeDtypeStruct(*v) for v in shapes]...  25.5 us
  transfers between devices with their start and end apart: 37, of which 18 were waited for; matrix products, arithmetic and copies ran while one was open for 0% of the time, Pallas kernels for 15%

profile of v5, /device:TPU:1, one launch (start us, length us, event | category | flops | bytes accessed | tf_op | source)
XLA Modules:
  0.0 133.0 jit_solution(813688441685864621)
XLA Ops:
  1.8 3.7 %collective-permute-start.3 = (bf16[64,1280]{1,0:T(8,128)(2,1)S(1)}, bf16[64,1280]{1,0:T(8,128)(2,1)S(1)}, u32[]{:S(2)}, u32[]{:S(2)}) collective-permute-start(bf16[64,1280]{1,0:T(8,128)(2,1)S(1)} %get-tuple-element.30.refs_0_), channel_id=1, source_target_pairs={{0,64},{1,65},{2,66},{3,67},{4,68},{5,69},{6,70},{7,71},{8,72},{9,... | collective-permute-start | bytes 491528 | tf_op jit(solution)/shard_map/ppermute | solution.py:33
  5.4 1.3 copy-done.1
  6.8 1.4 %collective-permute-start = (bf16[64,1280]{1,0:T(8,128)(2,1)S(1)}, bf16[64,1280]{1,0:T(8,128)(2,1)S(1)}, u32[]{:S(2)}, u32[]{:S(2)}) collective-permute-start(bf16[64,1280]{1,0:T(8,128)(2,1)S(1)} %stack.29.refs_0_), channel_id=1, source_target_pairs={{0,8},{1,9},{2,10},{3,11},{4,12},{5,13},{6,14},{7,15},{8,0},{9,1},... | collective-permute-start | bytes 491528 | tf_op jit(solution)/shard_map/ppermute | solution.py:33
  9.0 1.9 %collective-permute-start.2 = (bf16[64,1280]{1,0:T(8,128)(2,1)S(1)}, bf16[64,1280]{1,0:T(8,128)(2,1)S(1)}, u32[]{:S(2)}, u32[]{:S(2)}) collective-permute-start(bf16[64,1280]{1,0:T(8,128)(2,1)S(1)} %stack.29.refs_0_), channel_id=1, source_target_pairs={{0,24},{1,25},{2,26},{3,27},{4,28},{5,29},{6,30},{7,31},{8,16},{9,... | collective-permute-start | bytes 491528 | tf_op jit(solution)/shard_map/ppermute | solution.py:33
  10.9 1.6 %collective-permute-start.4 = (bf16[64,1280]{1,0:T(8,128)(2,1)S(1)}, bf16[64,1280]{1,0:T(8,128)(2,1)S(1)}, u32[]{:S(2)}, u32[]{:S(2)}) collective-permute-start(bf16[64,1280]{1,0:T(8,128)(2,1)S(1)} %collective-permute-done.3.refs_0_), channel_id=1, source_target_pairs={{0,1},{1,0},{2,3},{3,2},{4,5},{5,4},{6,7},{7,6},{8,9},{9,8},{10,11... | collective-permute-start | bytes 491528 | tf_op jit(solution)/shard_map/ppermute | solution.py:33
  12.6 2.8 %collective-permute-start.6 = (bf16[64,1280]{1,0:T(8,128)(2,1)S(1)}, bf16[64,1280]{1,0:T(8,128)(2,1)S(1)}, u32[]{:S(2)}, u32[]{:S(2)}) collective-permute-start(bf16[64,1280]{1,0:T(8,128)(2,1)S(1)} %collective-permute-done.3.refs_0_), channel_id=1, source_target_pairs={{0,3},{1,2},{2,1},{3,0},{4,7},{5,6},{6,5},{7,4},{8,11},{9,10},{10,... | collective-permute-start | bytes 491528 | tf_op jit(solution)/shard_map/ppermute | solution.py:33
  15.4 2.9 %collective-permute-start.1 = (bf16[64,1280]{1,0:T(8,128)(2,1)S(1)}, bf16[64,1280]{1,0:T(8,128)(2,1)S(1)}, u32[]{:S(2)}, u32[]{:S(2)}) collective-permute-start(bf16[64,1280]{1,0:T(8,128)(2,1)S(1)} %stack.29.refs_0_), channel_id=1, source_target_pairs={{0,16},{1,17},{2,18},{3,19},{4,20},{5,21},{6,22},{7,23},{8,24},{9,... | collective-permute-start | bytes 491528 | tf_op jit(solution)/shard_map/ppermute | solution.py:33
  18.4 1.3 copy-done.2
  20.3 1.8 %collective-permute-start.12 = (bf16[1250,256]{1,0:T(8,128)(2,1)S(1)}, bf16[1250,256]{1,0:T(8,128)(2,1)S(1)}, u32[]{:S(2)}, u32[]{:S(2)}) collective-permute-start(bf16[1250,256]{1,0:T(8,128)(2,1)S(1)} %cut.7.refs_10_), channel_id=1, source_target_pairs={{0,68},{1,69},{2,70},{3,71},{4,64},{5,65},{6,66},{7,67},{8,76},{9,... | collective-permute-start | bytes 1920008 | tf_op jit(solution)/shard_map/ppermute | solution.py:33
  22.1 2.4 %collective-permute-start.5 = (bf16[64,1280]{1,0:T(8,128)(2,1)S(1)}, bf16[64,1280]{1,0:T(8,128)(2,1)S(1)}, u32[]{:S(2)}, u32[]{:S(2)}) collective-permute-start(bf16[64,1280]{1,0:T(8,128)(2,1)S(1)} %collective-permute-done.3.refs_0_), channel_id=1, source_target_pairs={{0,2},{1,3},{2,0},{3,1},{4,6},{5,7},{6,4},{7,5},{8,10},{9,11},{10,... | collective-permute-start | bytes 491528 | tf_op jit(solution)/shard_map/ppermute | solution.py:33
  24.5 3.3 %collective-permute-done.5.refs_5_.refs_2_ = bf16[64,1280]{1,0:T(8,128)(2,1)S(1)} collective-permute-done((bf16[64,1280]{1,0:T(8,128)(2,1)S(1)}, bf16[64,1280]{1,0:T(8,128)(2,1)S(1)}, u32[]{:S(2)}, u32[]{:S(2)}) %collective-permute-start.5) | collective-permute-done | bytes 163872 | tf_op jit(solution)/shard_map/ppermute | solution.py:33
  27.8 1.8 %collective-permute-start.16 = (bf16[256,1280]{1,0:T(8,128)(2,1)S(1)}, bf16[256,1280]{1,0:T(8,128)(2,1)S(1)}, u32[]{:S(2)}, u32[]{:S(2)}) collective-permute-start(bf16[256,1280]{1,0:T(8,128)(2,1)S(1)} %stack.31.refs_5_), channel_id=1, source_target_pairs={{0,24},{1,25},{2,26},{3,27},{4,28},{5,29},{6,30},{7,31},{8,16},{9,... | collective-permute-start | bytes 1966088 | tf_op jit(solution)/shard_map/ppermute | solution.py:33
  29.8 2.3 %collective-permute-start.10 = (bf16[256,1280]{1,0:T(8,128)(2,1)S(1)}, bf16[256,1280]{1,0:T(8,128)(2,1)S(1)}, u32[]{:S(2)}, u32[]{:S(2)}) collective-permute-start(bf16[256,1280]{1,0:T(8,128)(2,1)S(1)} %stack.30.refs_0_), channel_id=1, source_target_pairs={{0,3},{1,2},{2,1},{3,0},{4,7},{5,6},{6,5},{7,4},{8,11},{9,10},{10,... | collective-permute-start | bytes 1966088 | tf_op jit(solution)/shard_map/ppermute | solution.py:33
  32.1 4.6 %collective-permute-done.11.refs_0_.refs_1_.refs_11_ = bf16[1250,256]{1,0:T(8,128)(2,1)S(1)} collective-permute-done((bf16[1250,256]{1,0:T(8,128)(2,1)S(1)}, bf16[1250,256]{1,0:T(8,128)(2,1)S(1)}, u32[]{:S(2)}, u32[]{:S(2)}) %collective-permute-start.11) | collective-permute-done | bytes 640032 | tf_op jit(solution)/shard_map/ppermute | solution.py:33
  36.7 1.6 %collective-permute-start.9 = (bf16[256,1280]{1,0:T(8,128)(2,1)S(1)}, bf16[256,1280]{1,0:T(8,128)(2,1)S(1)}, u32[]{:S(2)}, u32[]{:S(2)}) collective-permute-start(bf16[256,1280]{1,0:T(8,128)(2,1)S(1)} %stack.30.refs_0_), channel_id=1, source_target_pairs={{0,1},{1,0},{2,3},{3,2},{4,5},{5,4},{6,7},{7,6},{8,9},{9,8},{10,11... | collective-permute-start | bytes 1966088 | tf_op jit(solution)/shard_map/ppermute | solution.py:33
  41.8 2.1 %collective-permute-start.17 = (bf16[128,1280]{1,0:T(8,128)(2,1)S(1)}, bf16[128,1280]{1,0:T(8,128)(2,1)S(1)}, u32[]{:S(2)}, u32[]{:S(2)}) collective-permute-start(bf16[128,1280]{1,0:T(8,128)(2,1)S(1)} %cut.10), channel_id=1, source_target_pairs={{0,24},{1,25},{2,26},{3,27},{4,28},{5,29},{6,30},{7,31},{8,16},{9,... | collective-permute-start | bytes 983048 | tf_op jit(solution)/shard_map/ppermute | solution.py:33
  43.9 7.2 %collective-permute-done.9.source.refs_1_ = bf16[256,1280]{1,0:T(8,128)(2,1)S(1)} collective-permute-done((bf16[256,1280]{1,0:T(8,128)(2,1)S(1)}, bf16[256,1280]{1,0:T(8,128)(2,1)S(1)}, u32[]{:S(2)}, u32[]{:S(2)}) %collective-permute-start.9) | collective-permute-done | bytes 655392 | tf_op jit(solution)/shard_map/ppermute | solution.py:33
  51.1 1.3 collective-permute-start.14
  53.2 3.2 %collective-permute-start.13 = (bf16[128,1280]{1,0:T(8,128)(2,1)S(1)}, bf16[128,1280]{1,0:T(8,128)(2,1)S(1)}, u32[]{:S(2)}, u32[]{:S(2)}) collective-permute-start(bf16[128,1280]{1,0:T(8,128)(2,1)S(1)} %cut.8), channel_id=1, source_target_pairs={{0,3},{1,2},{2,1},{3,0},{4,7},{5,6},{6,5},{7,4},{8,11},{9,10},{10,... | collective-permute-start | bytes 983048 | tf_op jit(solution)/shard_map/ppermute | solution.py:33
  57.4 3.5 %collective-permute-done.13.refs_3_ = bf16[128,1280]{1,0:T(8,128)(2,1)S(1)} collective-permute-done((bf16[128,1280]{1,0:T(8,128)(2,1)S(1)}, bf16[128,1280]{1,0:T(8,128)(2,1)S(1)}, u32[]{:S(2)}, u32[]{:S(2)}) %collective-permute-start.13) | collective-permute-done | bytes 327712 | tf_op jit(solution)/shard_map/ppermute | solution.py:33
  60.9 3.6 %tile.3 = (f32[2,1024,128]{2,1,0:T(8,128)S(1)}, f32[2,1024,128]{2,1,0:T(8,128)S(1)}) custom-call(s32[5]{0:T(128)S(1)} %stack.28.at, bf16[256,1280]{1,0:T(8,128)(2,1)S(1)} %stack.30.refs_0_, bf16[256,1280]{1,0:T(8,128)(2,1)S(1)} %collective-permute-done.9.source.refs_1_, bf16[256,1280]{1,0:T(8,128)(2,1)S(1)} %collective-permute-done.10.source.refs_2_, ...), custom_call_target="tpu_custom_call" | custom-call | flops 2621440000 | bytes 10485760 | tf_op jit(solution)/shard_map/tile/pallas_call | solution.py:43
  64.5 4.3 %collective-permute-start.25 = (f32[2,1024,128]{2,1,0:T(8,128)S(1)}, f32[2,1024,128]{2,1,0:T(8,128)S(1)}, u32[]{:S(2)}, u32[]{:S(2)}) collective-permute-start(f32[2,1024,128]{2,1,0:T(8,128)S(1)} %get-tuple-element.36), channel_id=1, source_target_pairs={{0,32},{1,33},{2,34},{3,35},{4,36},{5,37},{6,38},{7,39},{8,40},{9,... | collective-permute-start | bytes 3145736 | tf_op jit(solution)/shard_map/ppermute | solution.py:33
  68.8 3.6 %tile.2 = (f32[2,1024,128]{2,1,0:T(8,128)S(1)}, f32[2,1024,128]{2,1,0:T(8,128)S(1)}) custom-call(s32[5]{0:T(128)S(1)} %stack.28.at, bf16[256,1280]{1,0:T(8,128)(2,1)S(1)} %stack.30.refs_0_, bf16[256,1280]{1,0:T(8,128)(2,1)S(1)} %collective-permute-done.9.source.refs_1_, bf16[256,1280]{1,0:T(8,128)(2,1)S(1)} %collective-permute-done.10.source.refs_2_, ...), custom_call_target="tpu_custom_call" | custom-call | flops 2621440000 | bytes 10485760 | tf_op jit(solution)/shard_map/tile/pallas_call | solution.py:43
  72.7 1.9 %turn.3 = (bf16[64,2048]{1,0:T(8,128)(2,1)S(1)}, bf16[64,2048]{1,0:T(8,128)(2,1)S(1)}) custom-call(f32[2,1024,128]{2,1,0:T(8,128)S(1)} %get-tuple-element.35.keep, f32[2,1024,128]{2,1,0:T(8,128)S(1)} %collective-permute-done.25.got), custom_call_target="tpu_custom_call" | custom-call | bytes 3145728 | tf_op jit(solution)/shard_map/turn/pallas_call | solution.py:43
  75.0 1.6 %collective-permute-start.28 = (bf16[64,2048]{1,0:T(8,128)(2,1)S(1)}, bf16[64,2048]{1,0:T(8,128)(2,1)S(1)}, u32[]{:S(2)}, u32[]{:S(2)}) collective-permute-start(bf16[64,2048]{1,0:T(8,128)(2,1)S(1)} %get-tuple-element.38), channel_id=1, source_target_pairs={{0,68},{1,69},{2,70},{3,71},{4,64},{5,65},{6,66},{7,67},{8,76},{9,... | collective-permute-start | bytes 786440 | tf_op jit(solution)/shard_map/ppermute | solution.py:33
  76.7 1.2 collective-permute-start.27
  77.9 1.9 %turn.2 = (bf16[64,2048]{1,0:T(8,128)(2,1)S(1)}, bf16[64,2048]{1,0:T(8,128)(2,1)S(1)}) custom-call(f32[2,1024,128]{2,1,0:T(8,128)S(1)} %get-tuple-element.31.keep, f32[2,1024,128]{2,1,0:T(8,128)S(1)} %collective-permute-done.21.got), custom_call_target="tpu_custom_call" | custom-call | bytes 3145728 | tf_op jit(solution)/shard_map/turn/pallas_call | solution.py:43
  80.3 1.6 %collective-permute-start.24 = (bf16[64,2048]{1,0:T(8,128)(2,1)S(1)}, bf16[64,2048]{1,0:T(8,128)(2,1)S(1)}, u32[]{:S(2)}, u32[]{:S(2)}) collective-permute-start(bf16[64,2048]{1,0:T(8,128)(2,1)S(1)} %get-tuple-element.34), channel_id=1, source_target_pairs={{0,68},{1,69},{2,70},{3,71},{4,64},{5,65},{6,66},{7,67},{8,76},{9,... | collective-permute-start | bytes 786440 | tf_op jit(solution)/shard_map/ppermute | solution.py:33
  82.0 6.0 %collective-permute-done.27.refs_2_ = bf16[64,2048]{1,0:T(8,128)(2,1)S(1)} collective-permute-done((bf16[64,2048]{1,0:T(8,128)(2,1)S(1)}, bf16[64,2048]{1,0:T(8,128)(2,1)S(1)}, u32[]{:S(2)}, u32[]{:S(2)}) %collective-permute-start.27) | collective-permute-done | bytes 262176 | tf_op jit(solution)/shard_map/ppermute | solution.py:33
  88.1 5.3 %collective-permute-done.22.refs_4_.refs_1_ = bf16[64,2048]{1,0:T(8,128)(2,1)S(1)} collective-permute-done((bf16[64,2048]{1,0:T(8,128)(2,1)S(1)}, bf16[64,2048]{1,0:T(8,128)(2,1)S(1)}, u32[]{:S(2)}, u32[]{:S(2)}) %collective-permute-start.22) | collective-permute-done | bytes 262176 | tf_op jit(solution)/shard_map/ppermute | solution.py:33
  93.3 1.2 collective-permute-done.24.refs_5_.refs_3_
  94.6 1.7 %collective-permute-start.29 = (bf16[256,2048]{1,0:T(8,128)(2,1)S(1)}, bf16[256,2048]{1,0:T(8,128)(2,1)S(1)}, u32[]{:S(2)}, u32[]{:S(2)}) collective-permute-start(bf16[256,2048]{1,0:T(8,128)(2,1)S(1)} %stack.32.part.mine), channel_id=1, source_target_pairs={{0,32},{1,33},{2,34},{3,35},{4,36},{5,37},{6,38},{7,39},{8,40},{9,... | collective-permute-start | bytes 3145736 | tf_op jit(solution)/shard_map/ppermute | solution.py:33
  96.6 1.6 %ladder.4 = (bf16[256,256]{1,0:T(8,128)(2,1)S(1)}, bf16[256,256]{1,0:T(8,128)(2,1)S(1)}, bf16[256,256]{1,0:T(8,128)(2,1)S(1)}) custom-call(s32[5]{0:T(128)S(1)} %stack.28.at, bf16[1024,2048]{1,0:T(8,128)(2,1)S(1)} %bitcast.9, bf16[256,2048]{1,0:T(8,128)(2,1)S(1)} %stack.32.part.mine), custom_call_target="tpu_custom_call" | custom-call | flops 805306368 | bytes 4194304 | tf_op jit(solution)/shard_map/ladder/pallas_call | solution.py:43
  98.6 1.5 %ladder.5 = (bf16[256,512]{1,0:T(8,128)(2,1)S(1)}, bf16[256,512]{1,0:T(8,128)(2,1)S(1)}, bf16[256,512]{1,0:T(8,128)(2,1)S(1)}) custom-call(s32[5]{0:T(128)S(1)} %stack.28.at, bf16[1024,2048]{1,0:T(8,128)(2,1)S(1)} %bitcast.10, bf16[256,2048]{1,0:T(8,128)(2,1)S(1)} %collective-permute-done.29.part.peer, bf16[256,256]{1,0:T(8,128)(2,1)S(1)} %get-tuple-element.39.refs_0_, ...), custom_call_target="tpu_custom_call" | custom-call | flops 805306368 | bytes 4194304 | tf_op jit(solution)/shard_map/ladder/pallas_call | solution.py:43
  100.6 2.4 %collective-permute-start.31 = (bf16[256,512]{1,0:T(8,128)(2,1)S(1)}, bf16[256,512]{1,0:T(8,128)(2,1)S(1)}, u32[]{:S(2)}, u32[]{:S(2)}) collective-permute-start(bf16[256,512]{1,0:T(8,128)(2,1)S(1)} %get-tuple-element.43), channel_id=1, source_target_pairs={{0,3},{1,2},{2,1},{3,0},{4,7},{5,6},{6,5},{7,4},{8,11},{9,10},{10,... | collective-permute-start | bytes 786440 | tf_op jit(solution)/shard_map/ppermute | solution.py:33
  103.0 2.7 %collective-permute-done.23.refs_2_ = bf16[64,2048]{1,0:T(8,128)(2,1)S(1)} collective-permute-done((bf16[64,2048]{1,0:T(8,128)(2,1)S(1)}, bf16[64,2048]{1,0:T(8,128)(2,1)S(1)}, u32[]{:S(2)}, u32[]{:S(2)}) %collective-permute-start.23) | collective-permute-done | bytes 262176 | tf_op jit(solution)/shard_map/ppermute | solution.py:33
  105.7 2.1 %collective-permute-done.30.refs_4_.r1 = bf16[256,512]{1,0:T(8,128)(2,1)S(1)} collective-permute-done((bf16[256,512]{1,0:T(8,128)(2,1)S(1)}, bf16[256,512]{1,0:T(8,128)(2,1)S(1)}, u32[]{:S(2)}, u32[]{:S(2)}) %collective-permute-start.30) | collective-permute-done | bytes 262176 | tf_op jit(solution)/shard_map/ppermute | solution.py:33
  109.1 1.6 %collective-permute-start.32 = (bf16[256,2048]{1,0:T(8,128)(2,1)S(1)}, bf16[256,2048]{1,0:T(8,128)(2,1)S(1)}, u32[]{:S(2)}, u32[]{:S(2)}) collective-permute-start(bf16[256,2048]{1,0:T(8,128)(2,1)S(1)} %stack.33.part.mine), channel_id=1, source_target_pairs={{0,32},{1,33},{2,34},{3,35},{4,36},{5,37},{6,38},{7,39},{8,40},{9,... | collective-permute-start | bytes 3145736 | tf_op jit(solution)/shard_map/ppermute | solution.py:33
  110.7 2.4 %collective-permute-start.36 = (bf16[256,512]{1,0:T(8,128)(2,1)S(1)}, bf16[256,512]{1,0:T(8,128)(2,1)S(1)}, u32[]{:S(2)}, u32[]{:S(2)}) collective-permute-start(bf16[256,512]{1,0:T(8,128)(2,1)S(1)} %get-tuple-element.52), channel_id=1, source_target_pairs={{0,2},{1,3},{2,0},{3,1},{4,6},{5,7},{6,4},{7,5},{8,10},{9,11},{10,... | collective-permute-start | bytes 786440 | tf_op jit(solution)/shard_map/ppermute | solution.py:33
  113.1 1.5 %ladder.6 = (bf16[256,256]{1,0:T(8,128)(2,1)S(1)}, bf16[256,256]{1,0:T(8,128)(2,1)S(1)}, bf16[256,256]{1,0:T(8,128)(2,1)S(1)}) custom-call(s32[5]{0:T(128)S(1)} %stack.28.at, bf16[1024,2048]{1,0:T(8,128)(2,1)S(1)} %bitcast.11, bf16[256,2048]{1,0:T(8,128)(2,1)S(1)} %stack.33.part.mine), custom_call_target="tpu_custom_call" | custom-call | flops 805306368 | bytes 4194304 | tf_op jit(solution)/shard_map/ladder/pallas_call | solution.py:43
  114.7 1.5 %ladder.7 = (bf16[256,512]{1,0:T(8,128)(2,1)S(1)}, bf16[256,512]{1,0:T(8,128)(2,1)S(1)}, bf16[256,512]{1,0:T(8,128)(2,1)S(1)}) custom-call(s32[5]{0:T(128)S(1)} %stack.28.at, bf16[1024,2048]{1,0:T(8,128)(2,1)S(1)} %bitcast.12, bf16[256,2048]{1,0:T(8,128)(2,1)S(1)} %collective-permute-done.32.part.peer, bf16[256,256]{1,0:T(8,128)(2,1)S(1)} %get-tuple-element.44.refs_0_, ...), custom_call_target="tpu_custom_call" | custom-call | flops 805306368 | bytes 4194304 | tf_op jit(solution)/shard_map/ladder/pallas_call | solution.py:43
  117.2 2.3 %collective-permute-start.35 = (bf16[256,512]{1,0:T(8,128)(2,1)S(1)}, bf16[256,512]{1,0:T(8,128)(2,1)S(1)}, u32[]{:S(2)}, u32[]{:S(2)}) collective-permute-start(bf16[256,512]{1,0:T(8,128)(2,1)S(1)} %get-tuple-element.49), channel_id=1, source_target_pairs={{0,2},{1,3},{2,0},{3,1},{4,6},{5,7},{6,4},{7,5},{8,10},{9,11},{10,... | collective-permute-start | bytes 786440 | tf_op jit(solution)/shard_map/ppermute | solution.py:33
  119.6 1.6 %prepare.1 = (bf16[512,512]{1,0:T(8,128)(2,1)S(1)}, f32[256,1024]{1,0:T(8,128)S(1)}) custom-call(s32[5]{0:T(128)S(1)} %stack.28.at, s32[2]{0:T(128)S(1)} %copy-done.5, f32[1400]{0:T(1024)S(1)} %copy-done.3, s32[2,256]{1,0:T(2,128)S(1)} %bitcast.17, f32[1,120]{1,0:T(1,128)S(1)} %bitcast.18), custom_call_target="tpu_custom_call" | custom-call | bytes 1048576 | tf_op jit(solution)/shard_map/prepare/pallas_call | solution.py:43
  121.2 1.3 own.3
  122.5 1.4 %finish.2.refs_0_ = f32[256,1024]{1,0:T(8,128)} custom-call(f32[256,512]{1,0:T(8,128)S(1)} %own.3, bf16[256,512]{1,0:T(8,128)(2,1)S(1)} %collective-permute-done.30.refs_4_.r1, bf16[256,512]{1,0:T(8,128)(2,1)S(1)} %collective-permute-done.31.refs_5_.r2, bf16[256,512]{1,0:T(8,128)(2,1)S(1)} %collective-permute-done.36.r3, ...), custom_call_target="tpu_custom_call" | custom-call | flops 402653184 | bytes 4194304 | tf_op jit(solution)/shard_map/finish/pallas_call | solution.py:43
  123.9 1.3 own.2
  125.8 5.6 %collective-permute-done.35.r3 = bf16[256,512]{1,0:T(8,128)(2,1)S(1)} collective-permute-done((bf16[256,512]{1,0:T(8,128)(2,1)S(1)}, bf16[256,512]{1,0:T(8,128)(2,1)S(1)}, u32[]{:S(2)}, u32[]{:S(2)}) %collective-permute-start.35) | collective-permute-done | bytes 262176 | tf_op jit(solution)/shard_map/ppermute | solution.py:33
  131.4 1.4 %finish.3 = f32[256,1024]{1,0:T(8,128)} custom-call(f32[256,512]{1,0:T(8,128)S(1)} %own.2, bf16[256,512]{1,0:T(8,128)(2,1)S(1)} %collective-permute-done.33.r1, bf16[256,512]{1,0:T(8,128)(2,1)S(1)} %collective-permute-done.34.r2, bf16[256,512]{1,0:T(8,128)(2,1)S(1)} %collective-permute-done.35.r3, ...), custom_call_target="tpu_custom_call", output_to_operand_aliasing={{}: (6, {})} | custom-call | flops 402653184 | bytes 4194304 | tf_op jit(solution)/shard_map/finish/pallas_call | solution.py:43
  (69 shorter events, 14.2 us)
Async XLA Ops:
  1.8 9.2 %collective-permute-start.3 = (bf16[64,1280]{1,0:T(8,128)(2,1)S(1)}, bf16[64,1280]{1,0:T(8,128)(2,1)S(1)}, u32[]{:S(2)}, u32[]{:S(2)}) collective-permute-start(bf16[64,1280]{1,0:T(8,128)(2,1)S(1)} %get-tuple-element.30.refs_0_), channel_id=1, source_target_pairs={{0,64},{1,65},{2,66},{3,67},{4,68},{5,69},{6,70},{7,71},{8,72},{9,... | collective-permute-start | bytes 491528 | tf_op jit(solution)/shard_map/ppermute | solution.py:33
  5.4 1.3 copy-start.1
  6.8 5.8 %collective-permute-start = (bf16[64,1280]{1,0:T(8,128)(2,1)S(1)}, bf16[64,1280]{1,0:T(8,128)(2,1)S(1)}, u32[]{:S(2)}, u32[]{:S(2)}) collective-permute-start(bf16[64,1280]{1,0:T(8,128)(2,1)S(1)} %stack.29.refs_0_), channel_id=1, source_target_pairs={{0,8},{1,9},{2,10},{3,11},{4,12},{5,13},{6,14},{7,15},{8,0},{9,1},... | collective-permute-start | bytes 491528 | tf_op jit(solution)/shard_map/ppermute | solution.py:33
  8.2 19.6 %collective-permute-start.7 = (bf16[1250,256]{1,0:T(8,128)(2,1)S(1)}, bf16[1250,256]{1,0:T(8,128)(2,1)S(1)}, u32[]{:S(2)}, u32[]{:S(2)}) collective-permute-start(bf16[1250,256]{1,0:T(8,128)(2,1)S(1)} %cut.6.refs_1_.refs_10_), channel_id=1, source_target_pairs={{0,4},{1,5},{2,6},{3,7},{4,0},{5,1},{6,2},{7,3},{8,12},{9,13},{10,... | collective-permute-start | bytes 1920008 | tf_op jit(solution)/shard_map/ppermute | solution.py:33
  8.5 19.3 %collective-permute-start.8 = (bf16[1250,256]{1,0:T(8,128)(2,1)S(1)}, bf16[1250,256]{1,0:T(8,128)(2,1)S(1)}, u32[]{:S(2)}, u32[]{:S(2)}) collective-permute-start(bf16[1250,256]{1,0:T(8,128)(2,1)S(1)} %cut.6.refs_1_.refs_10_), channel_id=1, source_target_pairs={{0,68},{1,69},{2,70},{3,71},{4,64},{5,65},{6,66},{7,67},{8,76},{9,... | collective-permute-start | bytes 1920008 | tf_op jit(solution)/shard_map/ppermute | solution.py:33
  9.0 6.3 %collective-permute-start.2 = (bf16[64,1280]{1,0:T(8,128)(2,1)S(1)}, bf16[64,1280]{1,0:T(8,128)(2,1)S(1)}, u32[]{:S(2)}, u32[]{:S(2)}) collective-permute-start(bf16[64,1280]{1,0:T(8,128)(2,1)S(1)} %stack.29.refs_0_), channel_id=1, source_target_pairs={{0,24},{1,25},{2,26},{3,27},{4,28},{5,29},{6,30},{7,31},{8,16},{9,... | collective-permute-start | bytes 491528 | tf_op jit(solution)/shard_map/ppermute | solution.py:33
  10.9 7.4 %collective-permute-start.4 = (bf16[64,1280]{1,0:T(8,128)(2,1)S(1)}, bf16[64,1280]{1,0:T(8,128)(2,1)S(1)}, u32[]{:S(2)}, u32[]{:S(2)}) collective-permute-start(bf16[64,1280]{1,0:T(8,128)(2,1)S(1)} %collective-permute-done.3.refs_0_), channel_id=1, source_target_pairs={{0,1},{1,0},{2,3},{3,2},{4,5},{5,4},{6,7},{7,6},{8,9},{9,8},{10,11... | collective-permute-start | bytes 491528 | tf_op jit(solution)/shard_map/ppermute | solution.py:33
  12.6 5.8 %collective-permute-start.6 = (bf16[64,1280]{1,0:T(8,128)(2,1)S(1)}, bf16[64,1280]{1,0:T(8,128)(2,1)S(1)}, u32[]{:S(2)}, u32[]{:S(2)}) collective-permute-start(bf16[64,1280]{1,0:T(8,128)(2,1)S(1)} %collective-permute-done.3.refs_0_), channel_id=1, source_target_pairs={{0,3},{1,2},{2,1},{3,0},{4,7},{5,6},{6,5},{7,4},{8,11},{9,10},{10,... | collective-permute-start | bytes 491528 | tf_op jit(solution)/shard_map/ppermute | solution.py:33
  15.4 6.7 %collective-permute-start.1 = (bf16[64,1280]{1,0:T(8,128)(2,1)S(1)}, bf16[64,1280]{1,0:T(8,128)(2,1)S(1)}, u32[]{:S(2)}, u32[]{:S(2)}) collective-permute-start(bf16[64,1280]{1,0:T(8,128)(2,1)S(1)} %stack.29.refs_0_), channel_id=1, source_target_pairs={{0,16},{1,17},{2,18},{3,19},{4,20},{5,21},{6,22},{7,23},{8,24},{9,... | collective-permute-start | bytes 491528 | tf_op jit(solution)/shard_map/ppermute | solution.py:33
  18.4 1.3 copy-start.2
  19.7 16.9 %collective-permute-start.11 = (bf16[1250,256]{1,0:T(8,128)(2,1)S(1)}, bf16[1250,256]{1,0:T(8,128)(2,1)S(1)}, u32[]{:S(2)}, u32[]{:S(2)}) collective-permute-start(bf16[1250,256]{1,0:T(8,128)(2,1)S(1)} %cut.7.refs_10_), channel_id=1, source_target_pairs={{0,4},{1,5},{2,6},{3,7},{4,0},{5,1},{6,2},{7,3},{8,12},{9,13},{10,... | collective-permute-start | bytes 1920008 | tf_op jit(solution)/shard_map/ppermute | solution.py:33
  20.3 18.2 %collective-permute-start.12 = (bf16[1250,256]{1,0:T(8,128)(2,1)S(1)}, bf16[1250,256]{1,0:T(8,128)(2,1)S(1)}, u32[]{:S(2)}, u32[]{:S(2)}) collective-permute-start(bf16[1250,256]{1,0:T(8,128)(2,1)S(1)} %cut.7.refs_10_), channel_id=1, source_target_pairs={{0,68},{1,69},{2,70},{3,71},{4,64},{5,65},{6,66},{7,67},{8,76},{9,... | collective-permute-start | bytes 1920008 | tf_op jit(solution)/shard_map/ppermute | solution.py:33
  22.1 5.7 %collective-permute-start.5 = (bf16[64,1280]{1,0:T(8,128)(2,1)S(1)}, bf16[64,1280]{1,0:T(8,128)(2,1)S(1)}, u32[]{:S(2)}, u32[]{:S(2)}) collective-permute-start(bf16[64,1280]{1,0:T(8,128)(2,1)S(1)} %collective-permute-done.3.refs_0_), channel_id=1, source_target_pairs={{0,2},{1,3},{2,0},{3,1},{4,6},{5,7},{6,4},{7,5},{8,10},{9,11},{10,... | collective-permute-start | bytes 491528 | tf_op jit(solution)/shard_map/ppermute | solution.py:33
  27.8 12.3 %collective-permute-start.16 = (bf16[256,1280]{1,0:T(8,128)(2,1)S(1)}, bf16[256,1280]{1,0:T(8,128)(2,1)S(1)}, u32[]{:S(2)}, u32[]{:S(2)}) collective-permute-start(bf16[256,1280]{1,0:T(8,128)(2,1)S(1)} %stack.31.refs_5_), channel_id=1, source_target_pairs={{0,24},{1,25},{2,26},{3,27},{4,28},{5,29},{6,30},{7,31},{8,16},{9,... | collective-permute-start | bytes 1966088 | tf_op jit(solution)/shard_map/ppermute | solution.py:33
  29.6 11.4 %collective-permute-start.15 = (bf16[256,1280]{1,0:T(8,128)(2,1)S(1)}, bf16[256,1280]{1,0:T(8,128)(2,1)S(1)}, u32[]{:S(2)}, u32[]{:S(2)}) collective-permute-start(bf16[256,1280]{1,0:T(8,128)(2,1)S(1)} %stack.31.refs_5_), channel_id=1, source_target_pairs={{0,8},{1,9},{2,10},{3,11},{4,12},{5,13},{6,14},{7,15},{8,0},{9,1},... | collective-permute-start | bytes 1966088 | tf_op jit(solution)/shard_map/ppermute | solution.py:33
  29.8 11.9 %collective-permute-start.10 = (bf16[256,1280]{1,0:T(8,128)(2,1)S(1)}, bf16[256,1280]{1,0:T(8,128)(2,1)S(1)}, u32[]{:S(2)}, u32[]{:S(2)}) collective-permute-start(bf16[256,1280]{1,0:T(8,128)(2,1)S(1)} %stack.30.refs_0_), channel_id=1, source_target_pairs={{0,3},{1,2},{2,1},{3,0},{4,7},{5,6},{6,5},{7,4},{8,11},{9,10},{10,... | collective-permute-start | bytes 1966088 | tf_op jit(solution)/shard_map/ppermute | solution.py:33
  36.7 14.4 %collective-permute-start.9 = (bf16[256,1280]{1,0:T(8,128)(2,1)S(1)}, bf16[256,1280]{1,0:T(8,128)(2,1)S(1)}, u32[]{:S(2)}, u32[]{:S(2)}) collective-permute-start(bf16[256,1280]{1,0:T(8,128)(2,1)S(1)} %stack.30.refs_0_), channel_id=1, source_target_pairs={{0,1},{1,0},{2,3},{3,2},{4,5},{5,4},{6,7},{7,6},{8,9},{9,8},{10,11... | collective-permute-start | bytes 1966088 | tf_op jit(solution)/shard_map/ppermute | solution.py:33
  38.4 14.8 %collective-permute-start.19 = (bf16[1250,256]{1,0:T(8,128)(2,1)S(1)}, bf16[1250,256]{1,0:T(8,128)(2,1)S(1)}, u32[]{:S(2)}, u32[]{:S(2)}) collective-permute-start(bf16[1250,256]{1,0:T(8,128)(2,1)S(1)} %join.2), channel_id=1, source_target_pairs={{0,68},{1,69},{2,70},{3,71},{4,64},{5,65},{6,66},{7,67},{8,76},{9,... | collective-permute-start | bytes 1920008 | tf_op jit(solution)/shard_map/ppermute | solution.py:33
  40.1 16.3 %collective-permute-start.20 = (bf16[1250,256]{1,0:T(8,128)(2,1)S(1)}, bf16[1250,256]{1,0:T(8,128)(2,1)S(1)}, u32[]{:S(2)}, u32[]{:S(2)}) collective-permute-start(bf16[1250,256]{1,0:T(8,128)(2,1)S(1)} %join.3), channel_id=1, source_target_pairs={{0,4},{1,5},{2,6},{3,7},{4,0},{5,1},{6,2},{7,3},{8,12},{9,13},{10,... | collective-permute-start | bytes 1920008 | tf_op jit(solution)/shard_map/ppermute | solution.py:33
  41.0 15.4 %collective-permute-start.18 = (bf16[128,1280]{1,0:T(8,128)(2,1)S(1)}, bf16[128,1280]{1,0:T(8,128)(2,1)S(1)}, u32[]{:S(2)}, u32[]{:S(2)}) collective-permute-start(bf16[128,1280]{1,0:T(8,128)(2,1)S(1)} %cut.11), channel_id=1, source_target_pairs={{0,8},{1,9},{2,10},{3,11},{4,12},{5,13},{6,14},{7,15},{8,0},{9,1},... | collective-permute-start | bytes 983048 | tf_op jit(solution)/shard_map/ppermute | solution.py:33
  41.8 14.7 %collective-permute-start.17 = (bf16[128,1280]{1,0:T(8,128)(2,1)S(1)}, bf16[128,1280]{1,0:T(8,128)(2,1)S(1)}, u32[]{:S(2)}, u32[]{:S(2)}) collective-permute-start(bf16[128,1280]{1,0:T(8,128)(2,1)S(1)} %cut.10), channel_id=1, source_target_pairs={{0,24},{1,25},{2,26},{3,27},{4,28},{5,29},{6,30},{7,31},{8,16},{9,... | collective-permute-start | bytes 983048 | tf_op jit(solution)/shard_map/ppermute | solution.py:33
  51.1 6.3 %collective-permute-start.14 = (bf16[128,1280]{1,0:T(8,128)(2,1)S(1)}, bf16[128,1280]{1,0:T(8,128)(2,1)S(1)}, u32[]{:S(2)}, u32[]{:S(2)}) collective-permute-start(bf16[128,1280]{1,0:T(8,128)(2,1)S(1)} %cut.9), channel_id=1, source_target_pairs={{0,1},{1,0},{2,3},{3,2},{4,5},{5,4},{6,7},{7,6},{8,9},{9,8},{10,11... | collective-permute-start | bytes 983048 | tf_op jit(solution)/shard_map/ppermute | solution.py:33
  53.2 7.6 %collective-permute-start.13 = (bf16[128,1280]{1,0:T(8,128)(2,1)S(1)}, bf16[128,1280]{1,0:T(8,128)(2,1)S(1)}, u32[]{:S(2)}, u32[]{:S(2)}) collective-permute-start(bf16[128,1280]{1,0:T(8,128)(2,1)S(1)} %cut.8), channel_id=1, source_target_pairs={{0,3},{1,2},{2,1},{3,0},{4,7},{5,6},{6,5},{7,4},{8,11},{9,10},{10,... | collective-permute-start | bytes 983048 | tf_op jit(solution)/shard_map/ppermute | solution.py:33
  64.5 8.2 %collective-permute-start.25 = (f32[2,1024,128]{2,1,0:T(8,128)S(1)}, f32[2,1024,128]{2,1,0:T(8,128)S(1)}, u32[]{:S(2)}, u32[]{:S(2)}) collective-permute-start(f32[2,1024,128]{2,1,0:T(8,128)S(1)} %get-tuple-element.36), channel_id=1, source_target_pairs={{0,32},{1,33},{2,34},{3,35},{4,36},{5,37},{6,38},{7,39},{8,40},{9,... | collective-permute-start | bytes 3145736 | tf_op jit(solution)/shard_map/ppermute | solution.py:33
  72.4 24.3 %copy-start = (bf16[1024,1,2048]{2,0,1:T(8,128)(2,1)S(1)}, bf16[1024,1,2048]{2,0,1:T(8,128)(2,1)}, u32[]{:S(2)}) copy-start(bf16[1024,1,2048]{2,0,1:T(8,128)(2,1)} %param.9) | copy-start | bytes 12582916
  72.4 5.5 %collective-permute-start.21 = (f32[2,1024,128]{2,1,0:T(8,128)S(1)}, f32[2,1024,128]{2,1,0:T(8,128)S(1)}, u32[]{:S(2)}, u32[]{:S(2)}) collective-permute-start(f32[2,1024,128]{2,1,0:T(8,128)S(1)} %get-tuple-element.32), channel_id=1, source_target_pairs={{0,32},{1,33},{2,34},{3,35},{4,36},{5,37},{6,38},{7,39},{8,40},{9,... | collective-permute-start | bytes 3145736 | tf_op jit(solution)/shard_map/ppermute | solution.py:33
  74.6 7.5 %collective-permute-start.26 = (bf16[64,2048]{1,0:T(8,128)(2,1)S(1)}, bf16[64,2048]{1,0:T(8,128)(2,1)S(1)}, u32[]{:S(2)}, u32[]{:S(2)}) collective-permute-start(bf16[64,2048]{1,0:T(8,128)(2,1)S(1)} %get-tuple-element.38), channel_id=1, source_target_pairs={{0,4},{1,5},{2,6},{3,7},{4,0},{5,1},{6,2},{7,3},{8,12},{9,13},{10,... | collective-permute-start | bytes 786440 | tf_op jit(solution)/shard_map/ppermute | solution.py:33
  75.0 13.0 %collective-permute-start.28 = (bf16[64,2048]{1,0:T(8,128)(2,1)S(1)}, bf16[64,2048]{1,0:T(8,128)(2,1)S(1)}, u32[]{:S(2)}, u32[]{:S(2)}) collective-permute-start(bf16[64,2048]{1,0:T(8,128)(2,1)S(1)} %get-tuple-element.38), channel_id=1, source_target_pairs={{0,68},{1,69},{2,70},{3,71},{4,64},{5,65},{6,66},{7,67},{8,76},{9,... | collective-permute-start | bytes 786440 | tf_op jit(solution)/shard_map/ppermute | solution.py:33
  76.7 11.4 %collective-permute-start.27 = (bf16[64,2048]{1,0:T(8,128)(2,1)S(1)}, bf16[64,2048]{1,0:T(8,128)(2,1)S(1)}, u32[]{:S(2)}, u32[]{:S(2)}) collective-permute-start(bf16[64,2048]{1,0:T(8,128)(2,1)S(1)} %get-tuple-element.37.refs_0_), channel_id=1, source_target_pairs={{0,64},{1,65},{2,66},{3,67},{4,68},{5,69},{6,70},{7,71},{8,72},{9,... | collective-permute-start | bytes 786440 | tf_op jit(solution)/shard_map/ppermute | solution.py:33
  79.8 13.5 %collective-permute-start.22 = (bf16[64,2048]{1,0:T(8,128)(2,1)S(1)}, bf16[64,2048]{1,0:T(8,128)(2,1)S(1)}, u32[]{:S(2)}, u32[]{:S(2)}) collective-permute-start(bf16[64,2048]{1,0:T(8,128)(2,1)S(1)} %get-tuple-element.34), channel_id=1, source_target_pairs={{0,4},{1,5},{2,6},{3,7},{4,0},{5,1},{6,2},{7,3},{8,12},{9,13},{10,... | collective-permute-start | bytes 786440 | tf_op jit(solution)/shard_map/ppermute | solution.py:33
  80.3 14.3 %collective-permute-start.24 = (bf16[64,2048]{1,0:T(8,128)(2,1)S(1)}, bf16[64,2048]{1,0:T(8,128)(2,1)S(1)}, u32[]{:S(2)}, u32[]{:S(2)}) collective-permute-start(bf16[64,2048]{1,0:T(8,128)(2,1)S(1)} %get-tuple-element.34), channel_id=1, source_target_pairs={{0,68},{1,69},{2,70},{3,71},{4,64},{5,65},{6,66},{7,67},{8,76},{9,... | collective-permute-start | bytes 786440 | tf_op jit(solution)/shard_map/ppermute | solution.py:33
  94.6 4.0 %collective-permute-start.29 = (bf16[256,2048]{1,0:T(8,128)(2,1)S(1)}, bf16[256,2048]{1,0:T(8,128)(2,1)S(1)}, u32[]{:S(2)}, u32[]{:S(2)}) collective-permute-start(bf16[256,2048]{1,0:T(8,128)(2,1)S(1)} %stack.32.part.mine), channel_id=1, source_target_pairs={{0,32},{1,33},{2,34},{3,35},{4,36},{5,37},{6,38},{7,39},{8,40},{9,... | collective-permute-start | bytes 3145736 | tf_op jit(solution)/shard_map/ppermute | solution.py:33
  96.4 9.4 %collective-permute-start.23 = (bf16[64,2048]{1,0:T(8,128)(2,1)S(1)}, bf16[64,2048]{1,0:T(8,128)(2,1)S(1)}, u32[]{:S(2)}, u32[]{:S(2)}) collective-permute-start(bf16[64,2048]{1,0:T(8,128)(2,1)S(1)} %get-tuple-element.33.refs_0_), channel_id=1, source_target_pairs={{0,64},{1,65},{2,66},{3,67},{4,68},{5,69},{6,70},{7,71},{8,72},{9,... | collective-permute-start | bytes 786440 | tf_op jit(solution)/shard_map/ppermute | solution.py:33
  100.2 7.6 %collective-permute-start.30 = (bf16[256,512]{1,0:T(8,128)(2,1)S(1)}, bf16[256,512]{1,0:T(8,128)(2,1)S(1)}, u32[]{:S(2)}, u32[]{:S(2)}) collective-permute-start(bf16[256,512]{1,0:T(8,128)(2,1)S(1)} %get-tuple-element.42.refs_0_), channel_id=1, source_target_pairs={{0,1},{1,0},{2,3},{3,2},{4,5},{5,4},{6,7},{7,6},{8,9},{9,8},{10,11... | collective-permute-start | bytes 786440 | tf_op jit(solution)/shard_map/ppermute | solution.py:33
  100.6 8.4 %collective-permute-start.31 = (bf16[256,512]{1,0:T(8,128)(2,1)S(1)}, bf16[256,512]{1,0:T(8,128)(2,1)S(1)}, u32[]{:S(2)}, u32[]{:S(2)}) collective-permute-start(bf16[256,512]{1,0:T(8,128)(2,1)S(1)} %get-tuple-element.43), channel_id=1, source_target_pairs={{0,3},{1,2},{2,1},{3,0},{4,7},{5,6},{6,5},{7,4},{8,11},{9,10},{10,... | collective-permute-start | bytes 786440 | tf_op jit(solution)/shard_map/ppermute | solution.py:33
  109.1 5.6 %collective-permute-start.32 = (bf16[256,2048]{1,0:T(8,128)(2,1)S(1)}, bf16[256,2048]{1,0:T(8,128)(2,1)S(1)}, u32[]{:S(2)}, u32[]{:S(2)}) collective-permute-start(bf16[256,2048]{1,0:T(8,128)(2,1)S(1)} %stack.33.part.mine), channel_id=1, source_target_pairs={{0,32},{1,33},{2,34},{3,35},{4,36},{5,37},{6,38},{7,39},{8,40},{9,... | collective-permute-start | bytes 3145736 | tf_op jit(solution)/shard_map/ppermute | solution.py:33
  110.7 8.9 %copy-start.3 = (f32[1400]{0:T(1024)S(1)}, f32[1400]{0:T(1024)}, u32[]{:S(2)}) copy-start(f32[1400]{0:T(1024)} %virt.1) | copy-start | bytes 16804
  110.7 8.9 %copy-start.4 = (s32[256,2]{0,1:T(2,128)S(1)}, s32[256,2]{0,1:T(2,128)}, u32[]{:S(2)}) copy-start(s32[256,2]{0,1:T(2,128)} %param.10) | copy-start | bytes 6148
  110.7 8.9 %copy-start.5 = (s32[2]{0:T(128)S(1)}, s32[2]{0:T(128)}, u32[]{:S(2)}) copy-start(s32[2]{0:T(128)} %offsets.1) | copy-start | bytes 28
  110.7 8.9 %copy-start.6 = (f32[120]{0:T(128)S(1)}, f32[120]{0:T(128)}, u32[]{:S(2)}) copy-start(f32[120]{0:T(128)} %param.12) | copy-start | bytes 1444
  110.7 11.8 %collective-permute-start.36 = (bf16[256,512]{1,0:T(8,128)(2,1)S(1)}, bf16[256,512]{1,0:T(8,128)(2,1)S(1)}, u32[]{:S(2)}, u32[]{:S(2)}) collective-permute-start(bf16[256,512]{1,0:T(8,128)(2,1)S(1)} %get-tuple-element.52), channel_id=1, source_target_pairs={{0,2},{1,3},{2,0},{3,1},{4,6},{5,7},{6,4},{7,5},{8,10},{9,11},{10,... | collective-permute-start | bytes 786440 | tf_op jit(solution)/shard_map/ppermute | solution.py:33
  116.2 9.6 %collective-permute-start.33 = (bf16[256,512]{1,0:T(8,128)(2,1)S(1)}, bf16[256,512]{1,0:T(8,128)(2,1)S(1)}, u32[]{:S(2)}, u32[]{:S(2)}) collective-permute-start(bf16[256,512]{1,0:T(8,128)(2,1)S(1)} %get-tuple-element.47.refs_0_), channel_id=1, source_target_pairs={{0,1},{1,0},{2,3},{3,2},{4,5},{5,4},{6,7},{7,6},{8,9},{9,8},{10,11... | collective-permute-start | bytes 786440 | tf_op jit(solution)/shard_map/ppermute | solution.py:33
  117.0 8.8 %collective-permute-start.34 = (bf16[256,512]{1,0:T(8,128)(2,1)S(1)}, bf16[256,512]{1,0:T(8,128)(2,1)S(1)}, u32[]{:S(2)}, u32[]{:S(2)}) collective-permute-start(bf16[256,512]{1,0:T(8,128)(2,1)S(1)} %get-tuple-element.48), channel_id=1, source_target_pairs={{0,3},{1,2},{2,1},{3,0},{4,7},{5,6},{6,5},{7,4},{8,11},{9,10},{10,... | collective-permute-start | bytes 786440 | tf_op jit(solution)/shard_map/ppermute | solution.py:33
  117.2 14.2 %collective-permute-start.35 = (bf16[256,512]{1,0:T(8,128)(2,1)S(1)}, bf16[256,512]{1,0:T(8,128)(2,1)S(1)}, u32[]{:S(2)}, u32[]{:S(2)}) collective-permute-start(bf16[256,512]{1,0:T(8,128)(2,1)S(1)} %get-tuple-element.49), channel_id=1, source_target_pairs={{0,2},{1,3},{2,0},{3,1},{4,6},{5,7},{6,4},{7,5},{8,10},{9,11},{10,... | collective-permute-start | bytes 786440 | tf_op jit(solution)/shard_map/ppermute | solution.py:33
